TPU v7x, 1024 devices: a whole 4x8x16 slice. The times are simulated.
1024 devices in a mesh: expert: 16 (over z), group: 64 (over x, y, core).
Axes of the slice: x: 4, y: 8, z: 16, core: 2. Of those that a mesh axis runs over, the one named last changes fastest.
Arguments:
- tokens: bfloat16 [4096, 2048], P('expert'), may hold values from -6 to 6
- routes: int32 [4096, 8], P('expert'), may hold values from 0 to 127, as said below
- combine: bfloat16 [4096, 8], P('expert'), may hold values from 0.049804688 to 0.3984375
- gate_weight: bfloat16 [196608, 2048], P(('expert', 'group')), may hold values from -0.125 to 0.125
- up_weight: bfloat16 [196608, 2048], P(('expert', 'group')), may hold values from -0.125 to 0.125
- direction: bfloat16 [196608, 2048], P(('expert', 'group')), may hold values from -0.29882812 to 0.29882812
Outputs:
- tangent_out: bfloat16 [4096, 2048], P('expert')
- curvature: bfloat16 [196608, 2048], P(('expert', 'group'))
Inputs may be any that keep to these rules, and one draw needn't show every extreme that they name: `routes`: each token names 8 different experts. In each block of 256 consecutive tokens no expert is named by more than 32 tokens, and some expert is named by exactly 32 tokens in every block.
All inputs are finite; a program needn't handle non-finite values.
Results may differ from a plain program's by a relative error of at most 0.015.
Values may be sent and summed in bfloat16 or wider, within the bound.
No kernel may reach another device: no remote copies, remote signals or barrier semaphores. Data moves between devices by JAX's collectives and lax.ppermute only.
A program may use at most 32 MiB of HBM per device.

v0:
```python
import jax
import jax.numpy as jnp
from jax import lax
from jax.sharding import PartitionSpec as P

TOP = 8
EXP_COL = 8


def contract_rows(left, right):
    return lax.dot_general(
        left, right, (((0,), (0,)), ((), ())), preferred_element_type=jnp.float32
    )


def shards(tokens, routes, combine, gate_weight, up_weight, direction):
    n_expert = lax.axis_size("expert")
    n_group = lax.axis_size("group")
    col_tok = tokens.shape[0]
    width = tokens.shape[1]
    unit_count = gate_weight.shape[0]
    split_count = n_group // EXP_COL
    slot_count = 2 * col_tok * TOP // (EXP_COL * n_expert)
    group_index = lax.axis_index("group")
    owner_ids = jnp.arange(n_expert, dtype=jnp.int32) * EXP_COL + group_index // split_count
    matches = routes[None, :, :] == owner_ids[:, None, None]
    member = jnp.any(matches, axis=2)
    weight_tok = jnp.sum(jnp.where(matches, combine[None, :, :].astype(jnp.float32), 0.0), axis=2)
    slot_rank = jnp.cumsum(member.astype(jnp.int32), axis=1) - 1
    slot_ids = jnp.arange(slot_count, dtype=jnp.int32)
    picked_slots = member[:, None, :] & (slot_rank[:, None, :] == slot_ids[None, :, None])
    select = picked_slots.astype(jnp.bfloat16)
    slot_weight = jnp.sum(jnp.where(picked_slots, weight_tok[:, None, :], 0.0), axis=2)
    outgoing = jnp.einsum("jst,td->jsd", select, tokens, preferred_element_type=jnp.float32).astype(
        jnp.bfloat16
    )
    arrived = lax.all_to_all(outgoing, "expert", split_axis=0, concat_axis=0, tiled=True)
    row_count = arrived.shape[1]
    flat_rows = arrived.reshape(n_expert * row_count, width)
    gate_value = lax.dot_general(
        flat_rows, gate_weight, (((1,), (1,)), ((), ())), preferred_element_type=jnp.float32
    )
    up_value = lax.dot_general(
        flat_rows, up_weight, (((1,), (1,)), ((), ())), preferred_element_type=jnp.float32
    )
    hidden = (jax.nn.silu(gate_value) * up_value).astype(jnp.bfloat16)
    partial_value = jnp.dot(hidden, direction, preferred_element_type=jnp.float32).astype(
        jnp.bfloat16
    )
    returned_rows = lax.all_to_all(
        partial_value.reshape(n_expert, row_count, width),
        "expert",
        split_axis=0,
        concat_axis=0,
        tiled=True,
    )
    returned, hidden = (returned_rows, hidden.reshape(n_expert, row_count, unit_count))
    weighted = (select.astype(jnp.float32) * slot_weight[:, :, None]).astype(jnp.bfloat16)
    spread = weighted.reshape(n_expert * slot_count, col_tok)
    returned_flat = returned.reshape(n_expert * slot_count, width)
    summed = lax.psum(contract_rows(spread, returned_flat), "group")
    tangent_out = summed.astype(jnp.bfloat16)
    picked = jnp.einsum("jst,td->jsd", select, tangent_out, preferred_element_type=jnp.float32)
    scaled = (picked * slot_weight[:, :, None]).astype(jnp.bfloat16)
    arrived_tangent = lax.all_to_all(scaled, "expert", split_axis=0, concat_axis=0, tiled=True)
    curvature = contract_rows(
        hidden.reshape(n_expert * slot_count, unit_count),
        arrived_tangent.reshape(n_expert * slot_count, width),
    ).astype(jnp.bfloat16)
    return (tangent_out, curvature)


def solution(mesh):
    return jax.shard_map(
        shards,
        mesh=mesh,
        in_specs=(
            P("expert", None),
            P("expert", None),
            P("expert", None),
            P(("expert", "group"), None),
            P(("expert", "group"), None),
            P(("expert", "group"), None),
        ),
        out_specs=(P("expert", None), P(("expert", "group"), None)),
        check_vma=False,
    )
```

profile of v0, /device:TPU:1, one launch (start us, length us, event | category | flops | bytes accessed | tf_op | source)
XLA Modules:
  0.0 592.8 jit_solution(7752516654620618262)
XLA Ops:
  0.6 0.0 copy-start
  0.7 0.9 compare_reduce_fusion
  1.6 0.6 reduce-window.6
  2.2 0.2 slice_reduce_fusion
  2.4 0.1 copy_bitcast_fusion
  2.5 0.0 copy-done
  2.5 0.7 convolution_convert_fusion.1
  3.2 0.0 copy-start.4
  3.2 109.6 %all_to_all.15 = bf16[16,32,2048]{2,1,0:T(8,128)(2,1)S(1)} all-to-all(bf16[16,32,2048]{2,1,0:T(8,128)(2,1)S(1)} %convolution_convert_fusion.1), channel_id=1, replica_groups=mesh['expert'=16,'group'=64] {'expert'}, dimensions={0} | all-to-all | bytes 4194304 | tf_op jit(solution)/shard_map/all_to_all | solution.py:37
  112.8 0.0 copy-done.4
  112.8 0.0 copy-start.5
  112.8 0.8 fusion.15
  113.7 0.3 copy-done.5
  114.0 0.0 copy-start.1
  114.0 0.9 fusion
  114.8 0.2 copy-done.1
  115.1 2.0 convolution_convert_fusion
  117.1 0.0 copy-start.3
  117.1 0.0 copy-start.2
  117.1 12.8 %all-to-all-start.1 = ((bf16[16,32,2048]{2,1,0:T(8,128)(2,1)}), bf16[16,32,2048]{2,1,0:T(8,128)(2,1)}, u32[]{:S(2)}, u32[]{:S(2)}) async-start(bf16[16,32,2048]{2,1,0:T(8,128)(2,1)} %bitcast.2), calls=%async_computation.1 | async-start | bytes 4194304 | tf_op jit(solution)/shard_map/all_to_all | solution.py:50
  129.9 0.0 copy-done.3
  129.9 0.0 copy-done.2
  129.9 0.1 fusion.14
  130.0 0.2 select_reduce_fusion
  130.2 91.6 %all-to-all-done.1 = bf16[16,32,2048]{2,1,0:T(8,128)(2,1)} async-done(((bf16[16,32,2048]{2,1,0:T(8,128)(2,1)}), bf16[16,32,2048]{2,1,0:T(8,128)(2,1)}, u32[]{:S(2)}, u32[]{:S(2)}) %all-to-all-start.1) | async-done | bytes 2097184 | tf_op jit(solution)/shard_map/all_to_all | solution.py:50
  221.8 2.4 convolution_bitcast_fusion
  224.2 267.2 %all-reduce.1 = bf16[256,2048]{1,0:T(8,128)(2,1)} all-reduce(f32[256,2048]{1,0:T(8,128)S(1)} %convolution_bitcast_fusion), channel_id=1, replica_groups=mesh['expert'=16,'group'=64] {'group'}, use_global_device_ids=true, to_apply=%region_5.6 | all-reduce | flops 524288 | bytes 3145728 | tf_op jit(solution)/shard_map/psum | solution.py:61
  491.4 1.9 multiply_convert_fusion
  493.4 98.0 %all_to_all.16 = bf16[16,32,2048]{2,1,0:T(8,128)(2,1)S(1)} all-to-all(bf16[16,32,2048]{2,1,0:T(8,128)(2,1)S(1)} %multiply_convert_fusion), channel_id=1, replica_groups=mesh['expert'=16,'group'=64] {'expert'}, dimensions={0} | all-to-all | bytes 4194304 | tf_op jit(solution)/shard_map/all_to_all | solution.py:65
  591.4 1.5 convolution_convert_fusion.2
  (5 shorter events, 0.1 us)
Async XLA Ops:
  0.6 1.8 copy-start
  3.2 109.6 %copy-start.4 = (bf16[192,2048]{1,0:T(8,128)(2,1)S(1)}, bf16[192,2048]{1,0:T(8,128)(2,1)}, u32[]{:S(2)}) copy-start(bf16[192,2048]{1,0:T(8,128)(2,1)} %param.9) | copy-start | bytes 2359300
  112.8 1.1 copy-start.5
  114.0 1.1 copy-start.1
  117.1 12.8 %copy-start.3 = (bf16[256,8]{0,1:T(8,128)(2,1)S(1)}, bf16[256,8]{0,1:T(8,128)(2,1)}, u32[]{:S(2)}) copy-start(bf16[256,8]{0,1:T(8,128)(2,1)} %param.8) | copy-start | bytes 12292
  117.1 12.8 %copy-start.2 = (s32[256,8]{0,1:T(8,128)S(1)}, s32[256,8]{0,1:T(8,128)}, u32[]{:S(2)}) copy-start(s32[256,8]{0,1:T(8,128)} %param.7) | copy-start | bytes 24580
  117.1 104.7 %all-to-all-start.1 = ((bf16[16,32,2048]{2,1,0:T(8,128)(2,1)}), bf16[16,32,2048]{2,1,0:T(8,128)(2,1)}, u32[]{:S(2)}, u32[]{:S(2)}) async-start(bf16[16,32,2048]{2,1,0:T(8,128)(2,1)} %bitcast.2), calls=%async_computation.1 | async-start | bytes 4194304 | tf_op jit(solution)/shard_map/all_to_all | solution.py:50
where the time goes:
time: 602 us; the launch traced here: 593 us
  blocking collectives  475 us (79%)
  waiting for transfers between devices  91.6 us (15%)
  starting transfers between devices  12.8 us (2%)
  matrix products  10.3 us (2%)
    psum x1, blocking collectives, shards(): summed = lax.psum(contract_rows(spread, returned_flat), 'group')  267 us
    all_to_all x1, blocking collectives, shards(): lax.all_to_all(outgoing, 'expert', split_axis=0, concat_axis=0, tiled=True)  110 us
    all_to_all x1, blocking collectives, shards(): lax.all_to_all(scaled, 'expert', split_axis=0, concat_axis=0, tiled=True)  98 us
    all_to_all x1, waiting for transfers between devices, shards(): lax.all_to_all(partial_value.reshape(n_expert, row_count, width), 'expert...  91.6 us
    all_to_all x1, starting transfers between devices, shards(): lax.all_to_all(partial_value.reshape(n_expert, row_count, width), 'expert...  12.8 us
  transfers between devices with their start and end apart: 1, of which 1 were waited for; matrix products, arithmetic and copies ran while one was open for 0% of the time, Pallas kernels for 0%

commit v1 on v0

v1 whole, which is shorter than its diff:
```python
import jax
import jax.numpy as jnp
from jax import lax
from jax.sharding import Mesh, PartitionSpec as P

TOP = 8
EXP_COL = 8
CORES = 2
LINE = 4


def contract_rows(left, right):
    return lax.dot_general(
        left, right, (((0,), (0,)), ((), ())), preferred_element_type=jnp.float32
    )


def shift_line(value, step):
    return lax.ppermute(value, "line", [(i, (i + step) % LINE) for i in range(LINE)])


def swap_cores(value):
    return lax.ppermute(value, "core", [(i, i ^ 1) for i in range(CORES)])


def swap_local(value, mask):
    return lax.ppermute(value, "local", [(i, i ^ mask) for i in range(EXP_COL)])


def shards(tokens, routes, combine, gate_weight, up_weight, direction):
    n_expert = lax.axis_size("expert")
    n_slice = LINE * CORES
    col_tok, width = tokens.shape
    unit_count = gate_weight.shape[0]
    cols = width // n_slice
    slot_count = 2 * col_tok * TOP // (EXP_COL * n_expert)
    rows = n_expert * slot_count
    local_index = lax.axis_index("local")
    line_index = lax.axis_index("line")
    core_index = lax.axis_index("core")

    def first_col(step, other):
        line = (line_index + step) & (LINE - 1)
        core = core_index ^ other
        return (line * CORES + core) * cols

    def columns(weight, step, other):
        return lax.dynamic_slice_in_dim(weight, first_col(step, other), cols, 1)

    with jax.named_scope("routing"):
        owner_ids = jnp.arange(n_expert, dtype=jnp.int32) * EXP_COL + local_index
        matches = routes[None, :, :] == owner_ids[:, None, None]
        member = jnp.any(matches, axis=2)
        weight_tok = jnp.sum(
            jnp.where(matches, combine[None, :, :].astype(jnp.float32), 0.0), axis=2
        )
        slot_rank = jnp.cumsum(member.astype(jnp.int32), axis=1) - 1
        slot_ids = jnp.arange(slot_count, dtype=jnp.int32)
        picked_slots = member[:, None, :] & (slot_rank[:, None, :] == slot_ids[None, :, None])
        select = picked_slots.astype(jnp.bfloat16).reshape(rows, col_tok)
        weighted = jnp.where(picked_slots, weight_tok[:, None, :], 0.0)
        slot_weight = jnp.sum(weighted, axis=2).reshape(rows, 1)
        spread = weighted.astype(jnp.bfloat16).reshape(rows, col_tok)

    def over_planes(slots):
        moved = lax.all_to_all(
            slots.reshape(n_expert, slot_count, cols), "expert", 0, 0, tiled=True
        )
        return moved.reshape(rows, cols)

    def gather_blocks(block):
        blocks = {(0, 0): block}
        for step in (2, 1, 3):
            blocks[(LINE - step, 0)] = shift_line(block, step)
        for step in (0, 1, 3, 2):
            blocks[(step, 1)] = swap_cores(blocks[(step, 0)])
        return blocks

    with jax.named_scope("dispatch"):
        own_cols = columns(tokens, 0, 0)
        outgoing = jnp.dot(select, own_cols, preferred_element_type=jnp.float32)
        row_blocks = gather_blocks(over_planes(outgoing.astype(jnp.bfloat16)))

    with jax.named_scope("experts"):
        both = jnp.concatenate([gate_weight, up_weight], axis=0)
        value = 0.0
        for (step, other), block in row_blocks.items():
            value += lax.dot_general(
                block,
                columns(both, step, other),
                (((1,), (1,)), ((), ())),
                preferred_element_type=jnp.float32,
            )
        hidden = jax.nn.silu(value[:, :unit_count]) * value[:, unit_count:]
        hidden = hidden.astype(jnp.bfloat16)

    with jax.named_scope("combine"):
        def slice_out(step, other):
            return jnp.dot(
                hidden, columns(direction, step, other), preferred_element_type=jnp.float32
            )

        steps = (2, 1, 3, 0)
        swapped = {
            step: swap_cores(slice_out(step, 1).astype(jnp.bfloat16)) for step in steps
        }
        pair_out = {
            step: (slice_out(step, 0) + swapped[step].astype(jnp.float32)).astype(jnp.bfloat16)
            for step in steps
        }
        expert_out = pair_out[0].astype(jnp.float32)
        for step in steps[:3]:
            expert_out += shift_line(pair_out[step], step).astype(jnp.float32)
        returned = over_planes(expert_out.astype(jnp.bfloat16))
        part = lax.optimization_barrier(contract_rows(spread, returned).astype(jnp.bfloat16))
        near = [swap_local(part, mask).astype(jnp.float32) for mask in (2, 4, 6)]
        half = (part.astype(jnp.float32) + near[0]) + (near[1] + near[2])
        half = lax.optimization_barrier(half.astype(jnp.bfloat16))
        total = half.astype(jnp.float32) + swap_local(half, 1).astype(jnp.float32)
        tangent_cols = total.astype(jnp.bfloat16)

    with jax.named_scope("tangent"):
        tangent_out = lax.all_gather(tangent_cols, ("line", "core"))
        tangent_out = tangent_out.transpose(1, 0, 2).reshape(col_tok, width)

    with jax.named_scope("curvature"):
        picked = jnp.dot(select, tangent_cols, preferred_element_type=jnp.float32)
        scaled = (picked * slot_weight).astype(jnp.bfloat16)
        curvature = jnp.zeros((unit_count, width), jnp.bfloat16)
        for (step, other), block in gather_blocks(over_planes(scaled)).items():
            curvature = lax.dynamic_update_slice_in_dim(
                curvature,
                contract_rows(hidden, block).astype(jnp.bfloat16),
                first_col(step, other),
                1,
            )
    return tangent_out, curvature


def solution(mesh):
    n_expert = mesh.shape["expert"]
    fine = Mesh(
        mesh.devices.reshape(n_expert, EXP_COL, LINE, CORES), ("expert", "local", "line", "core")
    )
    by_block = P("expert", None)
    by_device = P(("expert", "local", "line", "core"), None)
    return jax.shard_map(
        shards,
        mesh=fine,
        in_specs=(by_block, by_block, by_block, by_device, by_device, by_device),
        out_specs=(by_block, by_device),
        check_vma=False,
    )
```

time: 602 us -> 248 us (0.41); the launches traced: 593 us -> 247 us
  blocking collectives: 475 us -> 23 us
  starting transfers between devices: 12.8 us -> 125 us
  waiting for transfers between devices: 91.6 us -> 67.3 us
  between operations: 0.76 us -> 14.8 us
    psum x1 -> x0, blocking collectives: 267 us -> none  [shards(): summed = lax.psum(contract_rows(spread, returned_flat), 'group')]
    all_to_all x2 -> x1, blocking collectives: 208 us -> 23 us  [over_planes(): lax.all_to_all(slots.reshape(n_expert, slot_count, cols), 'expert', 0, 0,...]
    ppermute x0 -> x25, starting transfers between devices: none -> 96.4 us  [the longest x12 51.8 us: swap_cores(): return lax.ppermute(value, 'core', [(i, i ^ 1) for i in range(CORES)])]
    all_to_all x1 -> x2, waiting for transfers between devices: 91.6 us -> 25.5 us  [over_planes(): lax.all_to_all(slots.reshape(n_expert, slot_count, cols), 'expert', 0, 0,...]
    ppermute x0 -> x25, waiting for transfers between devices: none -> 26.2 us  [the longest x9 16.9 us: shift_line(): lax.ppermute(value, 'line', [(i, (i + step) % LINE) for i in range(LINE)])]
    all_to_all x1 -> x2, starting transfers between devices: 12.8 us -> 28.7 us  [over_planes(): lax.all_to_all(slots.reshape(n_expert, slot_count, cols), 'expert', 0, 0,...]
    all_gather x0 -> x1, waiting for transfers between devices: none -> 15.5 us  [shards(): tangent_out = lax.all_gather(tangent_cols, ('line', 'core'))]
  transfers between devices with their start and end apart: 1 -> 28, of which waited for: 1 -> 10; matrix products, arithmetic and copies ran while one was open for 0% -> 3% of each run, Pallas kernels for 0% -> 0%
where the time goes in v1:
time: 248 us; the launch traced here: 247 us
  starting transfers between devices  125 us (50%)
  waiting for transfers between devices  67.3 us (27%)
  blocking collectives  23 us (9%)
  between operations  14.8 us (6%)
  matrix products  7.73 us (3%)
  local copies, waits for them, and re-layouts  5.86 us (2%)
  other arithmetic  3.14 us (1%)
    ppermute x12, starting transfers between devices, swap_cores(): return lax.ppermute(value, 'core', [(i, i ^ 1) for i in range(CORES)])  51.8 us
    ppermute x9, starting transfers between devices, shift_line(): lax.ppermute(value, 'line', [(i, (i + step) % LINE) for i in range(LINE)])  29.5 us
    all_to_all x2, starting transfers between devices, over_planes(): lax.all_to_all(slots.reshape(n_expert, slot_count, cols), 'expert', 0, 0,...  28.7 us
    all_to_all x2, waiting for transfers between devices, over_planes(): lax.all_to_all(slots.reshape(n_expert, slot_count, cols), 'expert', 0, 0,...  25.5 us
    all_to_all x1, blocking collectives, over_planes(): lax.all_to_all(slots.reshape(n_expert, slot_count, cols), 'expert', 0, 0,...  23 us
    ppermute x9, waiting for transfers between devices, shift_line(): lax.ppermute(value, 'line', [(i, (i + step) % LINE) for i in range(LINE)])  16.9 us
    all_gather x1, waiting for transfers between devices, shards(): tangent_out = lax.all_gather(tangent_cols, ('line', 'core'))  15.5 us
    ppermute x4, starting transfers between devices, swap_local(): return lax.ppermute(value, 'local', [(i, i ^ mask) for i in range(EXP_COL)])  15.1 us
  transfers between devices with their start and end apart: 28, of which 10 were waited for; matrix products, arithmetic and copies ran while one was open for 3% of the time, Pallas kernels for 0%

profile of v1, /device:TPU:1, one launch (start us, length us, event | category | flops | bytes accessed | tf_op | source)
XLA Modules:
  0.0 246.9 jit_solution(18257965372689753739)
XLA Ops:
  7.2 0.9 compare_reduce_fusion
  8.1 0.6 reduce-window.6
  9.3 1.0 convolution_convert_fusion.4
  10.3 19.4 %all-to-all-start = ((bf16[16,32,256]{2,1,0:T(8,128)(2,1)}), bf16[16,32,256]{2,1,0:T(8,128)(2,1)S(1)}, u32[]{:S(2)}, u32[]{:S(2)}) async-start(bf16[16,32,256]{2,1,0:T(8,128)(2,1)} %bitcast.2), calls=%async_computation | async-start | bytes 524288 | tf_op jit(solution)/shard_map/dispatch/all_to_all | solution.py:66
  29.7 1.2 constant_dynamic-update-slice_fusion.1
  30.9 11.9 %all-to-all-done = bf16[16,32,256]{2,1,0:T(8,128)(2,1)S(1)} async-done(((bf16[16,32,256]{2,1,0:T(8,128)(2,1)}), bf16[16,32,256]{2,1,0:T(8,128)(2,1)S(1)}, u32[]{:S(2)}, u32[]{:S(2)}) %all-to-all-start) | async-done | bytes 262176 | tf_op jit(solution)/shard_map/dispatch/all_to_all | solution.py:66
  42.8 5.2 %collective-permute-start.2 = (bf16[512,256]{1,0:T(8,128)(2,1)S(1)}, bf16[512,256]{1,0:T(8,128)(2,1)S(1)}, u32[]{:S(2)}, u32[]{:S(2)}) collective-permute-start(bf16[512,256]{1,0:T(8,128)(2,1)S(1)} %bitcast.74), channel_id=1, source_target_pairs={{0,6},{2,0},{4,2},{6,4},{1,7},{3,1},{5,3},{7,5},{8,14},{10,8},{12,... | collective-permute-start | bytes 786440 | tf_op jit(solution)/shard_map/dispatch/ppermute | solution.py:19
  48.0 1.9 collective-permute-start.1
  50.0 1.2 constant_dynamic-update-slice_fusion
  51.2 2.3 collective-permute-start
  53.6 8.9 %collective-permute-start.3 = (bf16[512,256]{1,0:T(8,128)(2,1)S(1)}, bf16[512,256]{1,0:T(8,128)(2,1)S(1)}, u32[]{:S(2)}, u32[]{:S(2)}) collective-permute-start(bf16[512,256]{1,0:T(8,128)(2,1)S(1)} %bitcast.77), channel_id=1, source_target_pairs={{0,1},{1,0},{2,3},{3,2},{4,5},{5,4},{6,7},{7,6},{8,9},{9,8},{10,11... | collective-permute-start | bytes 786440 | tf_op jit(solution)/shard_map/dispatch/ppermute | solution.py:23
  62.8 5.2 %collective-permute-start.5 = (bf16[512,256]{1,0:T(8,128)(2,1)S(1)}, bf16[512,256]{1,0:T(8,128)(2,1)S(1)}, u32[]{:S(2)}, u32[]{:S(2)}) collective-permute-start(bf16[512,256]{1,0:T(8,128)(2,1)S(1)} %collective-permute-done.1), channel_id=1, source_target_pairs={{0,1},{1,0},{2,3},{3,2},{4,5},{5,4},{6,7},{7,6},{8,9},{9,8},{10,11... | collective-permute-start | bytes 786440 | tf_op jit(solution)/shard_map/dispatch/ppermute | solution.py:23
  68.0 1.9 collective-permute-start.4
  70.2 1.4 collective-permute-done
  71.6 4.8 %collective-permute-start.6 = (bf16[512,256]{1,0:T(8,128)(2,1)S(1)}, bf16[512,256]{1,0:T(8,128)(2,1)S(1)}, u32[]{:S(2)}, u32[]{:S(2)}) collective-permute-start(bf16[512,256]{1,0:T(8,128)(2,1)S(1)} %collective-permute-done), channel_id=1, source_target_pairs={{0,1},{1,0},{2,3},{3,2},{4,5},{5,4},{6,7},{7,6},{8,9},{9,8},{10,11... | collective-permute-start | bytes 786440 | tf_op jit(solution)/shard_map/dispatch/ppermute | solution.py:23
  78.0 0.3 fusion.1
  78.4 0.7 copy-done.3
  79.6 2.2 collective-permute-start.8
  82.1 2.1 collective-permute-start.10
  84.5 2.2 collective-permute-start.12
  86.7 2.1 collective-permute-start.7
  89.2 3.8 %collective-permute-start.9 = (bf16[512,256]{1,0:T(8,128)(2,1)S(1)}, bf16[512,256]{1,0:T(8,128)(2,1)S(1)}, u32[]{:S(2)}, u32[]{:S(2)}) collective-permute-start(bf16[512,256]{1,0:T(8,128)(2,1)S(1)} %add_convert_fusion.3), channel_id=1, source_target_pairs={{0,4},{2,6},{4,0},{6,2},{1,5},{3,7},{5,1},{7,3},{8,12},{10,14},{12... | collective-permute-start | bytes 786440 | tf_op jit(solution)/shard_map/combine/ppermute | solution.py:19
  93.2 1.9 collective-permute-start.11
  95.5 5.2 %collective-permute-start.13 = (bf16[512,256]{1,0:T(8,128)(2,1)S(1)}, bf16[512,256]{1,0:T(8,128)(2,1)S(1)}, u32[]{:S(2)}, u32[]{:S(2)}) collective-permute-start(bf16[512,256]{1,0:T(8,128)(2,1)S(1)} %add_convert_fusion.1), channel_id=1, source_target_pairs={{0,6},{2,0},{4,2},{6,4},{1,7},{3,1},{5,3},{7,5},{8,14},{10,8},{12,... | collective-permute-start | bytes 786440 | tf_op jit(solution)/shard_map/combine/ppermute | solution.py:19
  101.0 10.2 %collective-permute-done.9 = bf16[512,256]{1,0:T(8,128)(2,1)S(1)} collective-permute-done((bf16[512,256]{1,0:T(8,128)(2,1)S(1)}, bf16[512,256]{1,0:T(8,128)(2,1)S(1)}, u32[]{:S(2)}, u32[]{:S(2)}) %collective-permute-start.9) | collective-permute-done | bytes 262176 | tf_op jit(solution)/shard_map/combine/ppermute | solution.py:19
  111.2 5.3 %collective-permute-done.13 = bf16[512,256]{1,0:T(8,128)(2,1)S(1)} collective-permute-done((bf16[512,256]{1,0:T(8,128)(2,1)S(1)}, bf16[512,256]{1,0:T(8,128)(2,1)S(1)}, u32[]{:S(2)}, u32[]{:S(2)}) %collective-permute-start.13) | collective-permute-done | bytes 262176 | tf_op jit(solution)/shard_map/combine/ppermute | solution.py:19
  116.5 0.9 add_convert_fusion
  117.3 9.3 %all-to-all-start.1 = ((bf16[16,32,256]{2,1,0:T(8,128)(2,1)}), bf16[16,32,256]{2,1,0:T(8,128)(2,1)S(1)}, u32[]{:S(2)}, u32[]{:S(2)}) async-start(bf16[16,32,256]{2,1,0:T(8,128)(2,1)} %bitcast.4), calls=%async_computation.1 | async-start | bytes 524288 | tf_op jit(solution)/shard_map/combine/all_to_all | solution.py:66
  126.9 13.5 %all-to-all-done.1 = bf16[16,32,256]{2,1,0:T(8,128)(2,1)S(1)} async-done(((bf16[16,32,256]{2,1,0:T(8,128)(2,1)}), bf16[16,32,256]{2,1,0:T(8,128)(2,1)S(1)}, u32[]{:S(2)}, u32[]{:S(2)}) %all-to-all-start.1) | async-done | bytes 262176 | tf_op jit(solution)/shard_map/combine/all_to_all | solution.py:66
  140.4 0.3 fusion.5
  140.7 3.1 %collective-permute-start.14 = (bf16[256,256]{1,0:T(8,128)(2,1)S(1)}, bf16[256,256]{1,0:T(8,128)(2,1)S(1)}, u32[]{:S(2)}, u32[]{:S(2)}) collective-permute-start(bf16[256,256]{1,0:T(8,128)(2,1)S(1)} %fusion.5), channel_id=1, source_target_pairs={{0,16},{8,24},{16,0},{24,8},{32,48},{40,56},{48,32},{56,40},{1,17}... | collective-permute-start | bytes 393224 | tf_op jit(solution)/shard_map/combine/ppermute | solution.py:27
  143.8 4.4 %collective-permute-start.15 = (bf16[256,256]{1,0:T(8,128)(2,1)S(1)}, bf16[256,256]{1,0:T(8,128)(2,1)S(1)}, u32[]{:S(2)}, u32[]{:S(2)}) collective-permute-start(bf16[256,256]{1,0:T(8,128)(2,1)S(1)} %fusion.5), channel_id=1, source_target_pairs={{0,32},{8,40},{16,48},{24,56},{32,0},{40,8},{48,16},{56,24},{1,33}... | collective-permute-start | bytes 393224 | tf_op jit(solution)/shard_map/combine/ppermute | solution.py:27
  148.2 2.1 collective-permute-start.16
  150.3 0.7 collective-permute-done.15
  151.0 4.1 %collective-permute-done.16 = bf16[256,256]{1,0:T(8,128)(2,1)S(1)} collective-permute-done((bf16[256,256]{1,0:T(8,128)(2,1)S(1)}, bf16[256,256]{1,0:T(8,128)(2,1)S(1)}, u32[]{:S(2)}, u32[]{:S(2)}) %collective-permute-start.16) | collective-permute-done | bytes 131104 | tf_op jit(solution)/shard_map/combine/ppermute | solution.py:27
  155.2 5.5 %collective-permute-start.17 = (bf16[256,256]{1,0:T(8,128)(2,1)S(1)}, bf16[256,256]{1,0:T(8,128)(2,1)S(1)}, u32[]{:S(2)}, u32[]{:S(2)}) collective-permute-start(bf16[256,256]{1,0:T(8,128)(2,1)S(1)} %add_convert_fusion.6), channel_id=1, source_target_pairs={{0,8},{8,0},{16,24},{24,16},{32,40},{40,32},{48,56},{56,48},{1,9},... | collective-permute-start | bytes 393224 | tf_op jit(solution)/shard_map/combine/ppermute | solution.py:27
  161.0 3.8 %collective-permute-done.17 = bf16[256,256]{1,0:T(8,128)(2,1)S(1)} collective-permute-done((bf16[256,256]{1,0:T(8,128)(2,1)S(1)}, bf16[256,256]{1,0:T(8,128)(2,1)S(1)}, u32[]{:S(2)}, u32[]{:S(2)}) %collective-permute-start.17) | collective-permute-done | bytes 131104 | tf_op jit(solution)/shard_map/combine/ppermute | solution.py:27
  165.1 23.0 %all_to_all.15 = bf16[16,32,256]{2,1,0:T(8,128)(2,1)S(1)} all-to-all(bf16[16,32,256]{2,1,0:T(8,128)(2,1)S(1)} %bitcast.73), channel_id=1, replica_groups=mesh['expert'=16,'local'=8,'line'=4,'core'=2] {'expert'}, dimensions={0} | all-to-all | bytes 524288 | tf_op jit(solution)/shard_map/curvature/all_to_all | solution.py:66
  188.1 2.1 collective-permute-start.18
  190.2 2.8 %collective-permute-start.19 = (bf16[512,256]{1,0:T(8,128)(2,1)S(1)}, bf16[512,256]{1,0:T(8,128)(2,1)S(1)}, u32[]{:S(2)}, u32[]{:S(2)}) collective-permute-start(bf16[512,256]{1,0:T(8,128)(2,1)S(1)} %bitcast.67), channel_id=1, source_target_pairs={{0,2},{2,4},{4,6},{6,0},{1,3},{3,5},{5,7},{7,1},{8,10},{10,12},{12... | collective-permute-start | bytes 786440 | tf_op jit(solution)/shard_map/curvature/ppermute | solution.py:19
  193.0 4.2 %collective-permute-start.20 = (bf16[512,256]{1,0:T(8,128)(2,1)S(1)}, bf16[512,256]{1,0:T(8,128)(2,1)S(1)}, u32[]{:S(2)}, u32[]{:S(2)}) collective-permute-start(bf16[512,256]{1,0:T(8,128)(2,1)S(1)} %bitcast.68), channel_id=1, source_target_pairs={{0,6},{2,0},{4,2},{6,4},{1,7},{3,1},{5,3},{7,5},{8,14},{10,8},{12,... | collective-permute-start | bytes 786440 | tf_op jit(solution)/shard_map/curvature/ppermute | solution.py:19
  197.3 10.5 %collective-permute-start.21 = (bf16[512,256]{1,0:T(8,128)(2,1)S(1)}, bf16[512,256]{1,0:T(8,128)(2,1)S(1)}, u32[]{:S(2)}, u32[]{:S(2)}) collective-permute-start(bf16[512,256]{1,0:T(8,128)(2,1)S(1)} %bitcast.69), channel_id=1, source_target_pairs={{0,1},{1,0},{2,3},{3,2},{4,5},{5,4},{6,7},{7,6},{8,9},{9,8},{10,11... | collective-permute-start | bytes 786440 | tf_op jit(solution)/shard_map/curvature/ppermute | solution.py:23
  208.1 7.5 %collective-permute-start.24 = (bf16[512,256]{1,0:T(8,128)(2,1)S(1)}, bf16[512,256]{1,0:T(8,128)(2,1)S(1)}, u32[]{:S(2)}, u32[]{:S(2)}) collective-permute-start(bf16[512,256]{1,0:T(8,128)(2,1)S(1)} %collective-permute-done.18), channel_id=1, source_target_pairs={{0,1},{1,0},{2,3},{3,2},{4,5},{5,4},{6,7},{7,6},{8,9},{9,8},{10,11... | collective-permute-start | bytes 786440 | tf_op jit(solution)/shard_map/curvature/ppermute | solution.py:23
  215.8 1.9 collective-permute-start.23
  218.0 2.4 collective-permute-start.22
  220.8 0.7 collective-permute-done.22
  222.2 15.5 %all-gather.3.cloned.1.call-done = bf16[2048,256]{1,0:T(8,128)(2,1)} async-done(((bf16[256,256]{1,0:T(8,128)(2,1)}), bf16[2048,256]{1,0:T(8,128)(2,1)}) %all-gather.3.cloned.1.call-update) | async-done | bytes 1048592 | tf_op jit(solution)/shard_map/tangent/all_gather | solution.py:123
  237.8 2.3 copy.21
  (80 shorter events, 7.6 us)
Async XLA Ops:
  7.2 2.1 copy-start
  7.2 0.9 copy-start.8
  8.1 2.1 copy-start.4
  10.3 32.6 %all-to-all-start = ((bf16[16,32,256]{2,1,0:T(8,128)(2,1)}), bf16[16,32,256]{2,1,0:T(8,128)(2,1)S(1)}, u32[]{:S(2)}, u32[]{:S(2)}) async-start(bf16[16,32,256]{2,1,0:T(8,128)(2,1)} %bitcast.2), calls=%async_computation | async-start | bytes 524288 | tf_op jit(solution)/shard_map/dispatch/all_to_all | solution.py:66
  42.8 25.2 %collective-permute-start.2 = (bf16[512,256]{1,0:T(8,128)(2,1)S(1)}, bf16[512,256]{1,0:T(8,128)(2,1)S(1)}, u32[]{:S(2)}, u32[]{:S(2)}) collective-permute-start(bf16[512,256]{1,0:T(8,128)(2,1)S(1)} %bitcast.74), channel_id=1, source_target_pairs={{0,6},{2,0},{4,2},{6,4},{1,7},{3,1},{5,3},{7,5},{8,14},{10,8},{12,... | collective-permute-start | bytes 786440 | tf_op jit(solution)/shard_map/dispatch/ppermute | solution.py:19
  48.0 14.8 %collective-permute-start.1 = (bf16[512,256]{1,0:T(8,128)(2,1)S(1)}, bf16[512,256]{1,0:T(8,128)(2,1)S(1)}, u32[]{:S(2)}, u32[]{:S(2)}) collective-permute-start(bf16[512,256]{1,0:T(8,128)(2,1)S(1)} %bitcast.75), channel_id=1, source_target_pairs={{0,2},{2,4},{4,6},{6,0},{1,3},{3,5},{5,7},{7,1},{8,10},{10,12},{12... | collective-permute-start | bytes 786440 | tf_op jit(solution)/shard_map/dispatch/ppermute | solution.py:19
  51.2 20.4 %collective-permute-start = (bf16[512,256]{1,0:T(8,128)(2,1)S(1)}, bf16[512,256]{1,0:T(8,128)(2,1)S(1)}, u32[]{:S(2)}, u32[]{:S(2)}) collective-permute-start(bf16[512,256]{1,0:T(8,128)(2,1)S(1)} %bitcast.76), channel_id=1, source_target_pairs={{0,4},{2,6},{4,0},{6,2},{1,5},{3,7},{5,1},{7,3},{8,12},{10,14},{12... | collective-permute-start | bytes 786440 | tf_op jit(solution)/shard_map/dispatch/ppermute | solution.py:19
  53.6 23.2 %collective-permute-start.3 = (bf16[512,256]{1,0:T(8,128)(2,1)S(1)}, bf16[512,256]{1,0:T(8,128)(2,1)S(1)}, u32[]{:S(2)}, u32[]{:S(2)}) collective-permute-start(bf16[512,256]{1,0:T(8,128)(2,1)S(1)} %bitcast.77), channel_id=1, source_target_pairs={{0,1},{1,0},{2,3},{3,2},{4,5},{5,4},{6,7},{7,6},{8,9},{9,8},{10,11... | collective-permute-start | bytes 786440 | tf_op jit(solution)/shard_map/dispatch/ppermute | solution.py:23
  62.8 14.5 %collective-permute-start.5 = (bf16[512,256]{1,0:T(8,128)(2,1)S(1)}, bf16[512,256]{1,0:T(8,128)(2,1)S(1)}, u32[]{:S(2)}, u32[]{:S(2)}) collective-permute-start(bf16[512,256]{1,0:T(8,128)(2,1)S(1)} %collective-permute-done.1), channel_id=1, source_target_pairs={{0,1},{1,0},{2,3},{3,2},{4,5},{5,4},{6,7},{7,6},{8,9},{9,8},{10,11... | collective-permute-start | bytes 786440 | tf_op jit(solution)/shard_map/dispatch/ppermute | solution.py:23
  68.0 10.0 %collective-permute-start.4 = (bf16[512,256]{1,0:T(8,128)(2,1)S(1)}, bf16[512,256]{1,0:T(8,128)(2,1)S(1)}, u32[]{:S(2)}, u32[]{:S(2)}) collective-permute-start(bf16[512,256]{1,0:T(8,128)(2,1)S(1)} %collective-permute-done.2), channel_id=1, source_target_pairs={{0,1},{1,0},{2,3},{3,2},{4,5},{5,4},{6,7},{7,6},{8,9},{9,8},{10,11... | collective-permute-start | bytes 786440 | tf_op jit(solution)/shard_map/dispatch/ppermute | solution.py:23
  71.6 6.1 %collective-permute-start.6 = (bf16[512,256]{1,0:T(8,128)(2,1)S(1)}, bf16[512,256]{1,0:T(8,128)(2,1)S(1)}, u32[]{:S(2)}, u32[]{:S(2)}) collective-permute-start(bf16[512,256]{1,0:T(8,128)(2,1)S(1)} %collective-permute-done), channel_id=1, source_target_pairs={{0,1},{1,0},{2,3},{3,2},{4,5},{5,4},{6,7},{7,6},{8,9},{9,8},{10,11... | collective-permute-start | bytes 786440 | tf_op jit(solution)/shard_map/dispatch/ppermute | solution.py:23
  78.0 1.1 copy-start.3
  79.6 9.2 %collective-permute-start.8 = (bf16[512,256]{1,0:T(8,128)(2,1)S(1)}, bf16[512,256]{1,0:T(8,128)(2,1)S(1)}, u32[]{:S(2)}, u32[]{:S(2)}) collective-permute-start(bf16[512,256]{1,0:T(8,128)(2,1)S(1)} %convolution_convert_fusion.2), channel_id=1, source_target_pairs={{0,1},{1,0},{2,3},{3,2},{4,5},{5,4},{6,7},{7,6},{8,9},{9,8},{10,11... | collective-permute-start | bytes 786440 | tf_op jit(solution)/shard_map/combine/ppermute | solution.py:23
  82.1 10.9 %collective-permute-start.10 = (bf16[512,256]{1,0:T(8,128)(2,1)S(1)}, bf16[512,256]{1,0:T(8,128)(2,1)S(1)}, u32[]{:S(2)}, u32[]{:S(2)}) collective-permute-start(bf16[512,256]{1,0:T(8,128)(2,1)S(1)} %convolution_convert_fusion.1), channel_id=1, source_target_pairs={{0,1},{1,0},{2,3},{3,2},{4,5},{5,4},{6,7},{7,6},{8,9},{9,8},{10,11... | collective-permute-start | bytes 786440 | tf_op jit(solution)/shard_map/combine/ppermute | solution.py:23
  84.5 10.6 %collective-permute-start.12 = (bf16[512,256]{1,0:T(8,128)(2,1)S(1)}, bf16[512,256]{1,0:T(8,128)(2,1)S(1)}, u32[]{:S(2)}, u32[]{:S(2)}) collective-permute-start(bf16[512,256]{1,0:T(8,128)(2,1)S(1)} %convolution_convert_fusion), channel_id=1, source_target_pairs={{0,1},{1,0},{2,3},{3,2},{4,5},{5,4},{6,7},{7,6},{8,9},{9,8},{10,11... | collective-permute-start | bytes 786440 | tf_op jit(solution)/shard_map/combine/ppermute | solution.py:23
  86.7 14.2 %collective-permute-start.7 = (bf16[512,256]{1,0:T(8,128)(2,1)S(1)}, bf16[512,256]{1,0:T(8,128)(2,1)S(1)}, u32[]{:S(2)}, u32[]{:S(2)}) collective-permute-start(bf16[512,256]{1,0:T(8,128)(2,1)S(1)} %convolution_convert_fusion.3), channel_id=1, source_target_pairs={{0,1},{1,0},{2,3},{3,2},{4,5},{5,4},{6,7},{7,6},{8,9},{9,8},{10,11... | collective-permute-start | bytes 786440 | tf_op jit(solution)/shard_map/combine/ppermute | solution.py:23
  89.2 22.0 %collective-permute-start.9 = (bf16[512,256]{1,0:T(8,128)(2,1)S(1)}, bf16[512,256]{1,0:T(8,128)(2,1)S(1)}, u32[]{:S(2)}, u32[]{:S(2)}) collective-permute-start(bf16[512,256]{1,0:T(8,128)(2,1)S(1)} %add_convert_fusion.3), channel_id=1, source_target_pairs={{0,4},{2,6},{4,0},{6,2},{1,5},{3,7},{5,1},{7,3},{8,12},{10,14},{12... | collective-permute-start | bytes 786440 | tf_op jit(solution)/shard_map/combine/ppermute | solution.py:19
  93.2 17.9 %collective-permute-start.11 = (bf16[512,256]{1,0:T(8,128)(2,1)S(1)}, bf16[512,256]{1,0:T(8,128)(2,1)S(1)}, u32[]{:S(2)}, u32[]{:S(2)}) collective-permute-start(bf16[512,256]{1,0:T(8,128)(2,1)S(1)} %add_convert_fusion.2), channel_id=1, source_target_pairs={{0,2},{2,4},{4,6},{6,0},{1,3},{3,5},{5,7},{7,1},{8,10},{10,12},{12... | collective-permute-start | bytes 786440 | tf_op jit(solution)/shard_map/combine/ppermute | solution.py:19
  95.5 31.2 %copy-start.7 = (bf16[256,8]{0,1:T(8,128)(2,1)S(1)}, bf16[256,8]{0,1:T(8,128)(2,1)}, u32[]{:S(2)}) copy-start(bf16[256,8]{0,1:T(8,128)(2,1)} %param.8) | copy-start | bytes 12292
  95.5 31.2 %copy-start.6 = (s32[256,8]{0,1:T(8,128)S(1)}, s32[256,8]{0,1:T(8,128)}, u32[]{:S(2)}) copy-start(s32[256,8]{0,1:T(8,128)} %param.7) | copy-start | bytes 24580
  95.5 31.2 %copy-start.9 = (s32[16]{0:T(128)S(1)}, s32[16]{0:T(128)}, u32[]{:S(2)}) copy-start(s32[16]{0:T(128)} %copy-done.8) | copy-start | bytes 196
  95.5 44.9 %copy-start.5 = (pred[16,256]{1,0:T(8,128)(4,1)S(1)}, pred[16,256]{1,0:T(8,128)(4,1)}, u32[]{:S(2)}) copy-start(pred[16,256]{1,0:T(8,128)(4,1)} %copy-done.4) | copy-start | bytes 12292
  95.5 21.0 %collective-permute-start.13 = (bf16[512,256]{1,0:T(8,128)(2,1)S(1)}, bf16[512,256]{1,0:T(8,128)(2,1)S(1)}, u32[]{:S(2)}, u32[]{:S(2)}) collective-permute-start(bf16[512,256]{1,0:T(8,128)(2,1)S(1)} %add_convert_fusion.1), channel_id=1, source_target_pairs={{0,6},{2,0},{4,2},{6,4},{1,7},{3,1},{5,3},{7,5},{8,14},{10,8},{12,... | collective-permute-start | bytes 786440 | tf_op jit(solution)/shard_map/combine/ppermute | solution.py:19
  117.3 23.0 %all-to-all-start.1 = ((bf16[16,32,256]{2,1,0:T(8,128)(2,1)}), bf16[16,32,256]{2,1,0:T(8,128)(2,1)S(1)}, u32[]{:S(2)}, u32[]{:S(2)}) async-start(bf16[16,32,256]{2,1,0:T(8,128)(2,1)} %bitcast.4), calls=%async_computation.1 | async-start | bytes 524288 | tf_op jit(solution)/shard_map/combine/all_to_all | solution.py:66
  126.7 111.1 %all-gather.3.cloned.1.call-start = ((), (), s32[]{:S(2)}) async-start(), calls=%async_computation.3 | async-start | bytes 1179648 | tf_op jit(solution)/shard_map/tangent/all_gather | solution.py:123
  140.7 9.6 %collective-permute-start.14 = (bf16[256,256]{1,0:T(8,128)(2,1)S(1)}, bf16[256,256]{1,0:T(8,128)(2,1)S(1)}, u32[]{:S(2)}, u32[]{:S(2)}) collective-permute-start(bf16[256,256]{1,0:T(8,128)(2,1)S(1)} %fusion.5), channel_id=1, source_target_pairs={{0,16},{8,24},{16,0},{24,8},{32,48},{40,56},{48,32},{56,40},{1,17}... | collective-permute-start | bytes 393224 | tf_op jit(solution)/shard_map/combine/ppermute | solution.py:27
  143.8 7.2 %collective-permute-start.15 = (bf16[256,256]{1,0:T(8,128)(2,1)S(1)}, bf16[256,256]{1,0:T(8,128)(2,1)S(1)}, u32[]{:S(2)}, u32[]{:S(2)}) collective-permute-start(bf16[256,256]{1,0:T(8,128)(2,1)S(1)} %fusion.5), channel_id=1, source_target_pairs={{0,32},{8,40},{16,48},{24,56},{32,0},{40,8},{48,16},{56,24},{1,33}... | collective-permute-start | bytes 393224 | tf_op jit(solution)/shard_map/combine/ppermute | solution.py:27
  148.2 6.9 %collective-permute-start.16 = (bf16[256,256]{1,0:T(8,128)(2,1)S(1)}, bf16[256,256]{1,0:T(8,128)(2,1)S(1)}, u32[]{:S(2)}, u32[]{:S(2)}) collective-permute-start(bf16[256,256]{1,0:T(8,128)(2,1)S(1)} %fusion.5), channel_id=1, source_target_pairs={{0,48},{8,56},{16,32},{24,40},{32,16},{40,24},{48,0},{56,8},{1,49}... | collective-permute-start | bytes 393224 | tf_op jit(solution)/shard_map/combine/ppermute | solution.py:27
  155.2 9.6 %collective-permute-start.17 = (bf16[256,256]{1,0:T(8,128)(2,1)S(1)}, bf16[256,256]{1,0:T(8,128)(2,1)S(1)}, u32[]{:S(2)}, u32[]{:S(2)}) collective-permute-start(bf16[256,256]{1,0:T(8,128)(2,1)S(1)} %add_convert_fusion.6), channel_id=1, source_target_pairs={{0,8},{8,0},{16,24},{24,16},{32,40},{40,32},{48,56},{56,48},{1,9},... | collective-permute-start | bytes 393224 | tf_op jit(solution)/shard_map/combine/ppermute | solution.py:27
  164.8 25.3 %copy-start.1 = (bf16[256,256]{1,0:T(8,128)(2,1)}, bf16[256,256]{1,0:T(8,128)(2,1)S(1)}, u32[]{:S(2)}) copy-start(bf16[256,256]{1,0:T(8,128)(2,1)S(1)} %add_convert_fusion.5) | copy-start | bytes 393220
  188.1 20.0 %collective-permute-start.18 = (bf16[512,256]{1,0:T(8,128)(2,1)S(1)}, bf16[512,256]{1,0:T(8,128)(2,1)S(1)}, u32[]{:S(2)}, u32[]{:S(2)}) collective-permute-start(bf16[512,256]{1,0:T(8,128)(2,1)S(1)} %bitcast.66), channel_id=1, source_target_pairs={{0,4},{2,6},{4,0},{6,2},{1,5},{3,7},{5,1},{7,3},{8,12},{10,14},{12... | collective-permute-start | bytes 786440 | tf_op jit(solution)/shard_map/curvature/ppermute | solution.py:19
  190.2 25.6 %collective-permute-start.19 = (bf16[512,256]{1,0:T(8,128)(2,1)S(1)}, bf16[512,256]{1,0:T(8,128)(2,1)S(1)}, u32[]{:S(2)}, u32[]{:S(2)}) collective-permute-start(bf16[512,256]{1,0:T(8,128)(2,1)S(1)} %bitcast.67), channel_id=1, source_target_pairs={{0,2},{2,4},{4,6},{6,0},{1,3},{3,5},{5,7},{7,1},{8,10},{10,12},{12... | collective-permute-start | bytes 786440 | tf_op jit(solution)/shard_map/curvature/ppermute | solution.py:19
  193.0 24.9 %collective-permute-start.20 = (bf16[512,256]{1,0:T(8,128)(2,1)S(1)}, bf16[512,256]{1,0:T(8,128)(2,1)S(1)}, u32[]{:S(2)}, u32[]{:S(2)}) collective-permute-start(bf16[512,256]{1,0:T(8,128)(2,1)S(1)} %bitcast.68), channel_id=1, source_target_pairs={{0,6},{2,0},{4,2},{6,4},{1,7},{3,1},{5,3},{7,5},{8,14},{10,8},{12,... | collective-permute-start | bytes 786440 | tf_op jit(solution)/shard_map/curvature/ppermute | solution.py:19
  197.3 23.3 %collective-permute-start.21 = (bf16[512,256]{1,0:T(8,128)(2,1)S(1)}, bf16[512,256]{1,0:T(8,128)(2,1)S(1)}, u32[]{:S(2)}, u32[]{:S(2)}) collective-permute-start(bf16[512,256]{1,0:T(8,128)(2,1)S(1)} %bitcast.69), channel_id=1, source_target_pairs={{0,1},{1,0},{2,3},{3,2},{4,5},{5,4},{6,7},{7,6},{8,9},{9,8},{10,11... | collective-permute-start | bytes 786440 | tf_op jit(solution)/shard_map/curvature/ppermute | solution.py:23
  208.1 13.9 %collective-permute-start.24 = (bf16[512,256]{1,0:T(8,128)(2,1)S(1)}, bf16[512,256]{1,0:T(8,128)(2,1)S(1)}, u32[]{:S(2)}, u32[]{:S(2)}) collective-permute-start(bf16[512,256]{1,0:T(8,128)(2,1)S(1)} %collective-permute-done.18), channel_id=1, source_target_pairs={{0,1},{1,0},{2,3},{3,2},{4,5},{5,4},{6,7},{7,6},{8,9},{9,8},{10,11... | collective-permute-start | bytes 786440 | tf_op jit(solution)/shard_map/curvature/ppermute | solution.py:23
  215.8 5.9 %collective-permute-start.23 = (bf16[512,256]{1,0:T(8,128)(2,1)S(1)}, bf16[512,256]{1,0:T(8,128)(2,1)S(1)}, u32[]{:S(2)}, u32[]{:S(2)}) collective-permute-start(bf16[512,256]{1,0:T(8,128)(2,1)S(1)} %collective-permute-done.19), channel_id=1, source_target_pairs={{0,1},{1,0},{2,3},{3,2},{4,5},{5,4},{6,7},{7,6},{8,9},{9,8},{10,11... | collective-permute-start | bytes 786440 | tf_op jit(solution)/shard_map/curvature/ppermute | solution.py:23
  218.0 3.6 %collective-permute-start.22 = (bf16[512,256]{1,0:T(8,128)(2,1)S(1)}, bf16[512,256]{1,0:T(8,128)(2,1)S(1)}, u32[]{:S(2)}, u32[]{:S(2)}) collective-permute-start(bf16[512,256]{1,0:T(8,128)(2,1)S(1)} %collective-permute-done.20), channel_id=1, source_target_pairs={{0,1},{1,0},{2,3},{3,2},{4,5},{5,4},{6,7},{7,6},{8,9},{9,8},{10,11... | collective-permute-start | bytes 786440 | tf_op jit(solution)/shard_map/curvature/ppermute | solution.py:23
  222.2 17.9 %copy-start.2 = (bf16[192,2048]{1,0:T(8,128)(2,1)}, bf16[192,2048]{1,0:T(8,128)(2,1)S(1)}, u32[]{:S(2)}) copy-start(bf16[192,2048]{1,0:T(8,128)(2,1)S(1)} %fusion.13) | copy-start | bytes 2359300
Sparse Core Ops, SparseCore 0:
  190.3 47.4 all-gather.2

commit v2 on v1

v2 whole, which is shorter than its diff:
```python
import jax
import jax.numpy as jnp
from jax import lax
from jax.sharding import Mesh, PartitionSpec as P

TOP = 8
EXP_COL = 8
CORES = 2
LINE = 4
STEPS = (2, 1, 3)


def contract_rows(left, right):
    return lax.dot_general(
        left, right, (((0,), (0,)), ((), ())), preferred_element_type=jnp.float32
    )


def shift_line(value, step):
    return lax.ppermute(value, "line", [(i, (i + step) % LINE) for i in range(LINE)])


def swap_cores(value):
    return lax.ppermute(value, "core", [(i, i ^ 1) for i in range(CORES)])


def swap_local(value, mask):
    return lax.ppermute(value, "local", [(i, i ^ mask) for i in range(EXP_COL)])


def gather_blocks(block):
    blocks = {(0, 0): block}
    for step in STEPS:
        blocks[(LINE - step, 0)] = shift_line(block, step)
    for step in (0, 1, 3, 2):
        blocks[(step, 1)] = swap_cores(blocks[(step, 0)])
    return blocks


def exchange_blocks(piece):
    steps = (*STEPS, 0)
    swapped = swap_cores(jnp.stack([piece(step, 1) for step in steps]))
    pairs = {step: jnp.stack([piece(step, 0), swapped[i]]) for i, step in enumerate(steps)}
    blocks = {}
    for step in STEPS:
        arrived = shift_line(pairs[step], step)
        blocks[(LINE - step, 0)], blocks[(LINE - step, 1)] = arrived[0], arrived[1]
    blocks[(0, 0)], blocks[(0, 1)] = pairs[0][0], pairs[0][1]
    return blocks


def shards(tokens, routes, combine, gate_weight, up_weight, direction):
    n_expert = lax.axis_size("expert")
    col_tok, width = tokens.shape
    unit_count = gate_weight.shape[0]
    cols = width // (LINE * CORES)
    slot_count = 2 * col_tok * TOP // (EXP_COL * n_expert)
    rows = n_expert * slot_count
    local_index = lax.axis_index("local")
    line_index = lax.axis_index("line")
    core_index = lax.axis_index("core")

    def first_col(step, other):
        line = (line_index + step) & (LINE - 1)
        return (line * CORES + (core_index ^ other)) * cols

    def columns(weight, step, other):
        return lax.dynamic_slice_in_dim(weight, first_col(step, other), cols, 1)

    def assemble(blocks, height):
        whole = jnp.zeros((height, width), jnp.bfloat16)
        for (step, other), block in blocks.items():
            whole = lax.dynamic_update_slice_in_dim(whole, block, first_col(step, other), 1)
        return whole

    with jax.named_scope("routing"):
        owner_ids = jnp.arange(n_expert, dtype=jnp.int32) * EXP_COL + local_index
        matches = routes[None, :, :] == owner_ids[:, None, None]
        member = jnp.any(matches, axis=2)
        weight_tok = jnp.sum(
            jnp.where(matches, combine[None, :, :].astype(jnp.float32), 0.0), axis=2
        )
        slot_rank = jnp.cumsum(member.astype(jnp.int32), axis=1) - 1
        slot_ids = jnp.arange(slot_count, dtype=jnp.int32)
        picked_slots = member[:, None, :] & (slot_rank[:, None, :] == slot_ids[None, :, None])
        select = picked_slots.astype(jnp.bfloat16).reshape(rows, col_tok)
        weighted = jnp.where(picked_slots, weight_tok[:, None, :], 0.0)
        slot_weight = jnp.sum(weighted, axis=2).reshape(rows, 1)
        spread = weighted.astype(jnp.bfloat16).reshape(rows, col_tok)

    def over_planes(slots):
        moved = lax.all_to_all(
            slots.reshape(n_expert, slot_count, cols), "expert", 0, 0, tiled=True
        )
        return moved.reshape(rows, cols)

    with jax.named_scope("dispatch"):
        outgoing = jnp.dot(select, columns(tokens, 0, 0), preferred_element_type=jnp.float32)
        arrived = over_planes(outgoing.astype(jnp.bfloat16))

    with jax.named_scope("direction"):
        direction_blocks = exchange_blocks(lambda step, other: columns(direction, step, other))

    with jax.named_scope("experts"):
        both = jnp.concatenate([gate_weight, up_weight], axis=0)
        value = 0.0
        for (step, other), block in gather_blocks(arrived).items():
            value += lax.dot_general(
                columns(both, step, other),
                block,
                (((1,), (1,)), ((), ())),
                preferred_element_type=jnp.float32,
            )
        hidden = (jax.nn.silu(value[:unit_count]) * value[unit_count:]).astype(jnp.bfloat16)
        hidden_blocks = gather_blocks(hidden)

    with jax.named_scope("combine"):
        expert_out = 0.0
        for key, block in hidden_blocks.items():
            expert_out += contract_rows(block, direction_blocks[key])
        returned = over_planes(expert_out.astype(jnp.bfloat16))
        part = lax.optimization_barrier(contract_rows(spread, returned).astype(jnp.bfloat16))
        near = [swap_local(part, mask).astype(jnp.float32) for mask in (4, 2, 6)]
        half = (part.astype(jnp.float32) + near[1]) + (near[0] + near[2])
        half = lax.optimization_barrier(half.astype(jnp.bfloat16))
        total = half.astype(jnp.float32) + swap_local(half, 1).astype(jnp.float32)
        tangent_cols = total.astype(jnp.bfloat16)

    with jax.named_scope("curvature"):
        picked = jnp.dot(select, tangent_cols, preferred_element_type=jnp.float32)
        scaled = over_planes((picked * slot_weight).astype(jnp.bfloat16))

    with jax.named_scope("tangent"):
        tangent_out = assemble(gather_blocks(tangent_cols), col_tok)

    with jax.named_scope("curvature"):
        def product(step, other):
            value = jnp.dot(
                hidden_blocks[(step, other)], scaled, preferred_element_type=jnp.float32
            )
            return value.astype(jnp.bfloat16)

        curvature = assemble(exchange_blocks(product), unit_count)
    return tangent_out, curvature


def solution(mesh):
    n_expert = mesh.shape["expert"]
    fine = Mesh(
        mesh.devices.reshape(n_expert, EXP_COL, LINE, CORES), ("expert", "local", "line", "core")
    )
    by_block = P("expert", None)
    by_device = P(("expert", "local", "line", "core"), None)
    return jax.shard_map(
        shards,
        mesh=fine,
        in_specs=(by_block, by_block, by_block, by_device, by_device, by_device),
        out_specs=(by_block, by_device),
        check_vma=False,
    )
```

time: 248 us -> 237 us (0.956)
  blocking collectives: 23 us -> 0 us
  starting transfers between devices: 125 us -> 148 us
  between operations: 14.8 us -> 1.7 us
  waiting for transfers between devices: 67.3 us -> 58.6 us
  matrix products: 7.73 us -> 15.8 us
  other arithmetic: 3.14 us -> 5.74 us
    all_to_all x1 -> x0, blocking collectives: 23 us -> none  [over_planes(): lax.all_to_all(slots.reshape(n_expert, slot_count, cols), 'expert', 0, 0,...]
    ppermute x9 -> x15, waiting for transfers between devices: 16.9 us -> 35.4 us  [shift_line(): lax.ppermute(value, 'line', [(i, (i + step) % LINE) for i in range(LINE)])]
    all_gather x1 -> x0, waiting for transfers between devices: 15.5 us -> none  [shards(): tangent_out = lax.all_gather(tangent_cols, ('line', 'core'))]
    ppermute x9 -> x15, starting transfers between devices: 29.5 us -> 41.9 us  [shift_line(): lax.ppermute(value, 'line', [(i, (i + step) % LINE) for i in range(LINE)])]
    all_to_all x2 -> x3, waiting for transfers between devices: 25.5 us -> 13.6 us  [over_planes(): lax.all_to_all(slots.reshape(n_expert, slot_count, cols), 'expert', 0, 0,...]
    all_to_all x2 -> x3, starting transfers between devices: 28.7 us -> 37.4 us  [over_planes(): lax.all_to_all(slots.reshape(n_expert, slot_count, cols), 'expert', 0, 0,...]
    ppermute x4, starting transfers between devices: 15.1 us -> 21.7 us  [swap_local(): return lax.ppermute(value, 'local', [(i, i ^ mask) for i in range(EXP_COL)])]
    dot_general x9, matrix products: 1.99 us -> 7.7 us  [contract_rows(): lax.dot_general(left, right, (((0,), (0,)), ((), ())), preferred_element_...]
  transfers between devices with their start and end apart: 28 -> 36, of which waited for: 10 -> 15; matrix products, arithmetic and copies ran while one was open for 3% -> 6% of each run, Pallas kernels for 0% -> 0%
where the time goes in v2:
time: 237 us; the launch traced here: 234 us
  starting transfers between devices  148 us (62%)
  waiting for transfers between devices  58.6 us (25%)
  matrix products  15.8 us (7%)
  other arithmetic  5.74 us (2%)
  local copies, waits for them, and re-layouts  4.36 us (2%)
    ppermute x14, starting transfers between devices, swap_cores(): return lax.ppermute(value, 'core', [(i, i ^ 1) for i in range(CORES)])  46.7 us
    ppermute x15, starting transfers between devices, shift_line(): lax.ppermute(value, 'line', [(i, (i + step) % LINE) for i in range(LINE)])  41.9 us
    all_to_all x3, starting transfers between devices, over_planes(): lax.all_to_all(slots.reshape(n_expert, slot_count, cols), 'expert', 0, 0,...  37.4 us
    ppermute x15, waiting for transfers between devices, shift_line(): lax.ppermute(value, 'line', [(i, (i + step) % LINE) for i in range(LINE)])  35.4 us
    ppermute x4, starting transfers between devices, swap_local(): return lax.ppermute(value, 'local', [(i, i ^ mask) for i in range(EXP_COL)])  21.7 us
    all_to_all x3, waiting for transfers between devices, over_planes(): lax.all_to_all(slots.reshape(n_expert, slot_count, cols), 'expert', 0, 0,...  13.6 us
    dot_general x9, matrix products, contract_rows(): lax.dot_general(left, right, (((0,), (0,)), ((), ())), preferred_element_...  7.7 us
    ppermute x4, waiting for transfers between devices, swap_local(): return lax.ppermute(value, 'local', [(i, i ^ mask) for i in range(EXP_COL)])  6.86 us
  transfers between devices with their start and end apart: 36, of which 15 were waited for; matrix products, arithmetic and copies ran while one was open for 6% of the time, Pallas kernels for 0%

profile of v2, /device:TPU:1, one launch (start us, length us, event | category | flops | bytes accessed | tf_op | source)
XLA Modules:
  0.0 233.9 jit_solution(9041669408380345327)
XLA Ops:
  3.7 19.4 %all-to-all-start = ((bf16[16,32,256]{2,1,0:T(8,128)(2,1)}), bf16[16,32,256]{2,1,0:T(8,128)(2,1)S(1)}, u32[]{:S(2)}, u32[]{:S(2)}) async-start(bf16[16,32,256]{2,1,0:T(8,128)(2,1)} %bitcast.2), calls=%async_computation | async-start | bytes 524288 | tf_op jit(solution)/shard_map/dispatch/all_to_all | solution.py:92
  23.4 3.0 %collective-permute-start.8 = (bf16[4,192,256]{2,1,0:T(8,128)(2,1)S(1)}, bf16[4,192,256]{2,1,0:T(8,128)(2,1)S(1)}, u32[]{:S(2)}, u32[]{:S(2)}) collective-permute-start(bf16[4,192,256]{2,1,0:T(8,128)(2,1)S(1)} %pad_maximum_fusion), channel_id=1, source_target_pairs={{0,1},{1,0},{2,3},{3,2},{4,5},{5,4},{6,7},{7,6},{8,9},{9,8},{10,11... | collective-permute-start | bytes 1179656 | tf_op jit(solution)/shard_map/direction/ppermute | solution.py:24
  29.1 4.2 %collective-permute-start.9 = (bf16[2,192,256]{2,1,0:T(8,128)(2,1)}, bf16[2,192,256]{2,1,0:T(8,128)(2,1)}, u32[]{:S(2)}, u32[]{:S(2)}) collective-permute-start(bf16[2,192,256]{2,1,0:T(8,128)(2,1)} %pad_maximum_fusion.2), channel_id=1, source_target_pairs={{0,4},{2,6},{4,0},{6,2},{1,5},{3,7},{5,1},{7,3},{8,12},{10,14},{12... | collective-permute-start | bytes 589832 | tf_op jit(solution)/shard_map/direction/ppermute | solution.py:20
  34.0 3.0 %collective-permute-start.13 = (bf16[2,192,256]{2,1,0:T(8,128)(2,1)}, bf16[2,192,256]{2,1,0:T(8,128)(2,1)}, u32[]{:S(2)}, u32[]{:S(2)}) collective-permute-start(bf16[2,192,256]{2,1,0:T(8,128)(2,1)} %pad_maximum_fusion.4), channel_id=1, source_target_pairs={{0,6},{2,0},{4,2},{6,4},{1,7},{3,1},{5,3},{7,5},{8,14},{10,8},{12,... | collective-permute-start | bytes 589832 | tf_op jit(solution)/shard_map/direction/ppermute | solution.py:20
  37.0 7.4 %collective-permute-start.3 = (bf16[512,256]{1,0:T(8,128)(2,1)S(1)}, bf16[512,256]{1,0:T(8,128)(2,1)S(1)}, u32[]{:S(2)}, u32[]{:S(2)}) collective-permute-start(bf16[512,256]{1,0:T(8,128)(2,1)S(1)} %bitcast.146), channel_id=1, source_target_pairs={{0,1},{1,0},{2,3},{3,2},{4,5},{5,4},{6,7},{7,6},{8,9},{9,8},{10,11... | collective-permute-start | bytes 786440 | tf_op jit(solution)/shard_map/experts/ppermute | solution.py:24
  45.3 3.2 %collective-permute-start.11 = (bf16[2,192,256]{2,1,0:T(8,128)(2,1)S(1)}, bf16[2,192,256]{2,1,0:T(8,128)(2,1)S(1)}, u32[]{:S(2)}, u32[]{:S(2)}) collective-permute-start(bf16[2,192,256]{2,1,0:T(8,128)(2,1)S(1)} %pad_maximum_fusion.3), channel_id=1, source_target_pairs={{0,2},{2,4},{4,6},{6,0},{1,3},{3,5},{5,7},{7,1},{8,10},{10,12},{12... | collective-permute-start | bytes 589832 | tf_op jit(solution)/shard_map/direction/ppermute | solution.py:20
  48.5 4.0 %collective-permute-start.2 = (bf16[512,256]{1,0:T(8,128)(2,1)S(1)}, bf16[512,256]{1,0:T(8,128)(2,1)S(1)}, u32[]{:S(2)}, u32[]{:S(2)}) collective-permute-start(bf16[512,256]{1,0:T(8,128)(2,1)S(1)} %bitcast.147), channel_id=1, source_target_pairs={{0,6},{2,0},{4,2},{6,4},{1,7},{3,1},{5,3},{7,5},{8,14},{10,8},{12,... | collective-permute-start | bytes 786440 | tf_op jit(solution)/shard_map/experts/ppermute | solution.py:20
  52.8 2.3 %collective-permute-start = (bf16[512,256]{1,0:T(8,128)(2,1)S(1)}, bf16[512,256]{1,0:T(8,128)(2,1)S(1)}, u32[]{:S(2)}, u32[]{:S(2)}) collective-permute-start(bf16[512,256]{1,0:T(8,128)(2,1)S(1)} %bitcast.149), channel_id=1, source_target_pairs={{0,4},{2,6},{4,0},{6,2},{1,5},{3,7},{5,1},{7,3},{8,12},{10,14},{12... | collective-permute-start | bytes 786440 | tf_op jit(solution)/shard_map/experts/ppermute | solution.py:20
  55.4 6.1 %collective-permute-done.2 = bf16[512,256]{1,0:T(8,128)(2,1)S(1)} collective-permute-done((bf16[512,256]{1,0:T(8,128)(2,1)S(1)}, bf16[512,256]{1,0:T(8,128)(2,1)S(1)}, u32[]{:S(2)}, u32[]{:S(2)}) %collective-permute-start.2) | collective-permute-done | bytes 262176 | tf_op jit(solution)/shard_map/experts/ppermute | solution.py:20
  61.5 2.4 %collective-permute-start.1 = (bf16[512,256]{1,0:T(8,128)(2,1)S(1)}, bf16[512,256]{1,0:T(8,128)(2,1)S(1)}, u32[]{:S(2)}, u32[]{:S(2)}) collective-permute-start(bf16[512,256]{1,0:T(8,128)(2,1)S(1)} %bitcast.150), channel_id=1, source_target_pairs={{0,2},{2,4},{4,6},{6,0},{1,3},{3,5},{5,7},{7,1},{8,10},{10,12},{12... | collective-permute-start | bytes 786440 | tf_op jit(solution)/shard_map/experts/ppermute | solution.py:20
  64.3 14.1 %collective-permute-done = bf16[512,256]{1,0:T(8,128)(2,1)S(1)} collective-permute-done((bf16[512,256]{1,0:T(8,128)(2,1)S(1)}, bf16[512,256]{1,0:T(8,128)(2,1)S(1)}, u32[]{:S(2)}, u32[]{:S(2)}) %collective-permute-start) | collective-permute-done | bytes 262176 | tf_op jit(solution)/shard_map/experts/ppermute | solution.py:20
  78.4 2.4 %collective-permute-start.6 = (bf16[512,256]{1,0:T(8,128)(2,1)S(1)}, bf16[512,256]{1,0:T(8,128)(2,1)S(1)}, u32[]{:S(2)}, u32[]{:S(2)}) collective-permute-start(bf16[512,256]{1,0:T(8,128)(2,1)S(1)} %collective-permute-done), channel_id=1, source_target_pairs={{0,1},{1,0},{2,3},{3,2},{4,5},{5,4},{6,7},{7,6},{8,9},{9,8},{10,11... | collective-permute-start | bytes 786440 | tf_op jit(solution)/shard_map/experts/ppermute | solution.py:24
  81.1 2.0 collective-permute-start.5
  83.4 2.4 %collective-permute-start.4 = (bf16[512,256]{1,0:T(8,128)(2,1)S(1)}, bf16[512,256]{1,0:T(8,128)(2,1)S(1)}, u32[]{:S(2)}, u32[]{:S(2)}) collective-permute-start(bf16[512,256]{1,0:T(8,128)(2,1)S(1)} %collective-permute-done.2), channel_id=1, source_target_pairs={{0,1},{1,0},{2,3},{3,2},{4,5},{5,4},{6,7},{7,6},{8,9},{9,8},{10,11... | collective-permute-start | bytes 786440 | tf_op jit(solution)/shard_map/experts/ppermute | solution.py:24
  87.3 1.9 collective-permute-start.7
  89.2 1.9 collective-permute-start.12
  92.3 2.3 collective-permute-start.14
  94.6 1.8 collective-permute-done.7
  96.4 1.9 collective-permute-start.10
  99.5 6.3 %collective-permute-start.17 = (bf16[192,512]{1,0:T(8,128)(2,1)S(1)}, bf16[192,512]{1,0:T(8,128)(2,1)S(1)}, u32[]{:S(2)}, u32[]{:S(2)}) collective-permute-start(bf16[192,512]{1,0:T(8,128)(2,1)S(1)} %collective-permute-done.7), channel_id=1, source_target_pairs={{0,1},{1,0},{2,3},{3,2},{4,5},{5,4},{6,7},{7,6},{8,9},{9,8},{10,11... | collective-permute-start | bytes 589832 | tf_op jit(solution)/shard_map/experts/ppermute | solution.py:24
  105.9 2.6 %collective-permute-done.10 = bf16[192,512]{1,0:T(8,128)(2,1)S(1)} collective-permute-done((bf16[192,512]{1,0:T(8,128)(2,1)S(1)}, bf16[192,512]{1,0:T(8,128)(2,1)S(1)}, u32[]{:S(2)}, u32[]{:S(2)}) %collective-permute-start.10) | collective-permute-done | bytes 196640 | tf_op jit(solution)/shard_map/experts/ppermute | solution.py:20
  108.5 3.5 %collective-permute-start.16 = (bf16[192,512]{1,0:T(8,128)(2,1)S(1)}, bf16[192,512]{1,0:T(8,128)(2,1)S(1)}, u32[]{:S(2)}, u32[]{:S(2)}) collective-permute-start(bf16[192,512]{1,0:T(8,128)(2,1)S(1)} %collective-permute-done.10), channel_id=1, source_target_pairs={{0,1},{1,0},{2,3},{3,2},{4,5},{5,4},{6,7},{7,6},{8,9},{9,8},{10,11... | collective-permute-start | bytes 589832 | tf_op jit(solution)/shard_map/experts/ppermute | solution.py:24
  112.0 1.9 collective-permute-start.15
  117.3 1.9 fusion.8
  119.2 7.6 %all-to-all-start.1 = ((bf16[16,32,256]{2,1,0:T(8,128)(2,1)}), bf16[16,32,256]{2,1,0:T(8,128)(2,1)S(1)}, u32[]{:S(2)}, u32[]{:S(2)}) async-start(bf16[16,32,256]{2,1,0:T(8,128)(2,1)} %bitcast.18), calls=%async_computation.1 | async-start | bytes 524288 | tf_op jit(solution)/shard_map/combine/all_to_all | solution.py:92
  126.9 13.6 %all-to-all-done.1 = bf16[16,32,256]{2,1,0:T(8,128)(2,1)S(1)} async-done(((bf16[16,32,256]{2,1,0:T(8,128)(2,1)}), bf16[16,32,256]{2,1,0:T(8,128)(2,1)S(1)}, u32[]{:S(2)}, u32[]{:S(2)}) %all-to-all-start.1) | async-done | bytes 262176 | tf_op jit(solution)/shard_map/combine/all_to_all | solution.py:92
  140.8 3.1 %collective-permute-start.18 = (bf16[256,256]{1,0:T(8,128)(2,1)S(1)}, bf16[256,256]{1,0:T(8,128)(2,1)S(1)}, u32[]{:S(2)}, u32[]{:S(2)}) collective-permute-start(bf16[256,256]{1,0:T(8,128)(2,1)S(1)} %fusion.10), channel_id=1, source_target_pairs={{0,16},{8,24},{16,0},{24,8},{32,48},{40,56},{48,32},{56,40},{1,17}... | collective-permute-start | bytes 393224 | tf_op jit(solution)/shard_map/combine/ppermute | solution.py:28
  143.9 4.4 %collective-permute-start.19 = (bf16[256,256]{1,0:T(8,128)(2,1)S(1)}, bf16[256,256]{1,0:T(8,128)(2,1)S(1)}, u32[]{:S(2)}, u32[]{:S(2)}) collective-permute-start(bf16[256,256]{1,0:T(8,128)(2,1)S(1)} %fusion.10), channel_id=1, source_target_pairs={{0,32},{8,40},{16,48},{24,56},{32,0},{40,8},{48,16},{56,24},{1,33}... | collective-permute-start | bytes 393224 | tf_op jit(solution)/shard_map/combine/ppermute | solution.py:28
  148.3 2.1 collective-permute-start.20
  151.1 4.1 %collective-permute-done.20 = bf16[256,256]{1,0:T(8,128)(2,1)S(1)} collective-permute-done((bf16[256,256]{1,0:T(8,128)(2,1)S(1)}, bf16[256,256]{1,0:T(8,128)(2,1)S(1)}, u32[]{:S(2)}, u32[]{:S(2)}) %collective-permute-start.20) | collective-permute-done | bytes 131104 | tf_op jit(solution)/shard_map/combine/ppermute | solution.py:28
  155.3 12.1 %collective-permute-start.21 = (bf16[256,256]{1,0:T(8,128)(2,1)S(1)}, bf16[256,256]{1,0:T(8,128)(2,1)S(1)}, u32[]{:S(2)}, u32[]{:S(2)}) collective-permute-start(bf16[256,256]{1,0:T(8,128)(2,1)S(1)} %add_convert_fusion.1), channel_id=1, source_target_pairs={{0,8},{8,0},{16,24},{24,16},{32,40},{40,32},{48,56},{56,48},{1,9},... | collective-permute-start | bytes 393224 | tf_op jit(solution)/shard_map/combine/ppermute | solution.py:28
  167.6 2.1 collective-permute-done.21
  172.4 10.5 %all-to-all-start.2 = ((bf16[16,32,256]{2,1,0:T(8,128)(2,1)}), bf16[16,32,256]{2,1,0:T(8,128)(2,1)S(1)}, u32[]{:S(2)}, u32[]{:S(2)}) async-start(bf16[16,32,256]{2,1,0:T(8,128)(2,1)} %bitcast.20), calls=%async_computation.2 | async-start | bytes 524288 | tf_op jit(solution)/shard_map/curvature/all_to_all | solution.py:92
  182.8 1.9 collective-permute-start.22
  184.8 3.6 %collective-permute-start.23 = (bf16[256,256]{1,0:T(8,128)(2,1)}, bf16[256,256]{1,0:T(8,128)(2,1)S(1)}, u32[]{:S(2)}, u32[]{:S(2)}) collective-permute-start(bf16[256,256]{1,0:T(8,128)(2,1)} %copy-done.9), channel_id=1, source_target_pairs={{0,2},{2,4},{4,6},{6,0},{1,3},{3,5},{5,7},{7,1},{8,10},{10,12},{12... | collective-permute-start | bytes 393224 | tf_op jit(solution)/shard_map/tangent/ppermute | solution.py:20
  188.4 3.4 %collective-permute-start.24 = (bf16[256,256]{1,0:T(8,128)(2,1)}, bf16[256,256]{1,0:T(8,128)(2,1)S(1)}, u32[]{:S(2)}, u32[]{:S(2)}) collective-permute-start(bf16[256,256]{1,0:T(8,128)(2,1)} %copy-done.9), channel_id=1, source_target_pairs={{0,6},{2,0},{4,2},{6,4},{1,7},{3,1},{5,3},{7,5},{8,14},{10,8},{12,... | collective-permute-start | bytes 393224 | tf_op jit(solution)/shard_map/tangent/ppermute | solution.py:20
  191.9 7.3 %collective-permute-start.25 = (bf16[256,256]{1,0:T(8,128)(2,1)}, bf16[256,256]{1,0:T(8,128)(2,1)S(1)}, u32[]{:S(2)}, u32[]{:S(2)}) collective-permute-start(bf16[256,256]{1,0:T(8,128)(2,1)} %copy-done.9), channel_id=1, source_target_pairs={{0,1},{1,0},{2,3},{3,2},{4,5},{5,4},{6,7},{7,6},{8,9},{9,8},{10,11... | collective-permute-start | bytes 393224 | tf_op jit(solution)/shard_map/tangent/ppermute | solution.py:24
  199.2 1.9 collective-permute-start.28
  201.1 2.4 %collective-permute-start.27 = (bf16[256,256]{1,0:T(8,128)(2,1)S(1)}, bf16[256,256]{1,0:T(8,128)(2,1)S(1)}, u32[]{:S(2)}, u32[]{:S(2)}) collective-permute-start(bf16[256,256]{1,0:T(8,128)(2,1)S(1)} %collective-permute-done.23), channel_id=1, source_target_pairs={{0,1},{1,0},{2,3},{3,2},{4,5},{5,4},{6,7},{7,6},{8,9},{9,8},{10,11... | collective-permute-start | bytes 393224 | tf_op jit(solution)/shard_map/tangent/ppermute | solution.py:24
  203.6 1.9 collective-permute-start.26
  206.9 1.4 fusion.13
  210.0 2.1 collective-permute-start.29
  213.7 2.7 %collective-permute-start.30 = (bf16[2,192,256]{2,1,0:T(8,128)(2,1)S(1)}, bf16[2,192,256]{2,1,0:T(8,128)(2,1)S(1)}, u32[]{:S(2)}, u32[]{:S(2)}) collective-permute-start(bf16[2,192,256]{2,1,0:T(8,128)(2,1)S(1)} %pad_maximum_fusion.5), channel_id=1, source_target_pairs={{0,4},{2,6},{4,0},{6,2},{1,5},{3,7},{5,1},{7,3},{8,12},{10,14},{12... | collective-permute-start | bytes 589832 | tf_op jit(solution)/shard_map/curvature/ppermute | solution.py:20
  216.4 3.1 %collective-permute-start.32 = (bf16[2,192,256]{2,1,0:T(8,128)(2,1)S(1)}, bf16[2,192,256]{2,1,0:T(8,128)(2,1)S(1)}, u32[]{:S(2)}, u32[]{:S(2)}) collective-permute-start(bf16[2,192,256]{2,1,0:T(8,128)(2,1)S(1)} %pad_maximum_fusion.7), channel_id=1, source_target_pairs={{0,6},{2,0},{4,2},{6,4},{1,7},{3,1},{5,3},{7,5},{8,14},{10,8},{12,... | collective-permute-start | bytes 589832 | tf_op jit(solution)/shard_map/curvature/ppermute | solution.py:20
  219.6 2.2 collective-permute-start.31
  221.8 6.0 %collective-permute-done.30 = bf16[2,192,256]{2,1,0:T(8,128)(2,1)S(1)} collective-permute-done((bf16[2,192,256]{2,1,0:T(8,128)(2,1)S(1)}, bf16[2,192,256]{2,1,0:T(8,128)(2,1)S(1)}, u32[]{:S(2)}, u32[]{:S(2)}) %collective-permute-start.30) | collective-permute-done | bytes 196640 | tf_op jit(solution)/shard_map/curvature/ppermute | solution.py:20
  227.9 3.1 %collective-permute-done.31 = bf16[2,192,256]{2,1,0:T(8,128)(2,1)S(1)} collective-permute-done((bf16[2,192,256]{2,1,0:T(8,128)(2,1)S(1)}, bf16[2,192,256]{2,1,0:T(8,128)(2,1)S(1)}, u32[]{:S(2)}, u32[]{:S(2)}) %collective-permute-start.31) | collective-permute-done | bytes 196640 | tf_op jit(solution)/shard_map/curvature/ppermute | solution.py:20
  231.0 1.7 collective-permute-done.32
  (124 shorter events, 26.1 us)
Async XLA Ops:
  0.6 2.2 copy-start
  0.6 22.6 %copy-start.3 = (bf16[192,2048]{1,0:T(8,128)(2,1)S(1)}, bf16[192,2048]{1,0:T(8,128)(2,1)}, u32[]{:S(2)}) copy-start(bf16[192,2048]{1,0:T(8,128)(2,1)} %param.11) | copy-start | bytes 2359300
  3.7 33.2 %all-to-all-start = ((bf16[16,32,256]{2,1,0:T(8,128)(2,1)}), bf16[16,32,256]{2,1,0:T(8,128)(2,1)S(1)}, u32[]{:S(2)}, u32[]{:S(2)}) async-start(bf16[16,32,256]{2,1,0:T(8,128)(2,1)} %bitcast.2), calls=%async_computation | async-start | bytes 524288 | tf_op jit(solution)/shard_map/dispatch/all_to_all | solution.py:92
  23.2 4.4 %copy-start.2 = (bf16[192,2048]{1,0:T(8,128)(2,1)S(1)}, bf16[192,2048]{1,0:T(8,128)(2,1)}, u32[]{:S(2)}) copy-start(bf16[192,2048]{1,0:T(8,128)(2,1)} %param.10) | copy-start | bytes 2359300
  23.4 4.3 %collective-permute-start.8 = (bf16[4,192,256]{2,1,0:T(8,128)(2,1)S(1)}, bf16[4,192,256]{2,1,0:T(8,128)(2,1)S(1)}, u32[]{:S(2)}, u32[]{:S(2)}) collective-permute-start(bf16[4,192,256]{2,1,0:T(8,128)(2,1)S(1)} %pad_maximum_fusion), channel_id=1, source_target_pairs={{0,1},{1,0},{2,3},{3,2},{4,5},{5,4},{6,7},{7,6},{8,9},{9,8},{10,11... | collective-permute-start | bytes 1179656 | tf_op jit(solution)/shard_map/direction/ppermute | solution.py:24
  29.1 63.2 %collective-permute-start.9 = (bf16[2,192,256]{2,1,0:T(8,128)(2,1)}, bf16[2,192,256]{2,1,0:T(8,128)(2,1)}, u32[]{:S(2)}, u32[]{:S(2)}) collective-permute-start(bf16[2,192,256]{2,1,0:T(8,128)(2,1)} %pad_maximum_fusion.2), channel_id=1, source_target_pairs={{0,4},{2,6},{4,0},{6,2},{1,5},{3,7},{5,1},{7,3},{8,12},{10,14},{12... | collective-permute-start | bytes 589832 | tf_op jit(solution)/shard_map/direction/ppermute | solution.py:20
  34.0 65.5 %collective-permute-start.13 = (bf16[2,192,256]{2,1,0:T(8,128)(2,1)}, bf16[2,192,256]{2,1,0:T(8,128)(2,1)}, u32[]{:S(2)}, u32[]{:S(2)}) collective-permute-start(bf16[2,192,256]{2,1,0:T(8,128)(2,1)} %pad_maximum_fusion.4), channel_id=1, source_target_pairs={{0,6},{2,0},{4,2},{6,4},{1,7},{3,1},{5,3},{7,5},{8,14},{10,8},{12,... | collective-permute-start | bytes 589832 | tf_op jit(solution)/shard_map/direction/ppermute | solution.py:20
  37.0 15.8 %collective-permute-start.3 = (bf16[512,256]{1,0:T(8,128)(2,1)S(1)}, bf16[512,256]{1,0:T(8,128)(2,1)S(1)}, u32[]{:S(2)}, u32[]{:S(2)}) collective-permute-start(bf16[512,256]{1,0:T(8,128)(2,1)S(1)} %bitcast.146), channel_id=1, source_target_pairs={{0,1},{1,0},{2,3},{3,2},{4,5},{5,4},{6,7},{7,6},{8,9},{9,8},{10,11... | collective-permute-start | bytes 786440 | tf_op jit(solution)/shard_map/experts/ppermute | solution.py:24
  45.3 70.1 %collective-permute-start.11 = (bf16[2,192,256]{2,1,0:T(8,128)(2,1)S(1)}, bf16[2,192,256]{2,1,0:T(8,128)(2,1)S(1)}, u32[]{:S(2)}, u32[]{:S(2)}) collective-permute-start(bf16[2,192,256]{2,1,0:T(8,128)(2,1)S(1)} %pad_maximum_fusion.3), channel_id=1, source_target_pairs={{0,2},{2,4},{4,6},{6,0},{1,3},{3,5},{5,7},{7,1},{8,10},{10,12},{12... | collective-permute-start | bytes 589832 | tf_op jit(solution)/shard_map/direction/ppermute | solution.py:20
  48.5 13.0 %collective-permute-start.2 = (bf16[512,256]{1,0:T(8,128)(2,1)S(1)}, bf16[512,256]{1,0:T(8,128)(2,1)S(1)}, u32[]{:S(2)}, u32[]{:S(2)}) collective-permute-start(bf16[512,256]{1,0:T(8,128)(2,1)S(1)} %bitcast.147), channel_id=1, source_target_pairs={{0,6},{2,0},{4,2},{6,4},{1,7},{3,1},{5,3},{7,5},{8,14},{10,8},{12,... | collective-permute-start | bytes 786440 | tf_op jit(solution)/shard_map/experts/ppermute | solution.py:20
  52.8 25.6 %collective-permute-start = (bf16[512,256]{1,0:T(8,128)(2,1)S(1)}, bf16[512,256]{1,0:T(8,128)(2,1)S(1)}, u32[]{:S(2)}, u32[]{:S(2)}) collective-permute-start(bf16[512,256]{1,0:T(8,128)(2,1)S(1)} %bitcast.149), channel_id=1, source_target_pairs={{0,4},{2,6},{4,0},{6,2},{1,5},{3,7},{5,1},{7,3},{8,12},{10,14},{12... | collective-permute-start | bytes 786440 | tf_op jit(solution)/shard_map/experts/ppermute | solution.py:20
  61.5 19.5 %collective-permute-start.1 = (bf16[512,256]{1,0:T(8,128)(2,1)S(1)}, bf16[512,256]{1,0:T(8,128)(2,1)S(1)}, u32[]{:S(2)}, u32[]{:S(2)}) collective-permute-start(bf16[512,256]{1,0:T(8,128)(2,1)S(1)} %bitcast.150), channel_id=1, source_target_pairs={{0,2},{2,4},{4,6},{6,0},{1,3},{3,5},{5,7},{7,1},{8,10},{10,12},{12... | collective-permute-start | bytes 786440 | tf_op jit(solution)/shard_map/experts/ppermute | solution.py:20
  78.4 5.0 %collective-permute-start.6 = (bf16[512,256]{1,0:T(8,128)(2,1)S(1)}, bf16[512,256]{1,0:T(8,128)(2,1)S(1)}, u32[]{:S(2)}, u32[]{:S(2)}) collective-permute-start(bf16[512,256]{1,0:T(8,128)(2,1)S(1)} %collective-permute-done), channel_id=1, source_target_pairs={{0,1},{1,0},{2,3},{3,2},{4,5},{5,4},{6,7},{7,6},{8,9},{9,8},{10,11... | collective-permute-start | bytes 786440 | tf_op jit(solution)/shard_map/experts/ppermute | solution.py:24
  81.1 5.0 %collective-permute-start.5 = (bf16[512,256]{1,0:T(8,128)(2,1)S(1)}, bf16[512,256]{1,0:T(8,128)(2,1)S(1)}, u32[]{:S(2)}, u32[]{:S(2)}) collective-permute-start(bf16[512,256]{1,0:T(8,128)(2,1)S(1)} %collective-permute-done.1), channel_id=1, source_target_pairs={{0,1},{1,0},{2,3},{3,2},{4,5},{5,4},{6,7},{7,6},{8,9},{9,8},{10,11... | collective-permute-start | bytes 786440 | tf_op jit(solution)/shard_map/experts/ppermute | solution.py:24
  83.4 3.5 %collective-permute-start.4 = (bf16[512,256]{1,0:T(8,128)(2,1)S(1)}, bf16[512,256]{1,0:T(8,128)(2,1)S(1)}, u32[]{:S(2)}, u32[]{:S(2)}) collective-permute-start(bf16[512,256]{1,0:T(8,128)(2,1)S(1)} %collective-permute-done.2), channel_id=1, source_target_pairs={{0,1},{1,0},{2,3},{3,2},{4,5},{5,4},{6,7},{7,6},{8,9},{9,8},{10,11... | collective-permute-start | bytes 786440 | tf_op jit(solution)/shard_map/experts/ppermute | solution.py:24
  87.3 9.1 %collective-permute-start.7 = (bf16[192,512]{1,0:T(8,128)(2,1)S(1)}, bf16[192,512]{1,0:T(8,128)(2,1)S(1)}, u32[]{:S(2)}, u32[]{:S(2)}) collective-permute-start(bf16[192,512]{1,0:T(8,128)(2,1)S(1)} %fusion.21), channel_id=1, source_target_pairs={{0,4},{2,6},{4,0},{6,2},{1,5},{3,7},{5,1},{7,3},{8,12},{10,14},{12... | collective-permute-start | bytes 589832 | tf_op jit(solution)/shard_map/experts/ppermute | solution.py:20
  89.2 22.8 %collective-permute-start.12 = (bf16[192,512]{1,0:T(8,128)(2,1)S(1)}, bf16[192,512]{1,0:T(8,128)(2,1)S(1)}, u32[]{:S(2)}, u32[]{:S(2)}) collective-permute-start(bf16[192,512]{1,0:T(8,128)(2,1)S(1)} %fusion.21), channel_id=1, source_target_pairs={{0,6},{2,0},{4,2},{6,4},{1,7},{3,1},{5,3},{7,5},{8,14},{10,8},{12,... | collective-permute-start | bytes 589832 | tf_op jit(solution)/shard_map/experts/ppermute | solution.py:20
  92.3 22.8 %collective-permute-start.14 = (bf16[192,512]{1,0:T(8,128)(2,1)S(1)}, bf16[192,512]{1,0:T(8,128)(2,1)S(1)}, u32[]{:S(2)}, u32[]{:S(2)}) collective-permute-start(bf16[192,512]{1,0:T(8,128)(2,1)S(1)} %fusion.21), channel_id=1, source_target_pairs={{0,1},{1,0},{2,3},{3,2},{4,5},{5,4},{6,7},{7,6},{8,9},{9,8},{10,11... | collective-permute-start | bytes 589832 | tf_op jit(solution)/shard_map/experts/ppermute | solution.py:24
  96.4 19.3 %copy-start.7 = (bf16[192,512]{1,0:T(8,128)(2,1)}, bf16[192,512]{1,0:T(8,128)(2,1)S(1)}, u32[]{:S(2)}) copy-start(bf16[192,512]{1,0:T(8,128)(2,1)S(1)} %collective-permute-done.7) | copy-start | bytes 589828
  96.4 12.1 %collective-permute-start.10 = (bf16[192,512]{1,0:T(8,128)(2,1)S(1)}, bf16[192,512]{1,0:T(8,128)(2,1)S(1)}, u32[]{:S(2)}, u32[]{:S(2)}) collective-permute-start(bf16[192,512]{1,0:T(8,128)(2,1)S(1)} %fusion.21), channel_id=1, source_target_pairs={{0,2},{2,4},{4,6},{6,0},{1,3},{3,5},{5,7},{7,1},{8,10},{10,12},{12... | collective-permute-start | bytes 589832 | tf_op jit(solution)/shard_map/experts/ppermute | solution.py:20
  99.5 16.5 %collective-permute-start.17 = (bf16[192,512]{1,0:T(8,128)(2,1)S(1)}, bf16[192,512]{1,0:T(8,128)(2,1)S(1)}, u32[]{:S(2)}, u32[]{:S(2)}) collective-permute-start(bf16[192,512]{1,0:T(8,128)(2,1)S(1)} %collective-permute-done.7), channel_id=1, source_target_pairs={{0,1},{1,0},{2,3},{3,2},{4,5},{5,4},{6,7},{7,6},{8,9},{9,8},{10,11... | collective-permute-start | bytes 589832 | tf_op jit(solution)/shard_map/experts/ppermute | solution.py:24
  108.5 7.2 %collective-permute-start.16 = (bf16[192,512]{1,0:T(8,128)(2,1)S(1)}, bf16[192,512]{1,0:T(8,128)(2,1)S(1)}, u32[]{:S(2)}, u32[]{:S(2)}) collective-permute-start(bf16[192,512]{1,0:T(8,128)(2,1)S(1)} %collective-permute-done.10), channel_id=1, source_target_pairs={{0,1},{1,0},{2,3},{3,2},{4,5},{5,4},{6,7},{7,6},{8,9},{9,8},{10,11... | collective-permute-start | bytes 589832 | tf_op jit(solution)/shard_map/experts/ppermute | solution.py:24
  112.0 5.2 %collective-permute-start.15 = (bf16[192,512]{1,0:T(8,128)(2,1)S(1)}, bf16[192,512]{1,0:T(8,128)(2,1)S(1)}, u32[]{:S(2)}, u32[]{:S(2)}) collective-permute-start(bf16[192,512]{1,0:T(8,128)(2,1)S(1)} %collective-permute-done.12), channel_id=1, source_target_pairs={{0,1},{1,0},{2,3},{3,2},{4,5},{5,4},{6,7},{7,6},{8,9},{9,8},{10,11... | collective-permute-start | bytes 589832 | tf_op jit(solution)/shard_map/experts/ppermute | solution.py:24
  115.7 3.4 %copy-start.6 = (bf16[192,512]{1,0:T(8,128)(2,1)}, bf16[192,512]{1,0:T(8,128)(2,1)S(1)}, u32[]{:S(2)}) copy-start(bf16[192,512]{1,0:T(8,128)(2,1)S(1)} %collective-permute-done.16) | copy-start | bytes 589828
  116.0 10.7 %copy-start.12 = (bf16[256,8]{0,1:T(8,128)(2,1)S(1)}, bf16[256,8]{0,1:T(8,128)(2,1)}, u32[]{:S(2)}) copy-start(bf16[256,8]{0,1:T(8,128)(2,1)} %param.8) | copy-start | bytes 12292
  116.0 10.8 %copy-start.11 = (s32[256,8]{0,1:T(8,128)S(1)}, s32[256,8]{0,1:T(8,128)}, u32[]{:S(2)}) copy-start(s32[256,8]{0,1:T(8,128)} %param.7) | copy-start | bytes 24580
  116.1 3.1 %copy-start.5 = (bf16[192,512]{1,0:T(8,128)(2,1)}, bf16[192,512]{1,0:T(8,128)(2,1)S(1)}, u32[]{:S(2)}) copy-start(bf16[192,512]{1,0:T(8,128)(2,1)S(1)} %collective-permute-done.17) | copy-start | bytes 589828
  119.2 21.3 %all-to-all-start.1 = ((bf16[16,32,256]{2,1,0:T(8,128)(2,1)}), bf16[16,32,256]{2,1,0:T(8,128)(2,1)S(1)}, u32[]{:S(2)}, u32[]{:S(2)}) async-start(bf16[16,32,256]{2,1,0:T(8,128)(2,1)} %bitcast.18), calls=%async_computation.1 | async-start | bytes 524288 | tf_op jit(solution)/shard_map/combine/all_to_all | solution.py:92
  140.8 9.6 %collective-permute-start.18 = (bf16[256,256]{1,0:T(8,128)(2,1)S(1)}, bf16[256,256]{1,0:T(8,128)(2,1)S(1)}, u32[]{:S(2)}, u32[]{:S(2)}) collective-permute-start(bf16[256,256]{1,0:T(8,128)(2,1)S(1)} %fusion.10), channel_id=1, source_target_pairs={{0,16},{8,24},{16,0},{24,8},{32,48},{40,56},{48,32},{56,40},{1,17}... | collective-permute-start | bytes 393224 | tf_op jit(solution)/shard_map/combine/ppermute | solution.py:28
  143.9 7.2 %collective-permute-start.19 = (bf16[256,256]{1,0:T(8,128)(2,1)S(1)}, bf16[256,256]{1,0:T(8,128)(2,1)S(1)}, u32[]{:S(2)}, u32[]{:S(2)}) collective-permute-start(bf16[256,256]{1,0:T(8,128)(2,1)S(1)} %fusion.10), channel_id=1, source_target_pairs={{0,32},{8,40},{16,48},{24,56},{32,0},{40,8},{48,16},{56,24},{1,33}... | collective-permute-start | bytes 393224 | tf_op jit(solution)/shard_map/combine/ppermute | solution.py:28
  148.3 6.9 %collective-permute-start.20 = (bf16[256,256]{1,0:T(8,128)(2,1)S(1)}, bf16[256,256]{1,0:T(8,128)(2,1)S(1)}, u32[]{:S(2)}, u32[]{:S(2)}) collective-permute-start(bf16[256,256]{1,0:T(8,128)(2,1)S(1)} %fusion.10), channel_id=1, source_target_pairs={{0,48},{8,56},{16,32},{24,40},{32,16},{40,24},{48,0},{56,8},{1,49}... | collective-permute-start | bytes 393224 | tf_op jit(solution)/shard_map/combine/ppermute | solution.py:28
  155.3 14.4 %collective-permute-start.21 = (bf16[256,256]{1,0:T(8,128)(2,1)S(1)}, bf16[256,256]{1,0:T(8,128)(2,1)S(1)}, u32[]{:S(2)}, u32[]{:S(2)}) collective-permute-start(bf16[256,256]{1,0:T(8,128)(2,1)S(1)} %add_convert_fusion.1), channel_id=1, source_target_pairs={{0,8},{8,0},{16,24},{24,16},{32,40},{40,32},{48,56},{56,48},{1,9},... | collective-permute-start | bytes 393224 | tf_op jit(solution)/shard_map/combine/ppermute | solution.py:28
  171.4 1.0 copy-start.9
  172.4 34.5 %all-to-all-start.2 = ((bf16[16,32,256]{2,1,0:T(8,128)(2,1)}), bf16[16,32,256]{2,1,0:T(8,128)(2,1)S(1)}, u32[]{:S(2)}, u32[]{:S(2)}) async-start(bf16[16,32,256]{2,1,0:T(8,128)(2,1)} %bitcast.20), calls=%async_computation.2 | async-start | bytes 524288 | tf_op jit(solution)/shard_map/curvature/all_to_all | solution.py:92
  182.8 16.3 %collective-permute-start.22 = (bf16[256,256]{1,0:T(8,128)(2,1)}, bf16[256,256]{1,0:T(8,128)(2,1)S(1)}, u32[]{:S(2)}, u32[]{:S(2)}) collective-permute-start(bf16[256,256]{1,0:T(8,128)(2,1)} %copy-done.9), channel_id=1, source_target_pairs={{0,4},{2,6},{4,0},{6,2},{1,5},{3,7},{5,1},{7,3},{8,12},{10,14},{12... | collective-permute-start | bytes 393224 | tf_op jit(solution)/shard_map/tangent/ppermute | solution.py:20
  184.8 16.3 %collective-permute-start.23 = (bf16[256,256]{1,0:T(8,128)(2,1)}, bf16[256,256]{1,0:T(8,128)(2,1)S(1)}, u32[]{:S(2)}, u32[]{:S(2)}) collective-permute-start(bf16[256,256]{1,0:T(8,128)(2,1)} %copy-done.9), channel_id=1, source_target_pairs={{0,2},{2,4},{4,6},{6,0},{1,3},{3,5},{5,7},{7,1},{8,10},{10,12},{12... | collective-permute-start | bytes 393224 | tf_op jit(solution)/shard_map/tangent/ppermute | solution.py:20
  188.4 15.1 %collective-permute-start.24 = (bf16[256,256]{1,0:T(8,128)(2,1)}, bf16[256,256]{1,0:T(8,128)(2,1)S(1)}, u32[]{:S(2)}, u32[]{:S(2)}) collective-permute-start(bf16[256,256]{1,0:T(8,128)(2,1)} %copy-done.9), channel_id=1, source_target_pairs={{0,6},{2,0},{4,2},{6,4},{1,7},{3,1},{5,3},{7,5},{8,14},{10,8},{12,... | collective-permute-start | bytes 393224 | tf_op jit(solution)/shard_map/tangent/ppermute | solution.py:20
  191.9 13.7 %collective-permute-start.25 = (bf16[256,256]{1,0:T(8,128)(2,1)}, bf16[256,256]{1,0:T(8,128)(2,1)S(1)}, u32[]{:S(2)}, u32[]{:S(2)}) collective-permute-start(bf16[256,256]{1,0:T(8,128)(2,1)} %copy-done.9), channel_id=1, source_target_pairs={{0,1},{1,0},{2,3},{3,2},{4,5},{5,4},{6,7},{7,6},{8,9},{9,8},{10,11... | collective-permute-start | bytes 393224 | tf_op jit(solution)/shard_map/tangent/ppermute | solution.py:24
  199.2 7.7 %collective-permute-start.28 = (bf16[256,256]{1,0:T(8,128)(2,1)S(1)}, bf16[256,256]{1,0:T(8,128)(2,1)S(1)}, u32[]{:S(2)}, u32[]{:S(2)}) collective-permute-start(bf16[256,256]{1,0:T(8,128)(2,1)S(1)} %collective-permute-done.22), channel_id=1, source_target_pairs={{0,1},{1,0},{2,3},{3,2},{4,5},{5,4},{6,7},{7,6},{8,9},{9,8},{10,11... | collective-permute-start | bytes 393224 | tf_op jit(solution)/shard_map/tangent/ppermute | solution.py:24
  201.1 5.7 %collective-permute-start.27 = (bf16[256,256]{1,0:T(8,128)(2,1)S(1)}, bf16[256,256]{1,0:T(8,128)(2,1)S(1)}, u32[]{:S(2)}, u32[]{:S(2)}) collective-permute-start(bf16[256,256]{1,0:T(8,128)(2,1)S(1)} %collective-permute-done.23), channel_id=1, source_target_pairs={{0,1},{1,0},{2,3},{3,2},{4,5},{5,4},{6,7},{7,6},{8,9},{9,8},{10,11... | collective-permute-start | bytes 393224 | tf_op jit(solution)/shard_map/tangent/ppermute | solution.py:24
  203.6 3.2 %collective-permute-start.26 = (bf16[256,256]{1,0:T(8,128)(2,1)S(1)}, bf16[256,256]{1,0:T(8,128)(2,1)S(1)}, u32[]{:S(2)}, u32[]{:S(2)}) collective-permute-start(bf16[256,256]{1,0:T(8,128)(2,1)S(1)} %collective-permute-done.24), channel_id=1, source_target_pairs={{0,1},{1,0},{2,3},{3,2},{4,5},{5,4},{6,7},{7,6},{8,9},{9,8},{10,11... | collective-permute-start | bytes 393224 | tf_op jit(solution)/shard_map/tangent/ppermute | solution.py:24
  206.9 5.4 %copy-start.1 = (bf16[256,2048]{1,0:T(8,128)(2,1)}, bf16[256,2048]{1,0:T(8,128)(2,1)S(1)}, u32[]{:S(2)}) copy-start(bf16[256,2048]{1,0:T(8,128)(2,1)S(1)} %constant_dynamic-update-slice_fusion) | copy-start | bytes 3145732
  208.5 4.0 %copy-start.8 = (bf16[192,512]{1,0:T(8,128)(2,1)S(1)}, bf16[192,512]{1,0:T(8,128)(2,1)}, u32[]{:S(2)}) copy-start(bf16[192,512]{1,0:T(8,128)(2,1)} %copy-done.7) | copy-start | bytes 589828
  210.0 3.6 %collective-permute-start.29 = (bf16[4,192,256]{2,1,0:T(8,128)(2,1)S(1)}, bf16[4,192,256]{2,1,0:T(8,128)(2,1)S(1)}, u32[]{:S(2)}, u32[]{:S(2)}) collective-permute-start(bf16[4,192,256]{2,1,0:T(8,128)(2,1)S(1)} %pad_maximum_fusion.1), channel_id=1, source_target_pairs={{0,1},{1,0},{2,3},{3,2},{4,5},{5,4},{6,7},{7,6},{8,9},{9,8},{10,11... | collective-permute-start | bytes 1179656 | tf_op jit(solution)/shard_map/curvature/ppermute | solution.py:24
  213.7 14.1 %collective-permute-start.30 = (bf16[2,192,256]{2,1,0:T(8,128)(2,1)S(1)}, bf16[2,192,256]{2,1,0:T(8,128)(2,1)S(1)}, u32[]{:S(2)}, u32[]{:S(2)}) collective-permute-start(bf16[2,192,256]{2,1,0:T(8,128)(2,1)S(1)} %pad_maximum_fusion.5), channel_id=1, source_target_pairs={{0,4},{2,6},{4,0},{6,2},{1,5},{3,7},{5,1},{7,3},{8,12},{10,14},{12... | collective-permute-start | bytes 589832 | tf_op jit(solution)/shard_map/curvature/ppermute | solution.py:20
  216.4 16.3 %collective-permute-start.32 = (bf16[2,192,256]{2,1,0:T(8,128)(2,1)S(1)}, bf16[2,192,256]{2,1,0:T(8,128)(2,1)S(1)}, u32[]{:S(2)}, u32[]{:S(2)}) collective-permute-start(bf16[2,192,256]{2,1,0:T(8,128)(2,1)S(1)} %pad_maximum_fusion.7), channel_id=1, source_target_pairs={{0,6},{2,0},{4,2},{6,4},{1,7},{3,1},{5,3},{7,5},{8,14},{10,8},{12,... | collective-permute-start | bytes 589832 | tf_op jit(solution)/shard_map/curvature/ppermute | solution.py:20
  219.6 11.4 %collective-permute-start.31 = (bf16[2,192,256]{2,1,0:T(8,128)(2,1)S(1)}, bf16[2,192,256]{2,1,0:T(8,128)(2,1)S(1)}, u32[]{:S(2)}, u32[]{:S(2)}) collective-permute-start(bf16[2,192,256]{2,1,0:T(8,128)(2,1)S(1)} %pad_maximum_fusion.6), channel_id=1, source_target_pairs={{0,2},{2,4},{4,6},{6,0},{1,3},{3,5},{5,7},{7,1},{8,10},{10,12},{12... | collective-permute-start | bytes 589832 | tf_op jit(solution)/shard_map/curvature/ppermute | solution.py:20
  233.0 0.9 copy-start.4
  (1 other events, 0.7 us)

commit v3 on v2

--- a/solution.py
+++ b/solution.py
@@ -37,15 +37,11 @@
     return blocks
 
 
-def exchange_blocks(piece):
-    steps = (*STEPS, 0)
-    swapped = swap_cores(jnp.stack([piece(step, 1) for step in steps]))
-    pairs = {step: jnp.stack([piece(step, 0), swapped[i]]) for i, step in enumerate(steps)}
-    blocks = {}
+def pair_shift(pairs):
+    blocks = {(0, 0): pairs[0][0], (0, 1): pairs[0][1]}
     for step in STEPS:
-        arrived = shift_line(pairs[step], step)
+        arrived = shift_line(jnp.stack(pairs[step]), step)
         blocks[(LINE - step, 0)], blocks[(LINE - step, 1)] = arrived[0], arrived[1]
-    blocks[(0, 0)], blocks[(0, 1)] = pairs[0][0], pairs[0][1]
     return blocks
 
 
@@ -94,12 +90,19 @@
         )
         return moved.reshape(rows, cols)
 
+    with jax.named_scope("direction"):
+        swapped = swap_cores(jnp.stack([columns(direction, step, 1) for step in range(LINE)]))
+
     with jax.named_scope("dispatch"):
         outgoing = jnp.dot(select, columns(tokens, 0, 0), preferred_element_type=jnp.float32)
-        arrived = over_planes(outgoing.astype(jnp.bfloat16))
+        outgoing, swapped = lax.optimization_barrier((outgoing.astype(jnp.bfloat16), swapped))
+        arrived = over_planes(outgoing)
 
     with jax.named_scope("direction"):
-        direction_blocks = exchange_blocks(lambda step, other: columns(direction, step, other))
+        direction_blocks = pair_shift(
+            [(columns(direction, step, 0), swapped[step]) for step in range(LINE)]
+        )
+        arrived, direction_blocks = lax.optimization_barrier((arrived, direction_blocks))
 
     with jax.named_scope("experts"):
         both = jnp.concatenate([gate_weight, up_weight], axis=0)
@@ -119,12 +122,20 @@
         for key, block in hidden_blocks.items():
             expert_out += contract_rows(block, direction_blocks[key])
         returned = over_planes(expert_out.astype(jnp.bfloat16))
-        part = lax.optimization_barrier(contract_rows(spread, returned).astype(jnp.bfloat16))
-        near = [swap_local(part, mask).astype(jnp.float32) for mask in (4, 2, 6)]
-        half = (part.astype(jnp.float32) + near[1]) + (near[0] + near[2])
-        half = lax.optimization_barrier(half.astype(jnp.bfloat16))
-        total = half.astype(jnp.float32) + swap_local(half, 1).astype(jnp.float32)
-        tangent_cols = total.astype(jnp.bfloat16)
+        part = contract_rows(spread, returned).astype(jnp.bfloat16)
+        first, second = lax.optimization_barrier((part[: col_tok // 2], part[col_tok // 2 :]))
+
+        def add_half(value):
+            return value.astype(jnp.float32) + swap_local(value, 1).astype(jnp.float32)
+
+        def add_x(value):
+            near, far, last = (swap_local(value, mask).astype(jnp.float32) for mask in (2, 4, 6))
+            return (value.astype(jnp.float32) + near) + (far + last)
+
+        second, first = lax.optimization_barrier(
+            (add_half(second).astype(jnp.bfloat16), add_x(first).astype(jnp.bfloat16))
+        )
+        tangent_cols = jnp.concatenate([add_half(first), add_x(second)]).astype(jnp.bfloat16)
 
     with jax.named_scope("curvature"):
         picked = jnp.dot(select, tangent_cols, preferred_element_type=jnp.float32)
@@ -134,13 +145,19 @@
         tangent_out = assemble(gather_blocks(tangent_cols), col_tok)
 
     with jax.named_scope("curvature"):
-        def product(step, other):
-            value = jnp.dot(
-                hidden_blocks[(step, other)], scaled, preferred_element_type=jnp.float32
-            )
+        def product(block):
+            value = jnp.dot(block, scaled, preferred_element_type=jnp.float32)
             return value.astype(jnp.bfloat16)
 
-        curvature = assemble(exchange_blocks(product), unit_count)
+        other_units = jnp.concatenate([hidden_blocks[(step, 1)] for step in range(LINE)])
+        crossed = swap_cores(product(other_units)).reshape(LINE, unit_count, cols)
+        finished = {}
+        for step in STEPS:
+            finished[(LINE - step, 0)] = shift_line(product(hidden_blocks[(step, 0)]), step)
+        for step in STEPS:
+            finished[(LINE - step, 1)] = shift_line(crossed[step], step)
+        finished[(0, 0)], finished[(0, 1)] = product(hidden_blocks[(0, 0)]), crossed[0]
+        curvature = assemble(finished, unit_count)
     return tangent_out, curvature
 
 

time: 237 us -> 251 us (1.059)
  starting transfers between devices: 148 us -> 165 us
  local copies, waits for them, and re-layouts: 4.36 us -> 9.52 us
  matrix products: 15.8 us -> 11.1 us
  waiting for transfers between devices: 58.6 us -> 55.8 us
    ppermute x15 -> x18, starting transfers between devices: 41.9 us -> 57.3 us  [shift_line(): lax.ppermute(value, 'line', [(i, (i + step) % LINE) for i in range(LINE)])]
    all_to_all x3, starting transfers between devices: 37.4 us -> 27.9 us  [over_planes(): lax.all_to_all(slots.reshape(n_expert, slot_count, cols), 'expert', 0, 0,...]
    ppermute x4 -> x8, starting transfers between devices: 21.7 us -> 28.5 us  [swap_local(): return lax.ppermute(value, 'local', [(i, i ^ mask) for i in range(EXP_COL)])]
    ppermute x14, starting transfers between devices: 46.7 us -> 51.5 us  [swap_cores(): return lax.ppermute(value, 'core', [(i, i ^ 1) for i in range(CORES)])]
    dot_general x9, matrix products: 7.7 us -> 4.12 us  [contract_rows(): lax.dot_general(left, right, (((0,), (0,)), ((), ())), preferred_element_...]
    ppermute x15 -> x18, waiting for transfers between devices: 35.4 us -> 32.9 us  [shift_line(): lax.ppermute(value, 'line', [(i, (i + step) % LINE) for i in range(LINE)])]
    ppermute x4 -> x8, waiting for transfers between devices: 6.86 us -> 6.12 us  [swap_local(): return lax.ppermute(value, 'local', [(i, i ^ mask) for i in range(EXP_COL)])]
  transfers between devices with their start and end apart: 36 -> 43, of which waited for: 15 -> 12; matrix products, arithmetic and copies ran while one was open for 6% -> 5% of each run, Pallas kernels for 0% -> 0%
where the time goes in v3:
time: 251 us; the launch traced here: 247 us
  starting transfers between devices  165 us (66%)
  waiting for transfers between devices  55.8 us (22%)
  matrix products  11.1 us (4%)
  local copies, waits for them, and re-layouts  9.52 us (4%)
  other arithmetic  3.28 us (1%)
    ppermute x18, starting transfers between devices, shift_line(): lax.ppermute(value, 'line', [(i, (i + step) % LINE) for i in range(LINE)])  57.3 us
    ppermute x14, starting transfers between devices, swap_cores(): return lax.ppermute(value, 'core', [(i, i ^ 1) for i in range(CORES)])  51.5 us
    ppermute x18, waiting for transfers between devices, shift_line(): lax.ppermute(value, 'line', [(i, (i + step) % LINE) for i in range(LINE)])  32.9 us
    ppermute x8, starting transfers between devices, swap_local(): return lax.ppermute(value, 'local', [(i, i ^ mask) for i in range(EXP_COL)])  28.5 us
    all_to_all x3, starting transfers between devices, over_planes(): lax.all_to_all(slots.reshape(n_expert, slot_count, cols), 'expert', 0, 0,...  27.9 us
    all_to_all x3, waiting for transfers between devices, over_planes(): lax.all_to_all(slots.reshape(n_expert, slot_count, cols), 'expert', 0, 0,...  14.3 us
    ppermute x8, waiting for transfers between devices, swap_local(): return lax.ppermute(value, 'local', [(i, i ^ mask) for i in range(EXP_COL)])  6.12 us
  transfers between devices with their start and end apart: 43, of which 12 were waited for; matrix products, arithmetic and copies ran while one was open for 5% of the time, Pallas kernels for 0%

profile of v3, /device:TPU:1, one launch (start us, length us, event | category | flops | bytes accessed | tf_op | source)
XLA Modules:
  0.0 246.7 jit_solution(12534618295774336924)
XLA Ops:
  0.7 2.1 dynamic-slice_bitcast_fusion
  3.6 16.1 %collective-permute-start = (bf16[4,192,256]{2,1,0:T(8,128)(2,1)}, bf16[4,192,256]{2,1,0:T(8,128)(2,1)}, u32[]{:S(2)}, u32[]{:S(2)}) collective-permute-start(bf16[4,192,256]{2,1,0:T(8,128)(2,1)} %pad_maximum_fusion), channel_id=1, source_target_pairs={{0,1},{1,0},{2,3},{3,2},{4,5},{5,4},{6,7},{7,6},{8,9},{9,8},{10,11... | collective-permute-start | bytes 1179656 | tf_op jit(solution)/shard_map/direction/ppermute | solution.py:24
  24.2 5.9 %all-to-all-start = ((bf16[16,32,256]{2,1,0:T(8,128)(2,1)}), bf16[16,32,256]{2,1,0:T(8,128)(2,1)S(1)}, u32[]{:S(2)}, u32[]{:S(2)}) async-start(bf16[16,32,256]{2,1,0:T(8,128)(2,1)} %bitcast.6), calls=%async_computation | async-start | bytes 524288 | tf_op jit(solution)/shard_map/dispatch/all_to_all | solution.py:88
  31.1 3.2 %collective-permute-start.3 = (bf16[2,192,256]{2,1,0:T(8,128)(2,1)S(1)}, bf16[2,192,256]{2,1,0:T(8,128)(2,1)S(1)}, u32[]{:S(2)}, u32[]{:S(2)}) collective-permute-start(bf16[2,192,256]{2,1,0:T(8,128)(2,1)S(1)} %pad_maximum_fusion.3), channel_id=1, source_target_pairs={{0,2},{2,4},{4,6},{6,0},{1,3},{3,5},{5,7},{7,1},{8,10},{10,12},{12... | collective-permute-start | bytes 589832 | tf_op jit(solution)/shard_map/direction/ppermute | solution.py:20
  34.4 4.2 %collective-permute-start.2 = (bf16[2,192,256]{2,1,0:T(8,128)(2,1)S(1)}, bf16[2,192,256]{2,1,0:T(8,128)(2,1)S(1)}, u32[]{:S(2)}, u32[]{:S(2)}) collective-permute-start(bf16[2,192,256]{2,1,0:T(8,128)(2,1)S(1)} %pad_maximum_fusion.2), channel_id=1, source_target_pairs={{0,4},{2,6},{4,0},{6,2},{1,5},{3,7},{5,1},{7,3},{8,12},{10,14},{12... | collective-permute-start | bytes 589832 | tf_op jit(solution)/shard_map/direction/ppermute | solution.py:20
  38.6 3.0 %collective-permute-start.1 = (bf16[2,192,256]{2,1,0:T(8,128)(2,1)S(1)}, bf16[2,192,256]{2,1,0:T(8,128)(2,1)S(1)}, u32[]{:S(2)}, u32[]{:S(2)}) collective-permute-start(bf16[2,192,256]{2,1,0:T(8,128)(2,1)S(1)} %pad_maximum_fusion.1), channel_id=1, source_target_pairs={{0,6},{2,0},{4,2},{6,4},{1,7},{3,1},{5,3},{7,5},{8,14},{10,8},{12,... | collective-permute-start | bytes 589832 | tf_op jit(solution)/shard_map/direction/ppermute | solution.py:20
  42.3 7.9 %collective-permute-done.2 = bf16[2,192,256]{2,1,0:T(8,128)(2,1)S(1)} collective-permute-done((bf16[2,192,256]{2,1,0:T(8,128)(2,1)S(1)}, bf16[2,192,256]{2,1,0:T(8,128)(2,1)S(1)}, u32[]{:S(2)}, u32[]{:S(2)}) %collective-permute-start.2) | collective-permute-done | bytes 196640 | tf_op jit(solution)/shard_map/direction/ppermute | solution.py:20
  51.5 6.8 %collective-permute-start.6 = (bf16[512,256]{1,0:T(8,128)(2,1)S(1)}, bf16[512,256]{1,0:T(8,128)(2,1)S(1)}, u32[]{:S(2)}, u32[]{:S(2)}) collective-permute-start(bf16[512,256]{1,0:T(8,128)(2,1)S(1)} %bitcast.94), channel_id=1, source_target_pairs={{0,6},{2,0},{4,2},{6,4},{1,7},{3,1},{5,3},{7,5},{8,14},{10,8},{12,... | collective-permute-start | bytes 786440 | tf_op jit(solution)/shard_map/experts/ppermute | solution.py:20
  59.5 2.0 collective-permute-start.4
  61.5 3.2 %collective-permute-start.7 = (bf16[512,256]{1,0:T(8,128)(2,1)S(1)}, bf16[512,256]{1,0:T(8,128)(2,1)S(1)}, u32[]{:S(2)}, u32[]{:S(2)}) collective-permute-start(bf16[512,256]{1,0:T(8,128)(2,1)S(1)} %bitcast.96), channel_id=1, source_target_pairs={{0,1},{1,0},{2,3},{3,2},{4,5},{5,4},{6,7},{7,6},{8,9},{9,8},{10,11... | collective-permute-start | bytes 786440 | tf_op jit(solution)/shard_map/experts/ppermute | solution.py:24
  64.7 2.2 collective-permute-start.5
  67.5 2.2 collective-permute-start.8
  70.0 11.3 %collective-permute-done.4 = bf16[512,256]{1,0:T(8,128)(2,1)S(1)} collective-permute-done((bf16[512,256]{1,0:T(8,128)(2,1)S(1)}, bf16[512,256]{1,0:T(8,128)(2,1)S(1)}, u32[]{:S(2)}, u32[]{:S(2)}) %collective-permute-start.4) | collective-permute-done | bytes 262176 | tf_op jit(solution)/shard_map/experts/ppermute | solution.py:20
  81.3 3.1 %collective-permute-start.10 = (bf16[512,256]{1,0:T(8,128)(2,1)S(1)}, bf16[512,256]{1,0:T(8,128)(2,1)S(1)}, u32[]{:S(2)}, u32[]{:S(2)}) collective-permute-start(bf16[512,256]{1,0:T(8,128)(2,1)S(1)} %collective-permute-done.4), channel_id=1, source_target_pairs={{0,1},{1,0},{2,3},{3,2},{4,5},{5,4},{6,7},{7,6},{8,9},{9,8},{10,11... | collective-permute-start | bytes 786440 | tf_op jit(solution)/shard_map/experts/ppermute | solution.py:24
  84.7 1.9 collective-permute-start.9
  89.2 2.1 collective-permute-start.11
  91.3 2.1 collective-permute-start.13
  93.4 2.8 %collective-permute-start.14 = (bf16[192,512]{1,0:T(8,128)(2,1)S(1)}, bf16[192,512]{1,0:T(8,128)(2,1)}, u32[]{:S(2)}, u32[]{:S(2)}) collective-permute-start(bf16[192,512]{1,0:T(8,128)(2,1)S(1)} %fusion.21), channel_id=1, source_target_pairs={{0,1},{1,0},{2,3},{3,2},{4,5},{5,4},{6,7},{7,6},{8,9},{9,8},{10,11... | collective-permute-start | bytes 589832 | tf_op jit(solution)/shard_map/experts/ppermute | solution.py:24
  96.2 2.9 %collective-permute-start.12 = (bf16[192,512]{1,0:T(8,128)(2,1)S(1)}, bf16[192,512]{1,0:T(8,128)(2,1)S(1)}, u32[]{:S(2)}, u32[]{:S(2)}) collective-permute-start(bf16[192,512]{1,0:T(8,128)(2,1)S(1)} %fusion.21), channel_id=1, source_target_pairs={{0,2},{2,4},{4,6},{6,0},{1,3},{3,5},{5,7},{7,1},{8,10},{10,12},{12... | collective-permute-start | bytes 589832 | tf_op jit(solution)/shard_map/experts/ppermute | solution.py:20
  99.4 7.1 %collective-permute-done.12 = bf16[192,512]{1,0:T(8,128)(2,1)S(1)} collective-permute-done((bf16[192,512]{1,0:T(8,128)(2,1)S(1)}, bf16[192,512]{1,0:T(8,128)(2,1)S(1)}, u32[]{:S(2)}, u32[]{:S(2)}) %collective-permute-start.12) | collective-permute-done | bytes 196640 | tf_op jit(solution)/shard_map/experts/ppermute | solution.py:20
  106.5 2.8 %collective-permute-start.16 = (bf16[192,512]{1,0:T(8,128)(2,1)S(1)}, bf16[192,512]{1,0:T(8,128)(2,1)S(1)}, u32[]{:S(2)}, u32[]{:S(2)}) collective-permute-start(bf16[192,512]{1,0:T(8,128)(2,1)S(1)} %collective-permute-done.12), channel_id=1, source_target_pairs={{0,1},{1,0},{2,3},{3,2},{4,5},{5,4},{6,7},{7,6},{8,9},{9,8},{10,11... | collective-permute-start | bytes 589832 | tf_op jit(solution)/shard_map/experts/ppermute | solution.py:24
  109.3 1.9 collective-permute-start.17
  111.2 2.4 collective-permute-start.15
  117.7 11.6 %all-to-all-start.1 = ((bf16[16,32,256]{2,1,0:T(8,128)(2,1)}), bf16[16,32,256]{2,1,0:T(8,128)(2,1)S(1)}, u32[]{:S(2)}, u32[]{:S(2)}) async-start(bf16[16,32,256]{2,1,0:T(8,128)(2,1)} %bitcast.18), calls=%async_computation.1 | async-start | bytes 524288 | tf_op jit(solution)/shard_map/combine/all_to_all | solution.py:88
  129.5 14.3 %all-to-all-done.1 = bf16[16,32,256]{2,1,0:T(8,128)(2,1)S(1)} async-done(((bf16[16,32,256]{2,1,0:T(8,128)(2,1)}), bf16[16,32,256]{2,1,0:T(8,128)(2,1)S(1)}, u32[]{:S(2)}, u32[]{:S(2)}) %all-to-all-start.1) | async-done | bytes 262176 | tf_op jit(solution)/shard_map/combine/all_to_all | solution.py:88
  144.1 7.4 %collective-permute-start.18 = (bf16[128,256]{1,0:T(8,128)(2,1)S(1)}, bf16[128,256]{1,0:T(8,128)(2,1)S(1)}, u32[]{:S(2)}, u32[]{:S(2)}) collective-permute-start(bf16[128,256]{1,0:T(8,128)(2,1)S(1)} %get-tuple-element.28), channel_id=1, source_target_pairs={{0,8},{8,0},{16,24},{24,16},{32,40},{40,32},{48,56},{56,48},{1,9},... | collective-permute-start | bytes 196616 | tf_op jit(solution)/shard_map/combine/ppermute | solution.py:28
  151.5 3.1 %collective-permute-start.19 = (bf16[128,256]{1,0:T(8,128)(2,1)S(1)}, bf16[128,256]{1,0:T(8,128)(2,1)S(1)}, u32[]{:S(2)}, u32[]{:S(2)}) collective-permute-start(bf16[128,256]{1,0:T(8,128)(2,1)S(1)} %get-tuple-element.29), channel_id=1, source_target_pairs={{0,16},{8,24},{16,0},{24,8},{32,48},{40,56},{48,32},{56,40},{1,17}... | collective-permute-start | bytes 196616 | tf_op jit(solution)/shard_map/combine/ppermute | solution.py:28
  154.6 4.4 %collective-permute-start.20 = (bf16[128,256]{1,0:T(8,128)(2,1)S(1)}, bf16[128,256]{1,0:T(8,128)(2,1)S(1)}, u32[]{:S(2)}, u32[]{:S(2)}) collective-permute-start(bf16[128,256]{1,0:T(8,128)(2,1)S(1)} %get-tuple-element.29), channel_id=1, source_target_pairs={{0,32},{8,40},{16,48},{24,56},{32,0},{40,8},{48,16},{56,24},{1,33}... | collective-permute-start | bytes 196616 | tf_op jit(solution)/shard_map/combine/ppermute | solution.py:28
  159.0 2.1 collective-permute-start.21
  161.1 4.0 %collective-permute-done.21 = bf16[128,256]{1,0:T(8,128)(2,1)S(1)} collective-permute-done((bf16[128,256]{1,0:T(8,128)(2,1)S(1)}, bf16[128,256]{1,0:T(8,128)(2,1)S(1)}, u32[]{:S(2)}, u32[]{:S(2)}) %collective-permute-start.21) | collective-permute-done | bytes 65568 | tf_op jit(solution)/shard_map/combine/ppermute | solution.py:28
  169.3 3.6 %collective-permute-start.24 = (bf16[128,256]{1,0:T(8,128)(2,1)S(1)}, bf16[128,256]{1,0:T(8,128)(2,1)S(1)}, u32[]{:S(2)}, u32[]{:S(2)}) collective-permute-start(bf16[128,256]{1,0:T(8,128)(2,1)S(1)} %add_convert_fusion.3), channel_id=1, source_target_pairs={{0,32},{8,40},{16,48},{24,56},{32,0},{40,8},{48,16},{56,24},{1,33}... | collective-permute-start | bytes 196616 | tf_op jit(solution)/shard_map/combine/ppermute | solution.py:28
  172.9 4.1 %collective-permute-start.25 = (bf16[128,256]{1,0:T(8,128)(2,1)S(1)}, bf16[128,256]{1,0:T(8,128)(2,1)S(1)}, u32[]{:S(2)}, u32[]{:S(2)}) collective-permute-start(bf16[128,256]{1,0:T(8,128)(2,1)S(1)} %add_convert_fusion.3), channel_id=1, source_target_pairs={{0,48},{8,56},{16,32},{24,40},{32,16},{40,24},{48,0},{56,8},{1,49}... | collective-permute-start | bytes 196616 | tf_op jit(solution)/shard_map/combine/ppermute | solution.py:28
  177.1 2.1 collective-permute-done.25
  180.1 10.3 %all-to-all-start.2 = ((bf16[16,32,256]{2,1,0:T(8,128)(2,1)}), bf16[16,32,256]{2,1,0:T(8,128)(2,1)S(1)}, u32[]{:S(2)}, u32[]{:S(2)}) async-start(bf16[16,32,256]{2,1,0:T(8,128)(2,1)} %bitcast.20), calls=%async_computation.2 | async-start | bytes 524288 | tf_op jit(solution)/shard_map/curvature/all_to_all | solution.py:88
  190.6 3.7 %collective-permute-start.26 = (bf16[256,256]{1,0:T(8,128)(2,1)S(1)}, bf16[256,256]{1,0:T(8,128)(2,1)S(1)}, u32[]{:S(2)}, u32[]{:S(2)}) collective-permute-start(bf16[256,256]{1,0:T(8,128)(2,1)S(1)} %get-tuple-element.53), channel_id=1, source_target_pairs={{0,4},{2,6},{4,0},{6,2},{1,5},{3,7},{5,1},{7,3},{8,12},{10,14},{12... | collective-permute-start | bytes 393224 | tf_op jit(solution)/shard_map/tangent/ppermute | solution.py:20
  194.3 3.1 %collective-permute-start.27 = (bf16[256,256]{1,0:T(8,128)(2,1)S(1)}, bf16[256,256]{1,0:T(8,128)(2,1)S(1)}, u32[]{:S(2)}, u32[]{:S(2)}) collective-permute-start(bf16[256,256]{1,0:T(8,128)(2,1)S(1)} %get-tuple-element.53), channel_id=1, source_target_pairs={{0,2},{2,4},{4,6},{6,0},{1,3},{3,5},{5,7},{7,1},{8,10},{10,12},{12... | collective-permute-start | bytes 393224 | tf_op jit(solution)/shard_map/tangent/ppermute | solution.py:20
  197.4 4.0 %collective-permute-start.28 = (bf16[256,256]{1,0:T(8,128)(2,1)S(1)}, bf16[256,256]{1,0:T(8,128)(2,1)S(1)}, u32[]{:S(2)}, u32[]{:S(2)}) collective-permute-start(bf16[256,256]{1,0:T(8,128)(2,1)S(1)} %get-tuple-element.53), channel_id=1, source_target_pairs={{0,6},{2,0},{4,2},{6,4},{1,7},{3,1},{5,3},{7,5},{8,14},{10,8},{12,... | collective-permute-start | bytes 393224 | tf_op jit(solution)/shard_map/tangent/ppermute | solution.py:20
  201.4 6.8 %collective-permute-start.29 = (bf16[256,256]{1,0:T(8,128)(2,1)S(1)}, bf16[256,256]{1,0:T(8,128)(2,1)S(1)}, u32[]{:S(2)}, u32[]{:S(2)}) collective-permute-start(bf16[256,256]{1,0:T(8,128)(2,1)S(1)} %get-tuple-element.53), channel_id=1, source_target_pairs={{0,1},{1,0},{2,3},{3,2},{4,5},{5,4},{6,7},{7,6},{8,9},{9,8},{10,11... | collective-permute-start | bytes 393224 | tf_op jit(solution)/shard_map/tangent/ppermute | solution.py:24
  208.2 1.9 collective-permute-start.32
  210.2 2.4 collective-permute-start.31
  217.8 2.0 collective-permute-start.36
  222.3 2.5 collective-permute-start.33
  225.0 2.8 %collective-permute-start.34 = (bf16[192,256]{1,0:T(8,128)(2,1)S(1)}, bf16[192,256]{1,0:T(8,128)(2,1)S(1)}, u32[]{:S(2)}, u32[]{:S(2)}) collective-permute-start(bf16[192,256]{1,0:T(8,128)(2,1)S(1)} %convolution_convert_fusion.4), channel_id=1, source_target_pairs={{0,2},{2,4},{4,6},{6,0},{1,3},{3,5},{5,7},{7,1},{8,10},{10,12},{12... | collective-permute-start | bytes 294920 | tf_op jit(solution)/shard_map/curvature/ppermute | solution.py:20
  227.8 3.4 %collective-permute-done.33 = bf16[192,256]{1,0:T(8,128)(2,1)S(1)} collective-permute-done((bf16[192,256]{1,0:T(8,128)(2,1)S(1)}, bf16[192,256]{1,0:T(8,128)(2,1)S(1)}, u32[]{:S(2)}, u32[]{:S(2)}) %collective-permute-start.33) | collective-permute-done | bytes 98336 | tf_op jit(solution)/shard_map/curvature/ppermute | solution.py:20
  232.2 3.8 %collective-permute-start.37 = (bf16[192,256]{1,0:T(8,128)(2,1)S(1)}, bf16[192,256]{1,0:T(8,128)(2,1)S(1)}, u32[]{:S(2)}, u32[]{:S(2)}) collective-permute-start(bf16[192,256]{1,0:T(8,128)(2,1)S(1)} %get-tuple-element.42), channel_id=1, source_target_pairs={{0,4},{2,6},{4,0},{6,2},{1,5},{3,7},{5,1},{7,3},{8,12},{10,14},{12... | collective-permute-start | bytes 294920 | tf_op jit(solution)/shard_map/curvature/ppermute | solution.py:20
  236.0 2.6 %collective-permute-start.38 = (bf16[192,256]{1,0:T(8,128)(2,1)S(1)}, bf16[192,256]{1,0:T(8,128)(2,1)S(1)}, u32[]{:S(2)}, u32[]{:S(2)}) collective-permute-start(bf16[192,256]{1,0:T(8,128)(2,1)S(1)} %get-tuple-element.41), channel_id=1, source_target_pairs={{0,2},{2,4},{4,6},{6,0},{1,3},{3,5},{5,7},{7,1},{8,10},{10,12},{12... | collective-permute-start | bytes 294920 | tf_op jit(solution)/shard_map/curvature/ppermute | solution.py:20
  238.7 4.5 %collective-permute-start.39 = (bf16[192,256]{1,0:T(8,128)(2,1)S(1)}, bf16[192,256]{1,0:T(8,128)(2,1)S(1)}, u32[]{:S(2)}, u32[]{:S(2)}) collective-permute-start(bf16[192,256]{1,0:T(8,128)(2,1)S(1)} %get-tuple-element.40), channel_id=1, source_target_pairs={{0,6},{2,0},{4,2},{6,4},{1,7},{3,1},{5,3},{7,5},{8,14},{10,8},{12,... | collective-permute-start | bytes 294920 | tf_op jit(solution)/shard_map/curvature/ppermute | solution.py:20
  243.2 2.3 collective-permute-done.39
  (158 shorter events, 32.9 us)
Async XLA Ops:
  3.6 18.8 %collective-permute-start = (bf16[4,192,256]{2,1,0:T(8,128)(2,1)}, bf16[4,192,256]{2,1,0:T(8,128)(2,1)}, u32[]{:S(2)}, u32[]{:S(2)}) collective-permute-start(bf16[4,192,256]{2,1,0:T(8,128)(2,1)} %pad_maximum_fusion), channel_id=1, source_target_pairs={{0,1},{1,0},{2,3},{3,2},{4,5},{5,4},{6,7},{7,6},{8,9},{9,8},{10,11... | collective-permute-start | bytes 1179656 | tf_op jit(solution)/shard_map/direction/ppermute | solution.py:24
  24.2 27.2 %all-to-all-start = ((bf16[16,32,256]{2,1,0:T(8,128)(2,1)}), bf16[16,32,256]{2,1,0:T(8,128)(2,1)S(1)}, u32[]{:S(2)}, u32[]{:S(2)}) async-start(bf16[16,32,256]{2,1,0:T(8,128)(2,1)} %bitcast.6), calls=%async_computation | async-start | bytes 524288 | tf_op jit(solution)/shard_map/dispatch/all_to_all | solution.py:88
  31.1 10.5 %collective-permute-start.3 = (bf16[2,192,256]{2,1,0:T(8,128)(2,1)S(1)}, bf16[2,192,256]{2,1,0:T(8,128)(2,1)S(1)}, u32[]{:S(2)}, u32[]{:S(2)}) collective-permute-start(bf16[2,192,256]{2,1,0:T(8,128)(2,1)S(1)} %pad_maximum_fusion.3), channel_id=1, source_target_pairs={{0,2},{2,4},{4,6},{6,0},{1,3},{3,5},{5,7},{7,1},{8,10},{10,12},{12... | collective-permute-start | bytes 589832 | tf_op jit(solution)/shard_map/direction/ppermute | solution.py:20
  34.4 15.8 %collective-permute-start.2 = (bf16[2,192,256]{2,1,0:T(8,128)(2,1)S(1)}, bf16[2,192,256]{2,1,0:T(8,128)(2,1)S(1)}, u32[]{:S(2)}, u32[]{:S(2)}) collective-permute-start(bf16[2,192,256]{2,1,0:T(8,128)(2,1)S(1)} %pad_maximum_fusion.2), channel_id=1, source_target_pairs={{0,4},{2,6},{4,0},{6,2},{1,5},{3,7},{5,1},{7,3},{8,12},{10,14},{12... | collective-permute-start | bytes 589832 | tf_op jit(solution)/shard_map/direction/ppermute | solution.py:20
  38.6 12.2 %collective-permute-start.1 = (bf16[2,192,256]{2,1,0:T(8,128)(2,1)S(1)}, bf16[2,192,256]{2,1,0:T(8,128)(2,1)S(1)}, u32[]{:S(2)}, u32[]{:S(2)}) collective-permute-start(bf16[2,192,256]{2,1,0:T(8,128)(2,1)S(1)} %pad_maximum_fusion.1), channel_id=1, source_target_pairs={{0,6},{2,0},{4,2},{6,4},{1,7},{3,1},{5,3},{7,5},{8,14},{10,8},{12,... | collective-permute-start | bytes 589832 | tf_op jit(solution)/shard_map/direction/ppermute | solution.py:20
  51.5 15.7 %collective-permute-start.6 = (bf16[512,256]{1,0:T(8,128)(2,1)S(1)}, bf16[512,256]{1,0:T(8,128)(2,1)S(1)}, u32[]{:S(2)}, u32[]{:S(2)}) collective-permute-start(bf16[512,256]{1,0:T(8,128)(2,1)S(1)} %bitcast.94), channel_id=1, source_target_pairs={{0,6},{2,0},{4,2},{6,4},{1,7},{3,1},{5,3},{7,5},{8,14},{10,8},{12,... | collective-permute-start | bytes 786440 | tf_op jit(solution)/shard_map/experts/ppermute | solution.py:20
  59.5 21.8 %collective-permute-start.4 = (bf16[512,256]{1,0:T(8,128)(2,1)S(1)}, bf16[512,256]{1,0:T(8,128)(2,1)S(1)}, u32[]{:S(2)}, u32[]{:S(2)}) collective-permute-start(bf16[512,256]{1,0:T(8,128)(2,1)S(1)} %bitcast.95), channel_id=1, source_target_pairs={{0,4},{2,6},{4,0},{6,2},{1,5},{3,7},{5,1},{7,3},{8,12},{10,14},{12... | collective-permute-start | bytes 786440 | tf_op jit(solution)/shard_map/experts/ppermute | solution.py:20
  61.5 8.2 %collective-permute-start.7 = (bf16[512,256]{1,0:T(8,128)(2,1)S(1)}, bf16[512,256]{1,0:T(8,128)(2,1)S(1)}, u32[]{:S(2)}, u32[]{:S(2)}) collective-permute-start(bf16[512,256]{1,0:T(8,128)(2,1)S(1)} %bitcast.96), channel_id=1, source_target_pairs={{0,1},{1,0},{2,3},{3,2},{4,5},{5,4},{6,7},{7,6},{8,9},{9,8},{10,11... | collective-permute-start | bytes 786440 | tf_op jit(solution)/shard_map/experts/ppermute | solution.py:24
  64.7 20.0 %collective-permute-start.5 = (bf16[512,256]{1,0:T(8,128)(2,1)S(1)}, bf16[512,256]{1,0:T(8,128)(2,1)S(1)}, u32[]{:S(2)}, u32[]{:S(2)}) collective-permute-start(bf16[512,256]{1,0:T(8,128)(2,1)S(1)} %bitcast.97), channel_id=1, source_target_pairs={{0,2},{2,4},{4,6},{6,0},{1,3},{3,5},{5,7},{7,1},{8,10},{10,12},{12... | collective-permute-start | bytes 786440 | tf_op jit(solution)/shard_map/experts/ppermute | solution.py:20
  67.5 21.2 %collective-permute-start.8 = (bf16[512,256]{1,0:T(8,128)(2,1)S(1)}, bf16[512,256]{1,0:T(8,128)(2,1)S(1)}, u32[]{:S(2)}, u32[]{:S(2)}) collective-permute-start(bf16[512,256]{1,0:T(8,128)(2,1)S(1)} %collective-permute-done.6), channel_id=1, source_target_pairs={{0,1},{1,0},{2,3},{3,2},{4,5},{5,4},{6,7},{7,6},{8,9},{9,8},{10,11... | collective-permute-start | bytes 786440 | tf_op jit(solution)/shard_map/experts/ppermute | solution.py:24
  81.3 7.1 %collective-permute-start.10 = (bf16[512,256]{1,0:T(8,128)(2,1)S(1)}, bf16[512,256]{1,0:T(8,128)(2,1)S(1)}, u32[]{:S(2)}, u32[]{:S(2)}) collective-permute-start(bf16[512,256]{1,0:T(8,128)(2,1)S(1)} %collective-permute-done.4), channel_id=1, source_target_pairs={{0,1},{1,0},{2,3},{3,2},{4,5},{5,4},{6,7},{7,6},{8,9},{9,8},{10,11... | collective-permute-start | bytes 786440 | tf_op jit(solution)/shard_map/experts/ppermute | solution.py:24
  84.7 3.4 %collective-permute-start.9 = (bf16[512,256]{1,0:T(8,128)(2,1)S(1)}, bf16[512,256]{1,0:T(8,128)(2,1)S(1)}, u32[]{:S(2)}, u32[]{:S(2)}) collective-permute-start(bf16[512,256]{1,0:T(8,128)(2,1)S(1)} %collective-permute-done.5), channel_id=1, source_target_pairs={{0,1},{1,0},{2,3},{3,2},{4,5},{5,4},{6,7},{7,6},{8,9},{9,8},{10,11... | collective-permute-start | bytes 786440 | tf_op jit(solution)/shard_map/experts/ppermute | solution.py:24
  89.1 24.9 %copy-start.8 = (bf16[192,256]{1,0:T(8,128)(2,1)S(1)}, bf16[192,256]{1,0:T(8,128)(2,1)}, u32[]{:S(2)}) copy-start(bf16[192,256]{1,0:T(8,128)(2,1)} %get-tuple-element.23) | copy-start | bytes 294916
  89.2 25.0 %copy-start.5 = (bf16[192,256]{1,0:T(8,128)(2,1)S(1)}, bf16[192,256]{1,0:T(8,128)(2,1)}, u32[]{:S(2)}) copy-start(bf16[192,256]{1,0:T(8,128)(2,1)} %get-tuple-element.24) | copy-start | bytes 294916
  89.2 20.1 %collective-permute-start.11 = (bf16[192,512]{1,0:T(8,128)(2,1)S(1)}, bf16[192,512]{1,0:T(8,128)(2,1)S(1)}, u32[]{:S(2)}, u32[]{:S(2)}) collective-permute-start(bf16[192,512]{1,0:T(8,128)(2,1)S(1)} %fusion.21), channel_id=1, source_target_pairs={{0,4},{2,6},{4,0},{6,2},{1,5},{3,7},{5,1},{7,3},{8,12},{10,14},{12... | collective-permute-start | bytes 589832 | tf_op jit(solution)/shard_map/experts/ppermute | solution.py:20
  91.3 20.0 %collective-permute-start.13 = (bf16[192,512]{1,0:T(8,128)(2,1)S(1)}, bf16[192,512]{1,0:T(8,128)(2,1)S(1)}, u32[]{:S(2)}, u32[]{:S(2)}) collective-permute-start(bf16[192,512]{1,0:T(8,128)(2,1)S(1)} %fusion.21), channel_id=1, source_target_pairs={{0,6},{2,0},{4,2},{6,4},{1,7},{3,1},{5,3},{7,5},{8,14},{10,8},{12,... | collective-permute-start | bytes 589832 | tf_op jit(solution)/shard_map/experts/ppermute | solution.py:20
  93.4 20.9 %collective-permute-start.14 = (bf16[192,512]{1,0:T(8,128)(2,1)S(1)}, bf16[192,512]{1,0:T(8,128)(2,1)}, u32[]{:S(2)}, u32[]{:S(2)}) collective-permute-start(bf16[192,512]{1,0:T(8,128)(2,1)S(1)} %fusion.21), channel_id=1, source_target_pairs={{0,1},{1,0},{2,3},{3,2},{4,5},{5,4},{6,7},{7,6},{8,9},{9,8},{10,11... | collective-permute-start | bytes 589832 | tf_op jit(solution)/shard_map/experts/ppermute | solution.py:24
  96.2 10.3 %collective-permute-start.12 = (bf16[192,512]{1,0:T(8,128)(2,1)S(1)}, bf16[192,512]{1,0:T(8,128)(2,1)S(1)}, u32[]{:S(2)}, u32[]{:S(2)}) collective-permute-start(bf16[192,512]{1,0:T(8,128)(2,1)S(1)} %fusion.21), channel_id=1, source_target_pairs={{0,2},{2,4},{4,6},{6,0},{1,3},{3,5},{5,7},{7,1},{8,10},{10,12},{12... | collective-permute-start | bytes 589832 | tf_op jit(solution)/shard_map/experts/ppermute | solution.py:20
  106.5 9.3 %collective-permute-start.16 = (bf16[192,512]{1,0:T(8,128)(2,1)S(1)}, bf16[192,512]{1,0:T(8,128)(2,1)S(1)}, u32[]{:S(2)}, u32[]{:S(2)}) collective-permute-start(bf16[192,512]{1,0:T(8,128)(2,1)S(1)} %collective-permute-done.12), channel_id=1, source_target_pairs={{0,1},{1,0},{2,3},{3,2},{4,5},{5,4},{6,7},{7,6},{8,9},{9,8},{10,11... | collective-permute-start | bytes 589832 | tf_op jit(solution)/shard_map/experts/ppermute | solution.py:24
  109.3 6.8 %collective-permute-start.17 = (bf16[192,512]{1,0:T(8,128)(2,1)S(1)}, bf16[192,512]{1,0:T(8,128)(2,1)S(1)}, u32[]{:S(2)}, u32[]{:S(2)}) collective-permute-start(bf16[192,512]{1,0:T(8,128)(2,1)S(1)} %collective-permute-done.11), channel_id=1, source_target_pairs={{0,1},{1,0},{2,3},{3,2},{4,5},{5,4},{6,7},{7,6},{8,9},{9,8},{10,11... | collective-permute-start | bytes 589832 | tf_op jit(solution)/shard_map/experts/ppermute | solution.py:24
  111.2 5.4 %collective-permute-start.15 = (bf16[192,512]{1,0:T(8,128)(2,1)S(1)}, bf16[192,512]{1,0:T(8,128)(2,1)S(1)}, u32[]{:S(2)}, u32[]{:S(2)}) collective-permute-start(bf16[192,512]{1,0:T(8,128)(2,1)S(1)} %collective-permute-done.13), channel_id=1, source_target_pairs={{0,1},{1,0},{2,3},{3,2},{4,5},{5,4},{6,7},{7,6},{8,9},{9,8},{10,11... | collective-permute-start | bytes 589832 | tf_op jit(solution)/shard_map/experts/ppermute | solution.py:24
  116.1 27.6 %copy-start.17 = (pred[16,256]{1,0:T(8,128)(4,1)S(1)}, pred[16,256]{1,0:T(8,128)(4,1)}, u32[]{:S(2)}) copy-start(pred[16,256]{1,0:T(8,128)(4,1)} %copy-done.16) | copy-start | bytes 12292
  116.7 63.5 %copy-start.12 = (bf16[192,512]{1,0:T(8,128)(2,1)}, bf16[192,512]{1,0:T(8,128)(2,1)S(1)}, u32[]{:S(2)}) copy-start(bf16[192,512]{1,0:T(8,128)(2,1)S(1)} %collective-permute-done.15) | copy-start | bytes 589828
  117.7 26.1 %all-to-all-start.1 = ((bf16[16,32,256]{2,1,0:T(8,128)(2,1)}), bf16[16,32,256]{2,1,0:T(8,128)(2,1)S(1)}, u32[]{:S(2)}, u32[]{:S(2)}) async-start(bf16[16,32,256]{2,1,0:T(8,128)(2,1)} %bitcast.18), calls=%async_computation.1 | async-start | bytes 524288 | tf_op jit(solution)/shard_map/combine/all_to_all | solution.py:88
  144.1 17.0 %collective-permute-start.18 = (bf16[128,256]{1,0:T(8,128)(2,1)S(1)}, bf16[128,256]{1,0:T(8,128)(2,1)S(1)}, u32[]{:S(2)}, u32[]{:S(2)}) collective-permute-start(bf16[128,256]{1,0:T(8,128)(2,1)S(1)} %get-tuple-element.28), channel_id=1, source_target_pairs={{0,8},{8,0},{16,24},{24,16},{32,40},{40,32},{48,56},{56,48},{1,9},... | collective-permute-start | bytes 196616 | tf_op jit(solution)/shard_map/combine/ppermute | solution.py:28
  151.5 9.6 %collective-permute-start.19 = (bf16[128,256]{1,0:T(8,128)(2,1)S(1)}, bf16[128,256]{1,0:T(8,128)(2,1)S(1)}, u32[]{:S(2)}, u32[]{:S(2)}) collective-permute-start(bf16[128,256]{1,0:T(8,128)(2,1)S(1)} %get-tuple-element.29), channel_id=1, source_target_pairs={{0,16},{8,24},{16,0},{24,8},{32,48},{40,56},{48,32},{56,40},{1,17}... | collective-permute-start | bytes 196616 | tf_op jit(solution)/shard_map/combine/ppermute | solution.py:28
  154.6 6.5 %collective-permute-start.20 = (bf16[128,256]{1,0:T(8,128)(2,1)S(1)}, bf16[128,256]{1,0:T(8,128)(2,1)S(1)}, u32[]{:S(2)}, u32[]{:S(2)}) collective-permute-start(bf16[128,256]{1,0:T(8,128)(2,1)S(1)} %get-tuple-element.29), channel_id=1, source_target_pairs={{0,32},{8,40},{16,48},{24,56},{32,0},{40,8},{48,16},{56,24},{1,33}... | collective-permute-start | bytes 196616 | tf_op jit(solution)/shard_map/combine/ppermute | solution.py:28
  159.0 6.2 %collective-permute-start.21 = (bf16[128,256]{1,0:T(8,128)(2,1)S(1)}, bf16[128,256]{1,0:T(8,128)(2,1)S(1)}, u32[]{:S(2)}, u32[]{:S(2)}) collective-permute-start(bf16[128,256]{1,0:T(8,128)(2,1)S(1)} %get-tuple-element.29), channel_id=1, source_target_pairs={{0,48},{8,56},{16,32},{24,40},{32,16},{40,24},{48,0},{56,8},{1,49}... | collective-permute-start | bytes 196616 | tf_op jit(solution)/shard_map/combine/ppermute | solution.py:28
  165.2 11.8 %collective-permute-start.22 = (bf16[128,256]{1,0:T(8,128)(2,1)S(1)}, bf16[128,256]{1,0:T(8,128)(2,1)S(1)}, u32[]{:S(2)}, u32[]{:S(2)}) collective-permute-start(bf16[128,256]{1,0:T(8,128)(2,1)S(1)} %add_convert_fusion.2), channel_id=1, source_target_pairs={{0,8},{8,0},{16,24},{24,16},{32,40},{40,32},{48,56},{56,48},{1,9},... | collective-permute-start | bytes 196616 | tf_op jit(solution)/shard_map/combine/ppermute | solution.py:28
  167.4 9.6 %collective-permute-start.23 = (bf16[128,256]{1,0:T(8,128)(2,1)S(1)}, bf16[128,256]{1,0:T(8,128)(2,1)S(1)}, u32[]{:S(2)}, u32[]{:S(2)}) collective-permute-start(bf16[128,256]{1,0:T(8,128)(2,1)S(1)} %add_convert_fusion.3), channel_id=1, source_target_pairs={{0,16},{8,24},{16,0},{24,8},{32,48},{40,56},{48,32},{56,40},{1,17}... | collective-permute-start | bytes 196616 | tf_op jit(solution)/shard_map/combine/ppermute | solution.py:28
  169.3 7.7 %collective-permute-start.24 = (bf16[128,256]{1,0:T(8,128)(2,1)S(1)}, bf16[128,256]{1,0:T(8,128)(2,1)S(1)}, u32[]{:S(2)}, u32[]{:S(2)}) collective-permute-start(bf16[128,256]{1,0:T(8,128)(2,1)S(1)} %add_convert_fusion.3), channel_id=1, source_target_pairs={{0,32},{8,40},{16,48},{24,56},{32,0},{40,8},{48,16},{56,24},{1,33}... | collective-permute-start | bytes 196616 | tf_op jit(solution)/shard_map/combine/ppermute | solution.py:28
  172.9 6.2 %collective-permute-start.25 = (bf16[128,256]{1,0:T(8,128)(2,1)S(1)}, bf16[128,256]{1,0:T(8,128)(2,1)S(1)}, u32[]{:S(2)}, u32[]{:S(2)}) collective-permute-start(bf16[128,256]{1,0:T(8,128)(2,1)S(1)} %add_convert_fusion.3), channel_id=1, source_target_pairs={{0,48},{8,56},{16,32},{24,40},{32,16},{40,24},{48,0},{56,8},{1,49}... | collective-permute-start | bytes 196616 | tf_op jit(solution)/shard_map/combine/ppermute | solution.py:28
  180.1 35.8 %all-to-all-start.2 = ((bf16[16,32,256]{2,1,0:T(8,128)(2,1)}), bf16[16,32,256]{2,1,0:T(8,128)(2,1)S(1)}, u32[]{:S(2)}, u32[]{:S(2)}) async-start(bf16[16,32,256]{2,1,0:T(8,128)(2,1)} %bitcast.20), calls=%async_computation.2 | async-start | bytes 524288 | tf_op jit(solution)/shard_map/curvature/all_to_all | solution.py:88
  190.6 25.4 %copy-start.13 = (bf16[192,512]{1,0:T(8,128)(2,1)S(1)}, bf16[192,512]{1,0:T(8,128)(2,1)}, u32[]{:S(2)}) copy-start(bf16[192,512]{1,0:T(8,128)(2,1)} %copy-done.12) | copy-start | bytes 589828
  190.6 17.6 %collective-permute-start.26 = (bf16[256,256]{1,0:T(8,128)(2,1)S(1)}, bf16[256,256]{1,0:T(8,128)(2,1)S(1)}, u32[]{:S(2)}, u32[]{:S(2)}) collective-permute-start(bf16[256,256]{1,0:T(8,128)(2,1)S(1)} %get-tuple-element.53), channel_id=1, source_target_pairs={{0,4},{2,6},{4,0},{6,2},{1,5},{3,7},{5,1},{7,3},{8,12},{10,14},{12... | collective-permute-start | bytes 393224 | tf_op jit(solution)/shard_map/tangent/ppermute | solution.py:20
  194.3 15.9 %collective-permute-start.27 = (bf16[256,256]{1,0:T(8,128)(2,1)S(1)}, bf16[256,256]{1,0:T(8,128)(2,1)S(1)}, u32[]{:S(2)}, u32[]{:S(2)}) collective-permute-start(bf16[256,256]{1,0:T(8,128)(2,1)S(1)} %get-tuple-element.53), channel_id=1, source_target_pairs={{0,2},{2,4},{4,6},{6,0},{1,3},{3,5},{5,7},{7,1},{8,10},{10,12},{12... | collective-permute-start | bytes 393224 | tf_op jit(solution)/shard_map/tangent/ppermute | solution.py:20
  197.4 15.2 %collective-permute-start.28 = (bf16[256,256]{1,0:T(8,128)(2,1)S(1)}, bf16[256,256]{1,0:T(8,128)(2,1)S(1)}, u32[]{:S(2)}, u32[]{:S(2)}) collective-permute-start(bf16[256,256]{1,0:T(8,128)(2,1)S(1)} %get-tuple-element.53), channel_id=1, source_target_pairs={{0,6},{2,0},{4,2},{6,4},{1,7},{3,1},{5,3},{7,5},{8,14},{10,8},{12,... | collective-permute-start | bytes 393224 | tf_op jit(solution)/shard_map/tangent/ppermute | solution.py:20
  201.4 13.2 %collective-permute-start.29 = (bf16[256,256]{1,0:T(8,128)(2,1)S(1)}, bf16[256,256]{1,0:T(8,128)(2,1)S(1)}, u32[]{:S(2)}, u32[]{:S(2)}) collective-permute-start(bf16[256,256]{1,0:T(8,128)(2,1)S(1)} %get-tuple-element.53), channel_id=1, source_target_pairs={{0,1},{1,0},{2,3},{3,2},{4,5},{5,4},{6,7},{7,6},{8,9},{9,8},{10,11... | collective-permute-start | bytes 393224 | tf_op jit(solution)/shard_map/tangent/ppermute | solution.py:24
  208.2 7.7 %collective-permute-start.32 = (bf16[256,256]{1,0:T(8,128)(2,1)S(1)}, bf16[256,256]{1,0:T(8,128)(2,1)S(1)}, u32[]{:S(2)}, u32[]{:S(2)}) collective-permute-start(bf16[256,256]{1,0:T(8,128)(2,1)S(1)} %collective-permute-done.26), channel_id=1, source_target_pairs={{0,1},{1,0},{2,3},{3,2},{4,5},{5,4},{6,7},{7,6},{8,9},{9,8},{10,11... | collective-permute-start | bytes 393224 | tf_op jit(solution)/shard_map/tangent/ppermute | solution.py:24
  210.2 5.7 %collective-permute-start.31 = (bf16[256,256]{1,0:T(8,128)(2,1)S(1)}, bf16[256,256]{1,0:T(8,128)(2,1)S(1)}, u32[]{:S(2)}, u32[]{:S(2)}) collective-permute-start(bf16[256,256]{1,0:T(8,128)(2,1)S(1)} %collective-permute-done.27), channel_id=1, source_target_pairs={{0,1},{1,0},{2,3},{3,2},{4,5},{5,4},{6,7},{7,6},{8,9},{9,8},{10,11... | collective-permute-start | bytes 393224 | tf_op jit(solution)/shard_map/tangent/ppermute | solution.py:24
  212.6 3.2 %collective-permute-start.30 = (bf16[256,256]{1,0:T(8,128)(2,1)S(1)}, bf16[256,256]{1,0:T(8,128)(2,1)S(1)}, u32[]{:S(2)}, u32[]{:S(2)}) collective-permute-start(bf16[256,256]{1,0:T(8,128)(2,1)S(1)} %collective-permute-done.28), channel_id=1, source_target_pairs={{0,1},{1,0},{2,3},{3,2},{4,5},{5,4},{6,7},{7,6},{8,9},{9,8},{10,11... | collective-permute-start | bytes 393224 | tf_op jit(solution)/shard_map/tangent/ppermute | solution.py:24
  217.8 14.3 %collective-permute-start.36 = (bf16[768,256]{1,0:T(8,128)(2,1)S(1)}, bf16[768,256]{1,0:T(8,128)(2,1)S(1)}, u32[]{:S(2)}, u32[]{:S(2)}) collective-permute-start(bf16[768,256]{1,0:T(8,128)(2,1)S(1)} %convolution_convert_fusion), channel_id=1, source_target_pairs={{0,1},{1,0},{2,3},{3,2},{4,5},{5,4},{6,7},{7,6},{8,9},{9,8},{10,11... | collective-permute-start | bytes 1179656 | tf_op jit(solution)/shard_map/curvature/ppermute | solution.py:24
  220.1 15.9 %collective-permute-start.35 = (bf16[192,256]{1,0:T(8,128)(2,1)S(1)}, bf16[192,256]{1,0:T(8,128)(2,1)S(1)}, u32[]{:S(2)}, u32[]{:S(2)}) collective-permute-start(bf16[192,256]{1,0:T(8,128)(2,1)S(1)} %convolution_convert_fusion.3), channel_id=1, source_target_pairs={{0,6},{2,0},{4,2},{6,4},{1,7},{3,1},{5,3},{7,5},{8,14},{10,8},{12,... | collective-permute-start | bytes 294920 | tf_op jit(solution)/shard_map/curvature/ppermute | solution.py:20
  222.3 8.9 %collective-permute-start.33 = (bf16[192,256]{1,0:T(8,128)(2,1)S(1)}, bf16[192,256]{1,0:T(8,128)(2,1)S(1)}, u32[]{:S(2)}, u32[]{:S(2)}) collective-permute-start(bf16[192,256]{1,0:T(8,128)(2,1)S(1)} %convolution_convert_fusion.5), channel_id=1, source_target_pairs={{0,4},{2,6},{4,0},{6,2},{1,5},{3,7},{5,1},{7,3},{8,12},{10,14},{12... | collective-permute-start | bytes 294920 | tf_op jit(solution)/shard_map/curvature/ppermute | solution.py:20
  225.0 7.2 %collective-permute-start.34 = (bf16[192,256]{1,0:T(8,128)(2,1)S(1)}, bf16[192,256]{1,0:T(8,128)(2,1)S(1)}, u32[]{:S(2)}, u32[]{:S(2)}) collective-permute-start(bf16[192,256]{1,0:T(8,128)(2,1)S(1)} %convolution_convert_fusion.4), channel_id=1, source_target_pairs={{0,2},{2,4},{4,6},{6,0},{1,3},{3,5},{5,7},{7,1},{8,10},{10,12},{12... | collective-permute-start | bytes 294920 | tf_op jit(solution)/shard_map/curvature/ppermute | solution.py:20
  232.2 10.9 %collective-permute-start.37 = (bf16[192,256]{1,0:T(8,128)(2,1)S(1)}, bf16[192,256]{1,0:T(8,128)(2,1)S(1)}, u32[]{:S(2)}, u32[]{:S(2)}) collective-permute-start(bf16[192,256]{1,0:T(8,128)(2,1)S(1)} %get-tuple-element.42), channel_id=1, source_target_pairs={{0,4},{2,6},{4,0},{6,2},{1,5},{3,7},{5,1},{7,3},{8,12},{10,14},{12... | collective-permute-start | bytes 294920 | tf_op jit(solution)/shard_map/curvature/ppermute | solution.py:20
  236.0 7.2 %collective-permute-start.38 = (bf16[192,256]{1,0:T(8,128)(2,1)S(1)}, bf16[192,256]{1,0:T(8,128)(2,1)S(1)}, u32[]{:S(2)}, u32[]{:S(2)}) collective-permute-start(bf16[192,256]{1,0:T(8,128)(2,1)S(1)} %get-tuple-element.41), channel_id=1, source_target_pairs={{0,2},{2,4},{4,6},{6,0},{1,3},{3,5},{5,7},{7,1},{8,10},{10,12},{12... | collective-permute-start | bytes 294920 | tf_op jit(solution)/shard_map/curvature/ppermute | solution.py:20
  238.7 6.9 %collective-permute-start.39 = (bf16[192,256]{1,0:T(8,128)(2,1)S(1)}, bf16[192,256]{1,0:T(8,128)(2,1)S(1)}, u32[]{:S(2)}, u32[]{:S(2)}) collective-permute-start(bf16[192,256]{1,0:T(8,128)(2,1)S(1)} %get-tuple-element.40), channel_id=1, source_target_pairs={{0,6},{2,0},{4,2},{6,4},{1,7},{3,1},{5,3},{7,5},{8,14},{10,8},{12,... | collective-permute-start | bytes 294920 | tf_op jit(solution)/shard_map/curvature/ppermute | solution.py:20
  (18 other events, 174.3 us)

commit v4 on v1

--- a/solution.py
+++ b/solution.py
@@ -7,6 +7,8 @@
 EXP_COL = 8
 CORES = 2
 LINE = 4
+HALVES = 2
+STEPS = (2, 1, 3)
 
 
 def contract_rows(left, right):
@@ -23,8 +25,8 @@
     return lax.ppermute(value, "core", [(i, i ^ 1) for i in range(CORES)])
 
 
-def swap_local(value, mask):
-    return lax.ppermute(value, "local", [(i, i ^ mask) for i in range(EXP_COL)])
+def swap_halves(value):
+    return lax.ppermute(value, "half", [(i, i ^ 1) for i in range(HALVES)])
 
 
 def shards(tokens, routes, combine, gate_weight, up_weight, direction):
@@ -35,7 +37,7 @@
     cols = width // n_slice
     slot_count = 2 * col_tok * TOP // (EXP_COL * n_expert)
     rows = n_expert * slot_count
-    local_index = lax.axis_index("local")
+    local_index = lax.axis_index(("x", "half"))
     line_index = lax.axis_index("line")
     core_index = lax.axis_index("core")
 
@@ -70,7 +72,7 @@
 
     def gather_blocks(block):
         blocks = {(0, 0): block}
-        for step in (2, 1, 3):
+        for step in STEPS:
             blocks[(LINE - step, 0)] = shift_line(block, step)
         for step in (0, 1, 3, 2):
             blocks[(step, 1)] = swap_cores(blocks[(step, 0)])
@@ -95,39 +97,46 @@
         hidden = hidden.astype(jnp.bfloat16)
 
     with jax.named_scope("combine"):
-        def slice_out(step, other):
-            return jnp.dot(
-                hidden, columns(direction, step, other), preferred_element_type=jnp.float32
+        other_cols = jnp.concatenate([columns(direction, step, 1) for step in range(LINE)], axis=1)
+        crossed = swap_cores(
+            jnp.dot(hidden, other_cols, preferred_element_type=jnp.float32).astype(jnp.bfloat16)
+        )
+
+        def pair_out(step):
+            own = jnp.dot(
+                hidden, columns(direction, step, 0), preferred_element_type=jnp.float32
             )
+            other = crossed[:, step * cols : (step + 1) * cols].astype(jnp.float32)
+            return (own + other).astype(jnp.bfloat16)
 
-        steps = (2, 1, 3, 0)
-        swapped = {
-            step: swap_cores(slice_out(step, 1).astype(jnp.bfloat16)) for step in steps
-        }
-        pair_out = {
-            step: (slice_out(step, 0) + swapped[step].astype(jnp.float32)).astype(jnp.bfloat16)
-            for step in steps
-        }
-        expert_out = pair_out[0].astype(jnp.float32)
-        for step in steps[:3]:
-            expert_out += shift_line(pair_out[step], step).astype(jnp.float32)
+        arrived = [shift_line(pair_out(step), step).astype(jnp.float32) for step in STEPS]
+        expert_out = pair_out(0).astype(jnp.float32) + arrived[0] + arrived[1] + arrived[2]
         returned = over_planes(expert_out.astype(jnp.bfloat16))
-        part = lax.optimization_barrier(contract_rows(spread, returned).astype(jnp.bfloat16))
-        near = [swap_local(part, mask).astype(jnp.float32) for mask in (2, 4, 6)]
-        half = (part.astype(jnp.float32) + near[0]) + (near[1] + near[2])
-        half = lax.optimization_barrier(half.astype(jnp.bfloat16))
-        total = half.astype(jnp.float32) + swap_local(half, 1).astype(jnp.float32)
+        part = contract_rows(spread, returned).astype(jnp.bfloat16)
+        parts = lax.all_to_all(
+            jnp.broadcast_to(part, (EXP_COL // HALVES, col_tok, cols)), "x", 0, 0, tiled=True
+        )
+        half = jnp.sum(parts.astype(jnp.float32), axis=0).astype(jnp.bfloat16)
+        half = lax.optimization_barrier(half)
+        total = half.astype(jnp.float32) + swap_halves(half).astype(jnp.float32)
         tangent_cols = total.astype(jnp.bfloat16)
-
-    with jax.named_scope("tangent"):
-        tangent_out = lax.all_gather(tangent_cols, ("line", "core"))
-        tangent_out = tangent_out.transpose(1, 0, 2).reshape(col_tok, width)
 
     with jax.named_scope("curvature"):
         picked = jnp.dot(select, tangent_cols, preferred_element_type=jnp.float32)
         scaled = (picked * slot_weight).astype(jnp.bfloat16)
+        scaled, tangent_late = lax.optimization_barrier((scaled, tangent_cols))
+        moved = over_planes(scaled)
+
+    with jax.named_scope("tangent"):
+        tangent_out = jnp.zeros((col_tok, width), jnp.bfloat16)
+        for (step, other), block in gather_blocks(tangent_late).items():
+            tangent_out = lax.dynamic_update_slice_in_dim(
+                tangent_out, block, first_col(step, other), 1
+            )
+
+    with jax.named_scope("curvature"):
         curvature = jnp.zeros((unit_count, width), jnp.bfloat16)
-        for (step, other), block in gather_blocks(over_planes(scaled)).items():
+        for (step, other), block in gather_blocks(moved).items():
             curvature = lax.dynamic_update_slice_in_dim(
                 curvature,
                 contract_rows(hidden, block).astype(jnp.bfloat16),
@@ -140,10 +149,11 @@
 def solution(mesh):
     n_expert = mesh.shape["expert"]
     fine = Mesh(
-        mesh.devices.reshape(n_expert, EXP_COL, LINE, CORES), ("expert", "local", "line", "core")
+        mesh.devices.reshape(n_expert, EXP_COL // HALVES, HALVES, LINE, CORES),
+        ("expert", "x", "half", "line", "core"),
     )
     by_block = P("expert", None)
-    by_device = P(("expert", "local", "line", "core"), None)
+    by_device = P(("expert", "x", "half", "line", "core"), None)
     return jax.shard_map(
         shards,
         mesh=fine,

time: 248 us -> 225 us (0.907); the launches traced: 247 us -> 221 us
  between operations: 14.8 us -> 1.43 us
  blocking collectives: 23 us -> 10.7 us
  starting transfers between devices: 125 us -> 129 us
  waiting for transfers between devices: 67.3 us -> 63.5 us
    ppermute x9 -> x12, starting transfers between devices: 29.5 us -> 46 us  [shift_line(): lax.ppermute(value, 'line', [(i, (i + step) % LINE) for i in range(LINE)])]
    all_gather x1 -> x0, waiting for transfers between devices: 15.5 us -> none  [shards(): tangent_out = lax.all_gather(tangent_cols, ('line', 'core'))]
    ppermute x9 -> x12, waiting for transfers between devices: 16.9 us -> 32 us  [shift_line(): lax.ppermute(value, 'line', [(i, (i + step) % LINE) for i in range(LINE)])]
    ppermute x12 -> x13, starting transfers between devices: 51.8 us -> 38.9 us  [swap_cores(): return lax.ppermute(value, 'core', [(i, i ^ 1) for i in range(CORES)])]
    all_to_all x1, blocking collectives: 23 us -> 10.7 us  [shards(): lax.all_to_all(jnp.broadcast_to(part, (EXP_COL // HALVES, col_tok, cols))...]
    all_to_all x2 -> x3, starting transfers between devices: 28.7 us -> 36.9 us  [over_planes(): lax.all_to_all(slots.reshape(n_expert, slot_count, cols), 'expert', 0, 0,...]
    ppermute x4 -> x1, starting transfers between devices: 15.1 us -> 7.24 us  [swap_halves(): return lax.ppermute(value, 'half', [(i, i ^ 1) for i in range(HALVES)])]
    ppermute x4 -> x1, waiting for transfers between devices: 8.64 us -> 2.1 us  [swap_halves(): return lax.ppermute(value, 'half', [(i, i ^ 1) for i in range(HALVES)])]
  transfers between devices with their start and end apart: 28 -> 29, of which waited for: 10 -> 13; matrix products, arithmetic and copies ran while one was open for 3% -> 4% of each run, Pallas kernels for 0% -> 0%
where the time goes in v4:
time: 225 us; the launch traced here: 221 us
  starting transfers between devices  129 us (57%)
  waiting for transfers between devices  63.5 us (28%)
  blocking collectives  10.7 us (5%)
  matrix products  7.84 us (3%)
  local copies, waits for them, and re-layouts  5.25 us (2%)
  other arithmetic  3.16 us (1%)
    ppermute x12, starting transfers between devices, shift_line(): lax.ppermute(value, 'line', [(i, (i + step) % LINE) for i in range(LINE)])  46 us
    ppermute x13, starting transfers between devices, swap_cores(): return lax.ppermute(value, 'core', [(i, i ^ 1) for i in range(CORES)])  38.9 us
    all_to_all x3, starting transfers between devices, over_planes(): lax.all_to_all(slots.reshape(n_expert, slot_count, cols), 'expert', 0, 0,...  36.9 us
    ppermute x12, waiting for transfers between devices, shift_line(): lax.ppermute(value, 'line', [(i, (i + step) % LINE) for i in range(LINE)])  32 us
    all_to_all x3, waiting for transfers between devices, over_planes(): lax.all_to_all(slots.reshape(n_expert, slot_count, cols), 'expert', 0, 0,...  24.3 us
    all_to_all x1, blocking collectives, shards(): lax.all_to_all(jnp.broadcast_to(part, (EXP_COL // HALVES, col_tok, cols))...  10.7 us
    ppermute x1, starting transfers between devices, swap_halves(): return lax.ppermute(value, 'half', [(i, i ^ 1) for i in range(HALVES)])  7.24 us
    ppermute x13, waiting for transfers between devices, swap_cores(): return lax.ppermute(value, 'core', [(i, i ^ 1) for i in range(CORES)])  5.04 us
  transfers between devices with their start and end apart: 29, of which 13 were waited for; matrix products, arithmetic and copies ran while one was open for 4% of the time, Pallas kernels for 0%

profile of v4, /device:TPU:1, one launch (start us, length us, event | category | flops | bytes accessed | tf_op | source)
XLA Modules:
  0.0 220.9 jit_solution(4304624750551386214)
XLA Ops:
  0.7 0.9 compare_reduce_fusion
  2.7 1.0 convolution_convert_fusion.1
  3.7 19.4 %all-to-all-start = ((bf16[16,32,256]{2,1,0:T(8,128)(2,1)}), bf16[16,32,256]{2,1,0:T(8,128)(2,1)S(1)}, u32[]{:S(2)}, u32[]{:S(2)}) async-start(bf16[16,32,256]{2,1,0:T(8,128)(2,1)} %bitcast.2), calls=%async_computation | async-start | bytes 524288 | tf_op jit(solution)/shard_map/dispatch/all_to_all | solution.py:68
  23.2 1.3 constant_dynamic-update-slice_fusion.9
  24.6 11.7 %all-to-all-done = bf16[16,32,256]{2,1,0:T(8,128)(2,1)S(1)} async-done(((bf16[16,32,256]{2,1,0:T(8,128)(2,1)}), bf16[16,32,256]{2,1,0:T(8,128)(2,1)S(1)}, u32[]{:S(2)}, u32[]{:S(2)}) %all-to-all-start) | async-done | bytes 262176 | tf_op jit(solution)/shard_map/dispatch/all_to_all | solution.py:68
  36.3 8.1 %collective-permute-start.3 = (bf16[512,256]{1,0:T(8,128)(2,1)S(1)}, bf16[512,256]{1,0:T(8,128)(2,1)S(1)}, u32[]{:S(2)}, u32[]{:S(2)}) collective-permute-start(bf16[512,256]{1,0:T(8,128)(2,1)S(1)} %bitcast.63), channel_id=1, source_target_pairs={{0,1},{1,0},{2,3},{3,2},{4,5},{5,4},{6,7},{7,6},{8,9},{9,8},{10,11... | collective-permute-start | bytes 786440 | tf_op jit(solution)/shard_map/dispatch/ppermute | solution.py:25
  44.3 1.8 constant_dynamic-slice_fusion.3
  46.1 4.2 %collective-permute-start = (bf16[512,256]{1,0:T(8,128)(2,1)S(1)}, bf16[512,256]{1,0:T(8,128)(2,1)S(1)}, u32[]{:S(2)}, u32[]{:S(2)}) collective-permute-start(bf16[512,256]{1,0:T(8,128)(2,1)S(1)} %bitcast.64), channel_id=1, source_target_pairs={{0,4},{2,6},{4,0},{6,2},{1,5},{3,7},{5,1},{7,3},{8,12},{10,14},{12... | collective-permute-start | bytes 786440 | tf_op jit(solution)/shard_map/dispatch/ppermute | solution.py:21
  50.3 2.9 %collective-permute-start.2 = (bf16[512,256]{1,0:T(8,128)(2,1)S(1)}, bf16[512,256]{1,0:T(8,128)(2,1)S(1)}, u32[]{:S(2)}, u32[]{:S(2)}) collective-permute-start(bf16[512,256]{1,0:T(8,128)(2,1)S(1)} %bitcast.65), channel_id=1, source_target_pairs={{0,6},{2,0},{4,2},{6,4},{1,7},{3,1},{5,3},{7,5},{8,14},{10,8},{12,... | collective-permute-start | bytes 786440 | tf_op jit(solution)/shard_map/dispatch/ppermute | solution.py:21
  53.3 2.3 %collective-permute-start.1 = (bf16[512,256]{1,0:T(8,128)(2,1)S(1)}, bf16[512,256]{1,0:T(8,128)(2,1)S(1)}, u32[]{:S(2)}, u32[]{:S(2)}) collective-permute-start(bf16[512,256]{1,0:T(8,128)(2,1)S(1)} %bitcast.66), channel_id=1, source_target_pairs={{0,2},{2,4},{4,6},{6,0},{1,3},{3,5},{5,7},{7,1},{8,10},{10,12},{12... | collective-permute-start | bytes 786440 | tf_op jit(solution)/shard_map/dispatch/ppermute | solution.py:21
  56.2 6.2 %collective-permute-done = bf16[512,256]{1,0:T(8,128)(2,1)S(1)} collective-permute-done((bf16[512,256]{1,0:T(8,128)(2,1)S(1)}, bf16[512,256]{1,0:T(8,128)(2,1)S(1)}, u32[]{:S(2)}, u32[]{:S(2)}) %collective-permute-start) | collective-permute-done | bytes 262176 | tf_op jit(solution)/shard_map/dispatch/ppermute | solution.py:21
  62.5 3.1 %collective-permute-start.6 = (bf16[512,256]{1,0:T(8,128)(2,1)S(1)}, bf16[512,256]{1,0:T(8,128)(2,1)S(1)}, u32[]{:S(2)}, u32[]{:S(2)}) collective-permute-start(bf16[512,256]{1,0:T(8,128)(2,1)S(1)} %collective-permute-done), channel_id=1, source_target_pairs={{0,1},{1,0},{2,3},{3,2},{4,5},{5,4},{6,7},{7,6},{8,9},{9,8},{10,11... | collective-permute-start | bytes 786440 | tf_op jit(solution)/shard_map/dispatch/ppermute | solution.py:25
  65.6 4.4 %collective-permute-done.2 = bf16[512,256]{1,0:T(8,128)(2,1)S(1)} collective-permute-done((bf16[512,256]{1,0:T(8,128)(2,1)S(1)}, bf16[512,256]{1,0:T(8,128)(2,1)S(1)}, u32[]{:S(2)}, u32[]{:S(2)}) %collective-permute-start.2) | collective-permute-done | bytes 262176 | tf_op jit(solution)/shard_map/dispatch/ppermute | solution.py:21
  70.0 3.0 %collective-permute-start.4 = (bf16[512,256]{1,0:T(8,128)(2,1)S(1)}, bf16[512,256]{1,0:T(8,128)(2,1)S(1)}, u32[]{:S(2)}, u32[]{:S(2)}) collective-permute-start(bf16[512,256]{1,0:T(8,128)(2,1)S(1)} %collective-permute-done.2), channel_id=1, source_target_pairs={{0,1},{1,0},{2,3},{3,2},{4,5},{5,4},{6,7},{7,6},{8,9},{9,8},{10,11... | collective-permute-start | bytes 786440 | tf_op jit(solution)/shard_map/dispatch/ppermute | solution.py:25
  73.3 1.9 collective-permute-start.5
  78.4 2.0 collective-permute-start.7
  80.5 2.5 %collective-permute-done.7 = bf16[512,1024]{1,0:T(8,128)(2,1)S(1)} collective-permute-done((bf16[512,1024]{1,0:T(8,128)(2,1)S(1)}, bf16[512,1024]{1,0:T(8,128)(2,1)S(1)}, u32[]{:S(2)}, u32[]{:S(2)}) %collective-permute-start.7) | collective-permute-done | bytes 1048608 | tf_op jit(solution)/shard_map/combine/ppermute | solution.py:25
  83.3 5.1 %collective-permute-start.8 = (bf16[512,256]{1,0:T(8,128)(2,1)S(1)}, bf16[512,256]{1,0:T(8,128)(2,1)S(1)}, u32[]{:S(2)}, u32[]{:S(2)}) collective-permute-start(bf16[512,256]{1,0:T(8,128)(2,1)S(1)} %add_convert_fusion.3), channel_id=1, source_target_pairs={{0,4},{2,6},{4,0},{6,2},{1,5},{3,7},{5,1},{7,3},{8,12},{10,14},{12... | collective-permute-start | bytes 786440 | tf_op jit(solution)/shard_map/combine/ppermute | solution.py:21
  88.6 2.5 %collective-permute-start.9 = (bf16[512,256]{1,0:T(8,128)(2,1)S(1)}, bf16[512,256]{1,0:T(8,128)(2,1)S(1)}, u32[]{:S(2)}, u32[]{:S(2)}) collective-permute-start(bf16[512,256]{1,0:T(8,128)(2,1)S(1)} %add_convert_fusion.2), channel_id=1, source_target_pairs={{0,2},{2,4},{4,6},{6,0},{1,3},{3,5},{5,7},{7,1},{8,10},{10,12},{12... | collective-permute-start | bytes 786440 | tf_op jit(solution)/shard_map/combine/ppermute | solution.py:21
  91.4 4.6 %collective-permute-start.10 = (bf16[512,256]{1,0:T(8,128)(2,1)S(1)}, bf16[512,256]{1,0:T(8,128)(2,1)S(1)}, u32[]{:S(2)}, u32[]{:S(2)}) collective-permute-start(bf16[512,256]{1,0:T(8,128)(2,1)S(1)} %add_convert_fusion.1), channel_id=1, source_target_pairs={{0,6},{2,0},{4,2},{6,4},{1,7},{3,1},{5,3},{7,5},{8,14},{10,8},{12,... | collective-permute-start | bytes 786440 | tf_op jit(solution)/shard_map/combine/ppermute | solution.py:21
  96.3 9.7 %collective-permute-done.8 = bf16[512,256]{1,0:T(8,128)(2,1)S(1)} collective-permute-done((bf16[512,256]{1,0:T(8,128)(2,1)S(1)}, bf16[512,256]{1,0:T(8,128)(2,1)S(1)}, u32[]{:S(2)}, u32[]{:S(2)}) %collective-permute-start.8) | collective-permute-done | bytes 262176 | tf_op jit(solution)/shard_map/combine/ppermute | solution.py:21
  106.0 3.0 %collective-permute-done.10 = bf16[512,256]{1,0:T(8,128)(2,1)S(1)} collective-permute-done((bf16[512,256]{1,0:T(8,128)(2,1)S(1)}, bf16[512,256]{1,0:T(8,128)(2,1)S(1)}, u32[]{:S(2)}, u32[]{:S(2)}) %collective-permute-start.10) | collective-permute-done | bytes 262176 | tf_op jit(solution)/shard_map/combine/ppermute | solution.py:21
  109.0 0.9 add_convert_fusion
  109.9 5.5 %all-to-all-start.1 = ((bf16[16,32,256]{2,1,0:T(8,128)(2,1)}), bf16[16,32,256]{2,1,0:T(8,128)(2,1)S(1)}, u32[]{:S(2)}, u32[]{:S(2)}) async-start(bf16[16,32,256]{2,1,0:T(8,128)(2,1)} %bitcast.4), calls=%async_computation.1 | async-start | bytes 524288 | tf_op jit(solution)/shard_map/combine/all_to_all | solution.py:68
  115.5 12.6 %all-to-all-done.1 = bf16[16,32,256]{2,1,0:T(8,128)(2,1)S(1)} async-done(((bf16[16,32,256]{2,1,0:T(8,128)(2,1)}), bf16[16,32,256]{2,1,0:T(8,128)(2,1)S(1)}, u32[]{:S(2)}, u32[]{:S(2)}) %all-to-all-start.1) | async-done | bytes 262176 | tf_op jit(solution)/shard_map/combine/all_to_all | solution.py:68
  128.5 10.7 %all_to_all.20 = bf16[4,256,256]{2,1,0:T(8,128)(2,1)S(1)} all-to-all(bf16[4,256,256]{2,1,0:T(8,128)(2,1)S(1)} %broadcast_in_dim.45), channel_id=1, replica_groups=mesh['expert'=16,'x'=4,'half'=2,'line'=4,'core'=2] {'x'}, dimensions={0} | all-to-all | bytes 1048576 | tf_op jit(solution)/shard_map/combine/all_to_all | solution.py:116
  139.4 7.2 %collective-permute-start.11 = (bf16[256,256]{1,0:T(8,128)(2,1)S(1)}, bf16[256,256]{1,0:T(8,128)(2,1)S(1)}, u32[]{:S(2)}, u32[]{:S(2)}) collective-permute-start(bf16[256,256]{1,0:T(8,128)(2,1)S(1)} %reduce_sum.31), channel_id=1, source_target_pairs={{0,8},{8,0},{1,9},{9,1},{2,10},{10,2},{3,11},{11,3},{4,12},{12,4},... | collective-permute-start | bytes 393224 | tf_op jit(solution)/shard_map/combine/ppermute | solution.py:29
  146.9 2.1 collective-permute-done.11
  149.0 0.9 fusion.4
  150.0 12.0 %all-to-all-start.3 = ((bf16[16,32,256]{2,1,0:T(8,128)(2,1)}), bf16[16,32,256]{2,1,0:T(8,128)(2,1)S(1)}, u32[]{:S(2)}, u32[]{:S(2)}) async-start(bf16[16,32,256]{2,1,0:T(8,128)(2,1)} %bitcast.6), calls=%async_computation.3 | async-start | bytes 524288 | tf_op jit(solution)/shard_map/curvature/all_to_all | solution.py:68
  161.9 8.2 %collective-permute-start.12 = (bf16[256,256]{1,0:T(8,128)(2,1)S(1)}, bf16[256,256]{1,0:T(8,128)(2,1)S(1)}, u32[]{:S(2)}, u32[]{:S(2)}) collective-permute-start(bf16[256,256]{1,0:T(8,128)(2,1)S(1)} %add_convert_fusion.5), channel_id=1, source_target_pairs={{0,4},{2,6},{4,0},{6,2},{1,5},{3,7},{5,1},{7,3},{8,12},{10,14},{12... | collective-permute-start | bytes 393224 | tf_op jit(solution)/shard_map/tangent/ppermute | solution.py:21
  170.1 1.9 collective-permute-start.13
  172.1 5.2 %collective-permute-start.14 = (bf16[256,256]{1,0:T(8,128)(2,1)S(1)}, bf16[256,256]{1,0:T(8,128)(2,1)S(1)}, u32[]{:S(2)}, u32[]{:S(2)}) collective-permute-start(bf16[256,256]{1,0:T(8,128)(2,1)S(1)} %add_convert_fusion.5), channel_id=1, source_target_pairs={{0,6},{2,0},{4,2},{6,4},{1,7},{3,1},{5,3},{7,5},{8,14},{10,8},{12,... | collective-permute-start | bytes 393224 | tf_op jit(solution)/shard_map/tangent/ppermute | solution.py:21
  177.2 5.2 %collective-permute-start.15 = (bf16[256,256]{1,0:T(8,128)(2,1)S(1)}, bf16[256,256]{1,0:T(8,128)(2,1)S(1)}, u32[]{:S(2)}, u32[]{:S(2)}) collective-permute-start(bf16[256,256]{1,0:T(8,128)(2,1)S(1)} %add_convert_fusion.5), channel_id=1, source_target_pairs={{0,1},{1,0},{2,3},{3,2},{4,5},{5,4},{6,7},{7,6},{8,9},{9,8},{10,11... | collective-permute-start | bytes 393224 | tf_op jit(solution)/shard_map/tangent/ppermute | solution.py:25
  182.6 1.9 collective-permute-start.18
  184.5 2.4 %collective-permute-start.17 = (bf16[256,256]{1,0:T(8,128)(2,1)S(1)}, bf16[256,256]{1,0:T(8,128)(2,1)S(1)}, u32[]{:S(2)}, u32[]{:S(2)}) collective-permute-start(bf16[256,256]{1,0:T(8,128)(2,1)S(1)} %collective-permute-done.13), channel_id=1, source_target_pairs={{0,1},{1,0},{2,3},{3,2},{4,5},{5,4},{6,7},{7,6},{8,9},{9,8},{10,11... | collective-permute-start | bytes 393224 | tf_op jit(solution)/shard_map/tangent/ppermute | solution.py:25
  187.0 1.9 collective-permute-start.16
  189.0 1.3 collective-permute-done.16
  190.3 1.9 collective-permute-start.19
  192.3 1.9 collective-permute-start.20
  194.2 5.2 %collective-permute-start.21 = (bf16[512,256]{1,0:T(8,128)(2,1)S(1)}, bf16[512,256]{1,0:T(8,128)(2,1)S(1)}, u32[]{:S(2)}, u32[]{:S(2)}) collective-permute-start(bf16[512,256]{1,0:T(8,128)(2,1)S(1)} %bitcast.60), channel_id=1, source_target_pairs={{0,6},{2,0},{4,2},{6,4},{1,7},{3,1},{5,3},{7,5},{8,14},{10,8},{12,... | collective-permute-start | bytes 786440 | tf_op jit(solution)/shard_map/curvature/ppermute | solution.py:21
  199.4 2.6 %collective-permute-start.22 = (bf16[512,256]{1,0:T(8,128)(2,1)S(1)}, bf16[512,256]{1,0:T(8,128)(2,1)S(1)}, u32[]{:S(2)}, u32[]{:S(2)}) collective-permute-start(bf16[512,256]{1,0:T(8,128)(2,1)S(1)} %bitcast.61), channel_id=1, source_target_pairs={{0,1},{1,0},{2,3},{3,2},{4,5},{5,4},{6,7},{7,6},{8,9},{9,8},{10,11... | collective-permute-start | bytes 786440 | tf_op jit(solution)/shard_map/curvature/ppermute | solution.py:25
  202.3 8.0 %collective-permute-done.19 = bf16[512,256]{1,0:T(8,128)(2,1)S(1)} collective-permute-done((bf16[512,256]{1,0:T(8,128)(2,1)S(1)}, bf16[512,256]{1,0:T(8,128)(2,1)S(1)}, u32[]{:S(2)}, u32[]{:S(2)}) %collective-permute-start.19) | collective-permute-done | bytes 262176 | tf_op jit(solution)/shard_map/curvature/ppermute | solution.py:21
  210.3 2.4 %collective-permute-start.25 = (bf16[512,256]{1,0:T(8,128)(2,1)S(1)}, bf16[512,256]{1,0:T(8,128)(2,1)S(1)}, u32[]{:S(2)}, u32[]{:S(2)}) collective-permute-start(bf16[512,256]{1,0:T(8,128)(2,1)S(1)} %collective-permute-done.19), channel_id=1, source_target_pairs={{0,1},{1,0},{2,3},{3,2},{4,5},{5,4},{6,7},{7,6},{8,9},{9,8},{10,11... | collective-permute-start | bytes 786440 | tf_op jit(solution)/shard_map/curvature/ppermute | solution.py:25
  212.9 1.9 collective-permute-start.24
  215.1 0.7 collective-permute-done.21
  215.8 2.4 %collective-permute-start.23 = (bf16[512,256]{1,0:T(8,128)(2,1)S(1)}, bf16[512,256]{1,0:T(8,128)(2,1)S(1)}, u32[]{:S(2)}, u32[]{:S(2)}) collective-permute-start(bf16[512,256]{1,0:T(8,128)(2,1)S(1)} %collective-permute-done.21), channel_id=1, source_target_pairs={{0,1},{1,0},{2,3},{3,2},{4,5},{5,4},{6,7},{7,6},{8,9},{9,8},{10,11... | collective-permute-start | bytes 786440 | tf_op jit(solution)/shard_map/curvature/ppermute | solution.py:25
  220.0 0.9 copy-done.3
  (86 shorter events, 10.0 us)
Async XLA Ops:
  0.6 2.1 copy-start
  3.7 32.6 %all-to-all-start = ((bf16[16,32,256]{2,1,0:T(8,128)(2,1)}), bf16[16,32,256]{2,1,0:T(8,128)(2,1)S(1)}, u32[]{:S(2)}, u32[]{:S(2)}) async-start(bf16[16,32,256]{2,1,0:T(8,128)(2,1)} %bitcast.2), calls=%async_computation | async-start | bytes 524288 | tf_op jit(solution)/shard_map/dispatch/all_to_all | solution.py:68
  23.2 1.4 copy-start.2
  36.3 19.7 %collective-permute-start.3 = (bf16[512,256]{1,0:T(8,128)(2,1)S(1)}, bf16[512,256]{1,0:T(8,128)(2,1)S(1)}, u32[]{:S(2)}, u32[]{:S(2)}) collective-permute-start(bf16[512,256]{1,0:T(8,128)(2,1)S(1)} %bitcast.63), channel_id=1, source_target_pairs={{0,1},{1,0},{2,3},{3,2},{4,5},{5,4},{6,7},{7,6},{8,9},{9,8},{10,11... | collective-permute-start | bytes 786440 | tf_op jit(solution)/shard_map/dispatch/ppermute | solution.py:25
  46.1 16.4 %collective-permute-start = (bf16[512,256]{1,0:T(8,128)(2,1)S(1)}, bf16[512,256]{1,0:T(8,128)(2,1)S(1)}, u32[]{:S(2)}, u32[]{:S(2)}) collective-permute-start(bf16[512,256]{1,0:T(8,128)(2,1)S(1)} %bitcast.64), channel_id=1, source_target_pairs={{0,4},{2,6},{4,0},{6,2},{1,5},{3,7},{5,1},{7,3},{8,12},{10,14},{12... | collective-permute-start | bytes 786440 | tf_op jit(solution)/shard_map/dispatch/ppermute | solution.py:21
  50.3 19.6 %collective-permute-start.2 = (bf16[512,256]{1,0:T(8,128)(2,1)S(1)}, bf16[512,256]{1,0:T(8,128)(2,1)S(1)}, u32[]{:S(2)}, u32[]{:S(2)}) collective-permute-start(bf16[512,256]{1,0:T(8,128)(2,1)S(1)} %bitcast.65), channel_id=1, source_target_pairs={{0,6},{2,0},{4,2},{6,4},{1,7},{3,1},{5,3},{7,5},{8,14},{10,8},{12,... | collective-permute-start | bytes 786440 | tf_op jit(solution)/shard_map/dispatch/ppermute | solution.py:21
  53.3 20.0 %collective-permute-start.1 = (bf16[512,256]{1,0:T(8,128)(2,1)S(1)}, bf16[512,256]{1,0:T(8,128)(2,1)S(1)}, u32[]{:S(2)}, u32[]{:S(2)}) collective-permute-start(bf16[512,256]{1,0:T(8,128)(2,1)S(1)} %bitcast.66), channel_id=1, source_target_pairs={{0,2},{2,4},{4,6},{6,0},{1,3},{3,5},{5,7},{7,1},{8,10},{10,12},{12... | collective-permute-start | bytes 786440 | tf_op jit(solution)/shard_map/dispatch/ppermute | solution.py:21
  62.5 13.4 %collective-permute-start.6 = (bf16[512,256]{1,0:T(8,128)(2,1)S(1)}, bf16[512,256]{1,0:T(8,128)(2,1)S(1)}, u32[]{:S(2)}, u32[]{:S(2)}) collective-permute-start(bf16[512,256]{1,0:T(8,128)(2,1)S(1)} %collective-permute-done), channel_id=1, source_target_pairs={{0,1},{1,0},{2,3},{3,2},{4,5},{5,4},{6,7},{7,6},{8,9},{9,8},{10,11... | collective-permute-start | bytes 786440 | tf_op jit(solution)/shard_map/dispatch/ppermute | solution.py:25
  70.0 7.1 %collective-permute-start.4 = (bf16[512,256]{1,0:T(8,128)(2,1)S(1)}, bf16[512,256]{1,0:T(8,128)(2,1)S(1)}, u32[]{:S(2)}, u32[]{:S(2)}) collective-permute-start(bf16[512,256]{1,0:T(8,128)(2,1)S(1)} %collective-permute-done.2), channel_id=1, source_target_pairs={{0,1},{1,0},{2,3},{3,2},{4,5},{5,4},{6,7},{7,6},{8,9},{9,8},{10,11... | collective-permute-start | bytes 786440 | tf_op jit(solution)/shard_map/dispatch/ppermute | solution.py:25
  73.3 3.4 %collective-permute-start.5 = (bf16[512,256]{1,0:T(8,128)(2,1)S(1)}, bf16[512,256]{1,0:T(8,128)(2,1)S(1)}, u32[]{:S(2)}, u32[]{:S(2)}) collective-permute-start(bf16[512,256]{1,0:T(8,128)(2,1)S(1)} %collective-permute-done.1), channel_id=1, source_target_pairs={{0,1},{1,0},{2,3},{3,2},{4,5},{5,4},{6,7},{7,6},{8,9},{9,8},{10,11... | collective-permute-start | bytes 786440 | tf_op jit(solution)/shard_map/dispatch/ppermute | solution.py:25
  77.0 0.9 copy-start.5
  77.0 0.9 copy-start.6
  77.4 5.6 %copy-start.4 = (bf16[192,2048]{1,0:T(8,128)(2,1)S(1)}, bf16[192,2048]{1,0:T(8,128)(2,1)}, u32[]{:S(2)}) copy-start(bf16[192,2048]{1,0:T(8,128)(2,1)} %param.11) | copy-start | bytes 2359300
  78.4 4.6 %collective-permute-start.7 = (bf16[512,1024]{1,0:T(8,128)(2,1)S(1)}, bf16[512,1024]{1,0:T(8,128)(2,1)S(1)}, u32[]{:S(2)}, u32[]{:S(2)}) collective-permute-start(bf16[512,1024]{1,0:T(8,128)(2,1)S(1)} %convolution_convert_fusion), channel_id=1, source_target_pairs={{0,1},{1,0},{2,3},{3,2},{4,5},{5,4},{6,7},{7,6},{8,9},{9,8},{10,11... | collective-permute-start | bytes 3145736 | tf_op jit(solution)/shard_map/combine/ppermute | solution.py:25
  83.3 22.7 %collective-permute-start.8 = (bf16[512,256]{1,0:T(8,128)(2,1)S(1)}, bf16[512,256]{1,0:T(8,128)(2,1)S(1)}, u32[]{:S(2)}, u32[]{:S(2)}) collective-permute-start(bf16[512,256]{1,0:T(8,128)(2,1)S(1)} %add_convert_fusion.3), channel_id=1, source_target_pairs={{0,4},{2,6},{4,0},{6,2},{1,5},{3,7},{5,1},{7,3},{8,12},{10,14},{12... | collective-permute-start | bytes 786440 | tf_op jit(solution)/shard_map/combine/ppermute | solution.py:21
  88.6 17.4 %collective-permute-start.9 = (bf16[512,256]{1,0:T(8,128)(2,1)S(1)}, bf16[512,256]{1,0:T(8,128)(2,1)S(1)}, u32[]{:S(2)}, u32[]{:S(2)}) collective-permute-start(bf16[512,256]{1,0:T(8,128)(2,1)S(1)} %add_convert_fusion.2), channel_id=1, source_target_pairs={{0,2},{2,4},{4,6},{6,0},{1,3},{3,5},{5,7},{7,1},{8,10},{10,12},{12... | collective-permute-start | bytes 786440 | tf_op jit(solution)/shard_map/combine/ppermute | solution.py:21
  91.4 24.0 %copy-start.8 = (bf16[256,8]{0,1:T(8,128)(2,1)S(1)}, bf16[256,8]{0,1:T(8,128)(2,1)}, u32[]{:S(2)}) copy-start(bf16[256,8]{0,1:T(8,128)(2,1)} %param.8) | copy-start | bytes 12292
  91.4 24.0 %copy-start.7 = (s32[256,8]{0,1:T(8,128)S(1)}, s32[256,8]{0,1:T(8,128)}, u32[]{:S(2)}) copy-start(s32[256,8]{0,1:T(8,128)} %param.7) | copy-start | bytes 24580
  91.4 17.6 %collective-permute-start.10 = (bf16[512,256]{1,0:T(8,128)(2,1)S(1)}, bf16[512,256]{1,0:T(8,128)(2,1)S(1)}, u32[]{:S(2)}, u32[]{:S(2)}) collective-permute-start(bf16[512,256]{1,0:T(8,128)(2,1)S(1)} %add_convert_fusion.1), channel_id=1, source_target_pairs={{0,6},{2,0},{4,2},{6,4},{1,7},{3,1},{5,3},{7,5},{8,14},{10,8},{12,... | collective-permute-start | bytes 786440 | tf_op jit(solution)/shard_map/combine/ppermute | solution.py:21
  109.9 18.3 %all-to-all-start.1 = ((bf16[16,32,256]{2,1,0:T(8,128)(2,1)}), bf16[16,32,256]{2,1,0:T(8,128)(2,1)S(1)}, u32[]{:S(2)}, u32[]{:S(2)}) async-start(bf16[16,32,256]{2,1,0:T(8,128)(2,1)} %bitcast.4), calls=%async_computation.1 | async-start | bytes 524288 | tf_op jit(solution)/shard_map/combine/all_to_all | solution.py:68
  139.4 9.6 %collective-permute-start.11 = (bf16[256,256]{1,0:T(8,128)(2,1)S(1)}, bf16[256,256]{1,0:T(8,128)(2,1)S(1)}, u32[]{:S(2)}, u32[]{:S(2)}) collective-permute-start(bf16[256,256]{1,0:T(8,128)(2,1)S(1)} %reduce_sum.31), channel_id=1, source_target_pairs={{0,8},{8,0},{1,9},{9,1},{2,10},{10,2},{3,11},{11,3},{4,12},{12,4},... | collective-permute-start | bytes 393224 | tf_op jit(solution)/shard_map/combine/ppermute | solution.py:29
  150.0 40.3 %all-to-all-start.3 = ((bf16[16,32,256]{2,1,0:T(8,128)(2,1)}), bf16[16,32,256]{2,1,0:T(8,128)(2,1)S(1)}, u32[]{:S(2)}, u32[]{:S(2)}) async-start(bf16[16,32,256]{2,1,0:T(8,128)(2,1)} %bitcast.6), calls=%async_computation.3 | async-start | bytes 524288 | tf_op jit(solution)/shard_map/curvature/all_to_all | solution.py:68
  161.9 20.6 %collective-permute-start.12 = (bf16[256,256]{1,0:T(8,128)(2,1)S(1)}, bf16[256,256]{1,0:T(8,128)(2,1)S(1)}, u32[]{:S(2)}, u32[]{:S(2)}) collective-permute-start(bf16[256,256]{1,0:T(8,128)(2,1)S(1)} %add_convert_fusion.5), channel_id=1, source_target_pairs={{0,4},{2,6},{4,0},{6,2},{1,5},{3,7},{5,1},{7,3},{8,12},{10,14},{12... | collective-permute-start | bytes 393224 | tf_op jit(solution)/shard_map/tangent/ppermute | solution.py:21
  170.1 14.4 %collective-permute-start.13 = (bf16[256,256]{1,0:T(8,128)(2,1)S(1)}, bf16[256,256]{1,0:T(8,128)(2,1)S(1)}, u32[]{:S(2)}, u32[]{:S(2)}) collective-permute-start(bf16[256,256]{1,0:T(8,128)(2,1)S(1)} %add_convert_fusion.5), channel_id=1, source_target_pairs={{0,2},{2,4},{4,6},{6,0},{1,3},{3,5},{5,7},{7,1},{8,10},{10,12},{12... | collective-permute-start | bytes 393224 | tf_op jit(solution)/shard_map/tangent/ppermute | solution.py:21
  172.1 14.9 %collective-permute-start.14 = (bf16[256,256]{1,0:T(8,128)(2,1)S(1)}, bf16[256,256]{1,0:T(8,128)(2,1)S(1)}, u32[]{:S(2)}, u32[]{:S(2)}) collective-permute-start(bf16[256,256]{1,0:T(8,128)(2,1)S(1)} %add_convert_fusion.5), channel_id=1, source_target_pairs={{0,6},{2,0},{4,2},{6,4},{1,7},{3,1},{5,3},{7,5},{8,14},{10,8},{12,... | collective-permute-start | bytes 393224 | tf_op jit(solution)/shard_map/tangent/ppermute | solution.py:21
  177.2 11.7 %collective-permute-start.15 = (bf16[256,256]{1,0:T(8,128)(2,1)S(1)}, bf16[256,256]{1,0:T(8,128)(2,1)S(1)}, u32[]{:S(2)}, u32[]{:S(2)}) collective-permute-start(bf16[256,256]{1,0:T(8,128)(2,1)S(1)} %add_convert_fusion.5), channel_id=1, source_target_pairs={{0,1},{1,0},{2,3},{3,2},{4,5},{5,4},{6,7},{7,6},{8,9},{9,8},{10,11... | collective-permute-start | bytes 393224 | tf_op jit(solution)/shard_map/tangent/ppermute | solution.py:25
  182.6 9.6 %collective-permute-start.18 = (bf16[256,256]{1,0:T(8,128)(2,1)S(1)}, bf16[256,256]{1,0:T(8,128)(2,1)S(1)}, u32[]{:S(2)}, u32[]{:S(2)}) collective-permute-start(bf16[256,256]{1,0:T(8,128)(2,1)S(1)} %collective-permute-done.12), channel_id=1, source_target_pairs={{0,1},{1,0},{2,3},{3,2},{4,5},{5,4},{6,7},{7,6},{8,9},{9,8},{10,11... | collective-permute-start | bytes 393224 | tf_op jit(solution)/shard_map/tangent/ppermute | solution.py:25
  184.5 5.7 %collective-permute-start.17 = (bf16[256,256]{1,0:T(8,128)(2,1)S(1)}, bf16[256,256]{1,0:T(8,128)(2,1)S(1)}, u32[]{:S(2)}, u32[]{:S(2)}) collective-permute-start(bf16[256,256]{1,0:T(8,128)(2,1)S(1)} %collective-permute-done.13), channel_id=1, source_target_pairs={{0,1},{1,0},{2,3},{3,2},{4,5},{5,4},{6,7},{7,6},{8,9},{9,8},{10,11... | collective-permute-start | bytes 393224 | tf_op jit(solution)/shard_map/tangent/ppermute | solution.py:25
  187.0 3.2 %collective-permute-start.16 = (bf16[256,256]{1,0:T(8,128)(2,1)S(1)}, bf16[256,256]{1,0:T(8,128)(2,1)S(1)}, u32[]{:S(2)}, u32[]{:S(2)}) collective-permute-start(bf16[256,256]{1,0:T(8,128)(2,1)S(1)} %collective-permute-done.14), channel_id=1, source_target_pairs={{0,1},{1,0},{2,3},{3,2},{4,5},{5,4},{6,7},{7,6},{8,9},{9,8},{10,11... | collective-permute-start | bytes 393224 | tf_op jit(solution)/shard_map/tangent/ppermute | solution.py:25
  190.3 20.0 %collective-permute-start.19 = (bf16[512,256]{1,0:T(8,128)(2,1)S(1)}, bf16[512,256]{1,0:T(8,128)(2,1)S(1)}, u32[]{:S(2)}, u32[]{:S(2)}) collective-permute-start(bf16[512,256]{1,0:T(8,128)(2,1)S(1)} %bitcast.58), channel_id=1, source_target_pairs={{0,4},{2,6},{4,0},{6,2},{1,5},{3,7},{5,1},{7,3},{8,12},{10,14},{12... | collective-permute-start | bytes 786440 | tf_op jit(solution)/shard_map/curvature/ppermute | solution.py:21
  192.3 26.4 %copy-start.1 = (bf16[256,2048]{1,0:T(8,128)(2,1)}, bf16[256,2048]{1,0:T(8,128)(2,1)S(1)}, u32[]{:S(2)}) copy-start(bf16[256,2048]{1,0:T(8,128)(2,1)S(1)} %constant_dynamic-update-slice_fusion) | copy-start | bytes 3145732
  192.3 20.7 %collective-permute-start.20 = (bf16[512,256]{1,0:T(8,128)(2,1)S(1)}, bf16[512,256]{1,0:T(8,128)(2,1)S(1)}, u32[]{:S(2)}, u32[]{:S(2)}) collective-permute-start(bf16[512,256]{1,0:T(8,128)(2,1)S(1)} %bitcast.59), channel_id=1, source_target_pairs={{0,2},{2,4},{4,6},{6,0},{1,3},{3,5},{5,7},{7,1},{8,10},{10,12},{12... | collective-permute-start | bytes 786440 | tf_op jit(solution)/shard_map/curvature/ppermute | solution.py:21
  194.2 21.6 %collective-permute-start.21 = (bf16[512,256]{1,0:T(8,128)(2,1)S(1)}, bf16[512,256]{1,0:T(8,128)(2,1)S(1)}, u32[]{:S(2)}, u32[]{:S(2)}) collective-permute-start(bf16[512,256]{1,0:T(8,128)(2,1)S(1)} %bitcast.60), channel_id=1, source_target_pairs={{0,6},{2,0},{4,2},{6,4},{1,7},{3,1},{5,3},{7,5},{8,14},{10,8},{12,... | collective-permute-start | bytes 786440 | tf_op jit(solution)/shard_map/curvature/ppermute | solution.py:21
  199.4 19.1 %collective-permute-start.22 = (bf16[512,256]{1,0:T(8,128)(2,1)S(1)}, bf16[512,256]{1,0:T(8,128)(2,1)S(1)}, u32[]{:S(2)}, u32[]{:S(2)}) collective-permute-start(bf16[512,256]{1,0:T(8,128)(2,1)S(1)} %bitcast.61), channel_id=1, source_target_pairs={{0,1},{1,0},{2,3},{3,2},{4,5},{5,4},{6,7},{7,6},{8,9},{9,8},{10,11... | collective-permute-start | bytes 786440 | tf_op jit(solution)/shard_map/curvature/ppermute | solution.py:25
  210.3 9.5 %collective-permute-start.25 = (bf16[512,256]{1,0:T(8,128)(2,1)S(1)}, bf16[512,256]{1,0:T(8,128)(2,1)S(1)}, u32[]{:S(2)}, u32[]{:S(2)}) collective-permute-start(bf16[512,256]{1,0:T(8,128)(2,1)S(1)} %collective-permute-done.19), channel_id=1, source_target_pairs={{0,1},{1,0},{2,3},{3,2},{4,5},{5,4},{6,7},{7,6},{8,9},{9,8},{10,11... | collective-permute-start | bytes 786440 | tf_op jit(solution)/shard_map/curvature/ppermute | solution.py:25
  212.9 6.6 %collective-permute-start.24 = (bf16[512,256]{1,0:T(8,128)(2,1)S(1)}, bf16[512,256]{1,0:T(8,128)(2,1)S(1)}, u32[]{:S(2)}, u32[]{:S(2)}) collective-permute-start(bf16[512,256]{1,0:T(8,128)(2,1)S(1)} %collective-permute-done.20), channel_id=1, source_target_pairs={{0,1},{1,0},{2,3},{3,2},{4,5},{5,4},{6,7},{7,6},{8,9},{9,8},{10,11... | collective-permute-start | bytes 786440 | tf_op jit(solution)/shard_map/curvature/ppermute | solution.py:25
  215.8 3.5 %collective-permute-start.23 = (bf16[512,256]{1,0:T(8,128)(2,1)S(1)}, bf16[512,256]{1,0:T(8,128)(2,1)S(1)}, u32[]{:S(2)}, u32[]{:S(2)}) collective-permute-start(bf16[512,256]{1,0:T(8,128)(2,1)S(1)} %collective-permute-done.21), channel_id=1, source_target_pairs={{0,1},{1,0},{2,3},{3,2},{4,5},{5,4},{6,7},{7,6},{8,9},{9,8},{10,11... | collective-permute-start | bytes 786440 | tf_op jit(solution)/shard_map/curvature/ppermute | solution.py:25
  220.0 0.9 copy-start.3

commit v5 on v4

--- a/solution.py
+++ b/solution.py
@@ -8,7 +8,7 @@
 CORES = 2
 LINE = 4
 HALVES = 2
-STEPS = (2, 1, 3)
+MASKS = (1, 2, 3)
 
 
 def contract_rows(left, right):
@@ -17,8 +17,8 @@
     )
 
 
-def shift_line(value, step):
-    return lax.ppermute(value, "line", [(i, (i + step) % LINE) for i in range(LINE)])
+def swap_line(value, mask):
+    return lax.ppermute(value, "line", [(i, i ^ mask) for i in range(LINE)])
 
 
 def swap_cores(value):
@@ -41,13 +41,11 @@
     line_index = lax.axis_index("line")
     core_index = lax.axis_index("core")
 
-    def first_col(step, other):
-        line = (line_index + step) & (LINE - 1)
-        core = core_index ^ other
-        return (line * CORES + core) * cols
+    def first_col(mask, other):
+        return ((line_index ^ mask) * CORES + (core_index ^ other)) * cols
 
-    def columns(weight, step, other):
-        return lax.dynamic_slice_in_dim(weight, first_col(step, other), cols, 1)
+    def columns(weight, mask, other):
+        return lax.dynamic_slice_in_dim(weight, first_col(mask, other), cols, 1)
 
     with jax.named_scope("routing"):
         owner_ids = jnp.arange(n_expert, dtype=jnp.int32) * EXP_COL + local_index
@@ -70,26 +68,32 @@
         )
         return moved.reshape(rows, cols)
 
-    def gather_blocks(block):
-        blocks = {(0, 0): block}
-        for step in STEPS:
-            blocks[(LINE - step, 0)] = shift_line(block, step)
-        for step in (0, 1, 3, 2):
-            blocks[(step, 1)] = swap_cores(blocks[(step, 0)])
-        return blocks
+    def with_cores(pieces):
+        crossed = swap_cores(jnp.concatenate(pieces)).reshape(LINE, *pieces[0].shape)
+        return {
+            (mask, other): (pieces[mask], crossed[mask])[other]
+            for other in range(CORES)
+            for mask in range(LINE)
+        }
+
+    def gather_line(block):
+        return [block, *(swap_line(block, mask) for mask in MASKS)]
 
     with jax.named_scope("dispatch"):
         own_cols = columns(tokens, 0, 0)
         outgoing = jnp.dot(select, own_cols, preferred_element_type=jnp.float32)
-        row_blocks = gather_blocks(over_planes(outgoing.astype(jnp.bfloat16)))
+        arrived = over_planes(outgoing.astype(jnp.bfloat16))
+        other_cols = jnp.concatenate([columns(direction, mask, 1) for mask in range(LINE)], axis=1)
+        both = jnp.concatenate([gate_weight, up_weight], axis=0)
+        arrived, other_cols, both = lax.optimization_barrier((arrived, other_cols, both))
+        row_blocks = with_cores(gather_line(arrived))
 
     with jax.named_scope("experts"):
-        both = jnp.concatenate([gate_weight, up_weight], axis=0)
         value = 0.0
-        for (step, other), block in row_blocks.items():
+        for (mask, other), block in row_blocks.items():
             value += lax.dot_general(
                 block,
-                columns(both, step, other),
+                columns(both, mask, other),
                 (((1,), (1,)), ((), ())),
                 preferred_element_type=jnp.float32,
             )
@@ -97,19 +101,18 @@
         hidden = hidden.astype(jnp.bfloat16)
 
     with jax.named_scope("combine"):
-        other_cols = jnp.concatenate([columns(direction, step, 1) for step in range(LINE)], axis=1)
         crossed = swap_cores(
             jnp.dot(hidden, other_cols, preferred_element_type=jnp.float32).astype(jnp.bfloat16)
         )
 
-        def pair_out(step):
+        def pair_out(mask):
             own = jnp.dot(
-                hidden, columns(direction, step, 0), preferred_element_type=jnp.float32
+                hidden, columns(direction, mask, 0), preferred_element_type=jnp.float32
             )
-            other = crossed[:, step * cols : (step + 1) * cols].astype(jnp.float32)
+            other = crossed[:, mask * cols : (mask + 1) * cols].astype(jnp.float32)
             return (own + other).astype(jnp.bfloat16)
 
-        arrived = [shift_line(pair_out(step), step).astype(jnp.float32) for step in STEPS]
+        arrived = [swap_line(pair_out(mask), mask).astype(jnp.float32) for mask in MASKS]
         expert_out = pair_out(0).astype(jnp.float32) + arrived[0] + arrived[1] + arrived[2]
         returned = over_planes(expert_out.astype(jnp.bfloat16))
         part = contract_rows(spread, returned).astype(jnp.bfloat16)
@@ -128,20 +131,25 @@
         moved = over_planes(scaled)
 
     with jax.named_scope("tangent"):
-        tangent_out = jnp.zeros((col_tok, width), jnp.bfloat16)
-        for (step, other), block in gather_blocks(tangent_late).items():
-            tangent_out = lax.dynamic_update_slice_in_dim(
-                tangent_out, block, first_col(step, other), 1
-            )
+        pieces = gather_line(tangent_late)
+        moved, *pieces = lax.optimization_barrier((moved, *pieces))
 
     with jax.named_scope("curvature"):
+        scaled_blocks = with_cores(gather_line(moved))
         curvature = jnp.zeros((unit_count, width), jnp.bfloat16)
-        for (step, other), block in gather_blocks(moved).items():
+        for (mask, other), block in scaled_blocks.items():
             curvature = lax.dynamic_update_slice_in_dim(
                 curvature,
                 contract_rows(hidden, block).astype(jnp.bfloat16),
-                first_col(step, other),
+                first_col(mask, other),
                 1,
+            )
+
+    with jax.named_scope("tangent"):
+        tangent_out = jnp.zeros((col_tok, width), jnp.bfloat16)
+        for (mask, other), block in with_cores(pieces).items():
+            tangent_out = lax.dynamic_update_slice_in_dim(
+                tangent_out, block, first_col(mask, other), 1
             )
     return tangent_out, curvature
 

time: 225 us -> 222 us (0.987)
  matrix products: 7.84 us -> 12.7 us
  starting transfers between devices: 129 us -> 125 us
  waiting for transfers between devices: 63.5 us -> 61 us
  local copies, waits for them, and re-layouts: 5.25 us -> 2.95 us
    dot_general x12, matrix products: 3.48 us -> 8.39 us  [the longest x8 7.28 us: shards(): lax.dot_general(block, columns(both, mask, other), (((1,), (1,)), ((), ()...]
    ppermute x13 -> x4, starting transfers between devices: 38.9 us -> 34.1 us  [swap_cores(): return lax.ppermute(value, 'core', [(i, i ^ 1) for i in range(CORES)])]
    all_to_all x3, starting transfers between devices: 36.9 us -> 40.4 us  [over_planes(): lax.all_to_all(slots.reshape(n_expert, slot_count, cols), 'expert', 0, 0,...]
    ppermute x12, waiting for transfers between devices: 32 us -> 29.5 us  [swap_line(): return lax.ppermute(value, 'line', [(i, i ^ mask) for i in range(LINE)])]
    ppermute x13 -> x4, waiting for transfers between devices: 5.04 us -> 4.45 us  [swap_cores(): return lax.ppermute(value, 'core', [(i, i ^ 1) for i in range(CORES)])]
  transfers between devices with their start and end apart: 29 -> 20, of which waited for: 13 -> 12; matrix products, arithmetic and copies ran while one was open for 4% -> 2% of each run, Pallas kernels for 0% -> 0%
where the time goes in v5:
time: 222 us; the launch traced here: 219 us
  starting transfers between devices  125 us (56%)
  waiting for transfers between devices  61 us (27%)
  matrix products  12.7 us (6%)
  blocking collectives  10.8 us (5%)
  other arithmetic  4.51 us (2%)
  local copies, waits for them, and re-layouts  2.95 us (1%)
    ppermute x12, starting transfers between devices, swap_line(): return lax.ppermute(value, 'line', [(i, i ^ mask) for i in range(LINE)])  44.3 us
    all_to_all x3, starting transfers between devices, over_planes(): lax.all_to_all(slots.reshape(n_expert, slot_count, cols), 'expert', 0, 0,...  40.4 us
    ppermute x4, starting transfers between devices, swap_cores(): return lax.ppermute(value, 'core', [(i, i ^ 1) for i in range(CORES)])  34.1 us
    ppermute x12, waiting for transfers between devices, swap_line(): return lax.ppermute(value, 'line', [(i, i ^ mask) for i in range(LINE)])  29.5 us
    all_to_all x3, waiting for transfers between devices, over_planes(): lax.all_to_all(slots.reshape(n_expert, slot_count, cols), 'expert', 0, 0,...  24.2 us
    all_to_all x1, blocking collectives, shards(): lax.all_to_all(jnp.broadcast_to(part, (EXP_COL // HALVES, col_tok, cols))...  10.8 us
    dot_general x8, matrix products, shards(): lax.dot_general(block, columns(both, mask, other), (((1,), (1,)), ((), ()...  7.28 us
    ppermute x1, starting transfers between devices, swap_halves(): return lax.ppermute(value, 'half', [(i, i ^ 1) for i in range(HALVES)])  6.55 us
  transfers between devices with their start and end apart: 20, of which 12 were waited for; matrix products, arithmetic and copies ran while one was open for 2% of the time, Pallas kernels for 0%

profile of v5, /device:TPU:1, one launch (start us, length us, event | category | flops | bytes accessed | tf_op | source)
XLA Modules:
  0.0 218.7 jit_solution(13426210163552892186)
XLA Ops:
  0.7 0.9 compare_reduce_fusion
  1.6 0.6 reduce-window.6
  2.8 0.9 convolution_convert_fusion.1
  3.7 19.4 %all-to-all-start = ((bf16[16,32,256]{2,1,0:T(8,128)(2,1)}), bf16[16,32,256]{2,1,0:T(8,128)(2,1)S(1)}, u32[]{:S(2)}, u32[]{:S(2)}) async-start(bf16[16,32,256]{2,1,0:T(8,128)(2,1)} %bitcast.2), calls=%async_computation | async-start | bytes 524288 | tf_op jit(solution)/shard_map/dispatch/all_to_all | solution.py:66
  23.4 1.0 copy-done.8
  24.7 11.6 %all-to-all-done = bf16[16,32,256]{2,1,0:T(8,128)(2,1)S(1)} async-done(((bf16[16,32,256]{2,1,0:T(8,128)(2,1)}), bf16[16,32,256]{2,1,0:T(8,128)(2,1)S(1)}, u32[]{:S(2)}, u32[]{:S(2)}) %all-to-all-start) | async-done | bytes 262176 | tf_op jit(solution)/shard_map/dispatch/all_to_all | solution.py:66
  36.3 3.2 %collective-permute-start = (bf16[512,256]{1,0:T(8,128)(2,1)S(1)}, bf16[512,256]{1,0:T(8,128)(2,1)S(1)}, u32[]{:S(2)}, u32[]{:S(2)}) collective-permute-start(bf16[512,256]{1,0:T(8,128)(2,1)S(1)} %bitcast.56), channel_id=1, source_target_pairs={{0,2},{2,0},{4,6},{6,4},{1,3},{3,1},{5,7},{7,5},{8,10},{10,8},{12,... | collective-permute-start | bytes 786440 | tf_op jit(solution)/shard_map/dispatch/ppermute | solution.py:21
  39.5 4.2 %collective-permute-start.1 = (bf16[512,256]{1,0:T(8,128)(2,1)S(1)}, bf16[512,256]{1,0:T(8,128)(2,1)S(1)}, u32[]{:S(2)}, u32[]{:S(2)}) collective-permute-start(bf16[512,256]{1,0:T(8,128)(2,1)S(1)} %bitcast.57), channel_id=1, source_target_pairs={{0,4},{2,6},{4,0},{6,2},{1,5},{3,7},{5,1},{7,3},{8,12},{10,14},{12... | collective-permute-start | bytes 786440 | tf_op jit(solution)/shard_map/dispatch/ppermute | solution.py:21
  43.7 1.9 collective-permute-start.2
  45.7 5.3 %collective-permute-done.1 = bf16[512,256]{1,0:T(8,128)(2,1)S(1)} collective-permute-done((bf16[512,256]{1,0:T(8,128)(2,1)S(1)}, bf16[512,256]{1,0:T(8,128)(2,1)S(1)}, u32[]{:S(2)}, u32[]{:S(2)}) %collective-permute-start.1) | collective-permute-done | bytes 262176 | tf_op jit(solution)/shard_map/dispatch/ppermute | solution.py:21
  51.0 4.4 %collective-permute-done.2 = bf16[512,256]{1,0:T(8,128)(2,1)S(1)} collective-permute-done((bf16[512,256]{1,0:T(8,128)(2,1)S(1)}, bf16[512,256]{1,0:T(8,128)(2,1)S(1)}, u32[]{:S(2)}, u32[]{:S(2)}) %collective-permute-start.2) | collective-permute-done | bytes 262176 | tf_op jit(solution)/shard_map/dispatch/ppermute | solution.py:21
  55.4 1.1 pad_maximum_fusion.1
  56.5 12.3 %collective-permute-start.3 = (bf16[2048,256]{1,0:T(8,128)(2,1)}, bf16[2048,256]{1,0:T(8,128)(2,1)}, u32[]{:S(2)}, u32[]{:S(2)}) collective-permute-start(bf16[2048,256]{1,0:T(8,128)(2,1)} %pad_maximum_fusion.1), channel_id=1, source_target_pairs={{0,1},{1,0},{2,3},{3,2},{4,5},{5,4},{6,7},{7,6},{8,9},{9,8},{10,11... | collective-permute-start | bytes 3145736 | tf_op jit(solution)/shard_map/dispatch/ppermute | solution.py:25
  69.1 1.2 fusion.38
  70.7 0.7 collective-permute-done.3
  71.4 1.2 fusion.28
  72.7 1.3 fusion.26
  74.0 1.2 fusion.24
  75.2 1.2 fusion.22
  76.5 0.4 fusion.4
  77.0 0.5 convolution_convert_fusion
  77.5 2.3 %collective-permute-start.4 = (bf16[512,1024]{1,0:T(8,128)(2,1)S(1)}, bf16[512,1024]{1,0:T(8,128)(2,1)S(1)}, u32[]{:S(2)}, u32[]{:S(2)}) collective-permute-start(bf16[512,1024]{1,0:T(8,128)(2,1)S(1)} %convolution_convert_fusion), channel_id=1, source_target_pairs={{0,1},{1,0},{2,3},{3,2},{4,5},{5,4},{6,7},{7,6},{8,9},{9,8},{10,11... | collective-permute-start | bytes 3145736 | tf_op jit(solution)/shard_map/combine/ppermute | solution.py:25
  79.8 2.3 %collective-permute-done.4 = bf16[512,1024]{1,0:T(8,128)(2,1)S(1)} collective-permute-done((bf16[512,1024]{1,0:T(8,128)(2,1)S(1)}, bf16[512,1024]{1,0:T(8,128)(2,1)S(1)}, u32[]{:S(2)}, u32[]{:S(2)}) %collective-permute-start.4) | collective-permute-done | bytes 1048608 | tf_op jit(solution)/shard_map/combine/ppermute | solution.py:25
  82.3 4.3 %collective-permute-start.5 = (bf16[512,256]{1,0:T(8,128)(2,1)S(1)}, bf16[512,256]{1,0:T(8,128)(2,1)S(1)}, u32[]{:S(2)}, u32[]{:S(2)}) collective-permute-start(bf16[512,256]{1,0:T(8,128)(2,1)S(1)} %add_convert_fusion.3), channel_id=1, source_target_pairs={{0,2},{2,0},{4,6},{6,4},{1,3},{3,1},{5,7},{7,5},{8,10},{10,8},{12,... | collective-permute-start | bytes 786440 | tf_op jit(solution)/shard_map/combine/ppermute | solution.py:21
  86.9 2.9 %collective-permute-start.6 = (bf16[512,256]{1,0:T(8,128)(2,1)S(1)}, bf16[512,256]{1,0:T(8,128)(2,1)S(1)}, u32[]{:S(2)}, u32[]{:S(2)}) collective-permute-start(bf16[512,256]{1,0:T(8,128)(2,1)S(1)} %add_convert_fusion.2), channel_id=1, source_target_pairs={{0,4},{2,6},{4,0},{6,2},{1,5},{3,7},{5,1},{7,3},{8,12},{10,14},{12... | collective-permute-start | bytes 786440 | tf_op jit(solution)/shard_map/combine/ppermute | solution.py:21
  90.2 3.1 %collective-permute-start.7 = (bf16[512,256]{1,0:T(8,128)(2,1)S(1)}, bf16[512,256]{1,0:T(8,128)(2,1)S(1)}, u32[]{:S(2)}, u32[]{:S(2)}) collective-permute-start(bf16[512,256]{1,0:T(8,128)(2,1)S(1)} %add_convert_fusion.1), channel_id=1, source_target_pairs={{0,6},{2,4},{4,2},{6,0},{1,7},{3,5},{5,3},{7,1},{8,14},{10,12},{12... | collective-permute-start | bytes 786440 | tf_op jit(solution)/shard_map/combine/ppermute | solution.py:21
  93.6 2.4 %collective-permute-done.5 = bf16[512,256]{1,0:T(8,128)(2,1)S(1)} collective-permute-done((bf16[512,256]{1,0:T(8,128)(2,1)S(1)}, bf16[512,256]{1,0:T(8,128)(2,1)S(1)}, u32[]{:S(2)}, u32[]{:S(2)}) %collective-permute-start.5) | collective-permute-done | bytes 262176 | tf_op jit(solution)/shard_map/combine/ppermute | solution.py:21
  96.0 12.3 %collective-permute-done.6 = bf16[512,256]{1,0:T(8,128)(2,1)S(1)} collective-permute-done((bf16[512,256]{1,0:T(8,128)(2,1)S(1)}, bf16[512,256]{1,0:T(8,128)(2,1)S(1)}, u32[]{:S(2)}, u32[]{:S(2)}) %collective-permute-start.6) | collective-permute-done | bytes 262176 | tf_op jit(solution)/shard_map/combine/ppermute | solution.py:21
  108.3 0.9 add_convert_fusion
  109.1 10.9 %all-to-all-start.1 = ((bf16[16,32,256]{2,1,0:T(8,128)(2,1)}), bf16[16,32,256]{2,1,0:T(8,128)(2,1)S(1)}, u32[]{:S(2)}, u32[]{:S(2)}) async-start(bf16[16,32,256]{2,1,0:T(8,128)(2,1)} %bitcast.4), calls=%async_computation.1 | async-start | bytes 524288 | tf_op jit(solution)/shard_map/combine/all_to_all | solution.py:66
  120.2 12.6 %all-to-all-done.1 = bf16[16,32,256]{2,1,0:T(8,128)(2,1)S(1)} async-done(((bf16[16,32,256]{2,1,0:T(8,128)(2,1)}), bf16[16,32,256]{2,1,0:T(8,128)(2,1)S(1)}, u32[]{:S(2)}, u32[]{:S(2)}) %all-to-all-start.1) | async-done | bytes 262176 | tf_op jit(solution)/shard_map/combine/all_to_all | solution.py:66
  133.2 10.8 %all_to_all.20 = bf16[4,256,256]{2,1,0:T(8,128)(2,1)S(1)} all-to-all(bf16[4,256,256]{2,1,0:T(8,128)(2,1)S(1)} %broadcast_in_dim.45), channel_id=1, replica_groups=mesh['expert'=16,'x'=4,'half'=2,'line'=4,'core'=2] {'x'}, dimensions={0} | all-to-all | bytes 1048576 | tf_op jit(solution)/shard_map/combine/all_to_all | solution.py:119
  144.0 6.5 %collective-permute-start.8 = (bf16[256,256]{1,0:T(8,128)(2,1)S(1)}, bf16[256,256]{1,0:T(8,128)(2,1)S(1)}, u32[]{:S(2)}, u32[]{:S(2)}) collective-permute-start(bf16[256,256]{1,0:T(8,128)(2,1)S(1)} %reduce_sum.31), channel_id=1, source_target_pairs={{0,8},{8,0},{1,9},{9,1},{2,10},{10,2},{3,11},{11,3},{4,12},{12,4},... | collective-permute-start | bytes 393224 | tf_op jit(solution)/shard_map/combine/ppermute | solution.py:29
  150.9 2.8 %collective-permute-done.8 = bf16[256,256]{1,0:T(8,128)(2,1)S(1)} collective-permute-done((bf16[256,256]{1,0:T(8,128)(2,1)S(1)}, bf16[256,256]{1,0:T(8,128)(2,1)S(1)}, u32[]{:S(2)}, u32[]{:S(2)}) %collective-permute-start.8) | collective-permute-done | bytes 131104 | tf_op jit(solution)/shard_map/combine/ppermute | solution.py:29
  153.7 0.9 fusion.5
  154.6 10.0 %all-to-all-start.3 = ((bf16[16,32,256]{2,1,0:T(8,128)(2,1)}), bf16[16,32,256]{2,1,0:T(8,128)(2,1)S(1)}, u32[]{:S(2)}, u32[]{:S(2)}) async-start(bf16[16,32,256]{2,1,0:T(8,128)(2,1)} %bitcast.6), calls=%async_computation.3 | async-start | bytes 524288 | tf_op jit(solution)/shard_map/curvature/all_to_all | solution.py:66
  164.6 10.4 %collective-permute-start.10 = (bf16[256,256]{1,0:T(8,128)(2,1)S(1)}, bf16[256,256]{1,0:T(8,128)(2,1)S(1)}, u32[]{:S(2)}, u32[]{:S(2)}) collective-permute-start(bf16[256,256]{1,0:T(8,128)(2,1)S(1)} %add_convert_fusion.5), channel_id=1, source_target_pairs={{0,4},{2,6},{4,0},{6,2},{1,5},{3,7},{5,1},{7,3},{8,12},{10,14},{12... | collective-permute-start | bytes 393224 | tf_op jit(solution)/shard_map/tangent/ppermute | solution.py:21
  175.1 3.0 %collective-permute-start.11 = (bf16[256,256]{1,0:T(8,128)(2,1)S(1)}, bf16[256,256]{1,0:T(8,128)(2,1)S(1)}, u32[]{:S(2)}, u32[]{:S(2)}) collective-permute-start(bf16[256,256]{1,0:T(8,128)(2,1)S(1)} %add_convert_fusion.5), channel_id=1, source_target_pairs={{0,6},{2,4},{4,2},{6,0},{1,7},{3,5},{5,3},{7,1},{8,14},{10,12},{12... | collective-permute-start | bytes 393224 | tf_op jit(solution)/shard_map/tangent/ppermute | solution.py:21
  178.1 1.9 collective-permute-start.9
  180.0 4.0 %collective-permute-done.11 = bf16[256,256]{1,0:T(8,128)(2,1)S(1)} collective-permute-done((bf16[256,256]{1,0:T(8,128)(2,1)S(1)}, bf16[256,256]{1,0:T(8,128)(2,1)S(1)}, u32[]{:S(2)}, u32[]{:S(2)}) %collective-permute-start.11) | collective-permute-done | bytes 131104 | tf_op jit(solution)/shard_map/tangent/ppermute | solution.py:21
  184.0 1.1 collective-permute-done.9
  185.1 1.9 collective-permute-start.13
  187.1 4.0 %collective-permute-start.14 = (bf16[512,256]{1,0:T(8,128)(2,1)S(1)}, bf16[512,256]{1,0:T(8,128)(2,1)S(1)}, u32[]{:S(2)}, u32[]{:S(2)}) collective-permute-start(bf16[512,256]{1,0:T(8,128)(2,1)S(1)} %bitcast.52), channel_id=1, source_target_pairs={{0,4},{2,6},{4,0},{6,2},{1,5},{3,7},{5,1},{7,3},{8,12},{10,14},{12... | collective-permute-start | bytes 786440 | tf_op jit(solution)/shard_map/curvature/ppermute | solution.py:21
  191.1 3.3 %collective-permute-start.15 = (bf16[512,256]{1,0:T(8,128)(2,1)S(1)}, bf16[512,256]{1,0:T(8,128)(2,1)S(1)}, u32[]{:S(2)}, u32[]{:S(2)}) collective-permute-start(bf16[512,256]{1,0:T(8,128)(2,1)S(1)} %bitcast.53), channel_id=1, source_target_pairs={{0,6},{2,4},{4,2},{6,0},{1,7},{3,5},{5,3},{7,1},{8,14},{10,12},{12... | collective-permute-start | bytes 786440 | tf_op jit(solution)/shard_map/curvature/ppermute | solution.py:21
  194.5 8.1 %collective-permute-start.12 = (bf16[1024,256]{1,0:T(8,128)(2,1)S(1)}, bf16[1024,256]{1,0:T(8,128)(2,1)S(1)}, u32[]{:S(2)}, u32[]{:S(2)}) collective-permute-start(bf16[1024,256]{1,0:T(8,128)(2,1)S(1)} %pad_maximum_fusion.3), channel_id=1, source_target_pairs={{0,1},{1,0},{2,3},{3,2},{4,5},{5,4},{6,7},{7,6},{8,9},{9,8},{10,11... | collective-permute-start | bytes 1572872 | tf_op jit(solution)/shard_map/tangent/ppermute | solution.py:25
  203.2 11.4 %collective-permute-start.16 = (bf16[2048,256]{1,0:T(8,128)(2,1)S(1)}, bf16[2048,256]{1,0:T(8,128)(2,1)S(1)}, u32[]{:S(2)}, u32[]{:S(2)}) collective-permute-start(bf16[2048,256]{1,0:T(8,128)(2,1)S(1)} %pad_maximum_fusion.2), channel_id=1, source_target_pairs={{0,1},{1,0},{2,3},{3,2},{4,5},{5,4},{6,7},{7,6},{8,9},{9,8},{10,11... | collective-permute-start | bytes 3145736 | tf_op jit(solution)/shard_map/curvature/ppermute | solution.py:25
  215.4 1.5 collective-permute-done.16
  217.8 0.9 copy-done.7
  (81 shorter events, 5.9 us)
Async XLA Ops:
  0.6 2.2 copy-start
  0.6 22.6 %copy-start.10 = (bf16[192,2048]{1,0:T(8,128)(2,1)S(1)}, bf16[192,2048]{1,0:T(8,128)(2,1)}, u32[]{:S(2)}) copy-start(bf16[192,2048]{1,0:T(8,128)(2,1)} %param.11) | copy-start | bytes 2359300
  3.7 32.6 %all-to-all-start = ((bf16[16,32,256]{2,1,0:T(8,128)(2,1)}), bf16[16,32,256]{2,1,0:T(8,128)(2,1)S(1)}, u32[]{:S(2)}, u32[]{:S(2)}) async-start(bf16[16,32,256]{2,1,0:T(8,128)(2,1)} %bitcast.2), calls=%async_computation | async-start | bytes 524288 | tf_op jit(solution)/shard_map/dispatch/all_to_all | solution.py:66
  23.2 1.1 copy-start.8
  23.2 1.4 copy-start.9
  36.3 9.4 %collective-permute-start = (bf16[512,256]{1,0:T(8,128)(2,1)S(1)}, bf16[512,256]{1,0:T(8,128)(2,1)S(1)}, u32[]{:S(2)}, u32[]{:S(2)}) collective-permute-start(bf16[512,256]{1,0:T(8,128)(2,1)S(1)} %bitcast.56), channel_id=1, source_target_pairs={{0,2},{2,0},{4,6},{6,4},{1,3},{3,1},{5,7},{7,5},{8,10},{10,8},{12,... | collective-permute-start | bytes 786440 | tf_op jit(solution)/shard_map/dispatch/ppermute | solution.py:21
  39.5 11.5 %collective-permute-start.1 = (bf16[512,256]{1,0:T(8,128)(2,1)S(1)}, bf16[512,256]{1,0:T(8,128)(2,1)S(1)}, u32[]{:S(2)}, u32[]{:S(2)}) collective-permute-start(bf16[512,256]{1,0:T(8,128)(2,1)S(1)} %bitcast.57), channel_id=1, source_target_pairs={{0,4},{2,6},{4,0},{6,2},{1,5},{3,7},{5,1},{7,3},{8,12},{10,14},{12... | collective-permute-start | bytes 786440 | tf_op jit(solution)/shard_map/dispatch/ppermute | solution.py:21
  43.7 11.7 %collective-permute-start.2 = (bf16[512,256]{1,0:T(8,128)(2,1)S(1)}, bf16[512,256]{1,0:T(8,128)(2,1)S(1)}, u32[]{:S(2)}, u32[]{:S(2)}) collective-permute-start(bf16[512,256]{1,0:T(8,128)(2,1)S(1)} %bitcast.58), channel_id=1, source_target_pairs={{0,6},{2,4},{4,2},{6,0},{1,7},{3,5},{5,3},{7,1},{8,14},{10,12},{12... | collective-permute-start | bytes 786440 | tf_op jit(solution)/shard_map/dispatch/ppermute | solution.py:21
  45.7 10.8 %copy-start.4 = (bf16[512,256]{1,0:T(8,128)(2,1)}, bf16[512,256]{1,0:T(8,128)(2,1)S(1)}, u32[]{:S(2)}) copy-start(bf16[512,256]{1,0:T(8,128)(2,1)S(1)} %collective-permute-done) | copy-start | bytes 786436
  51.0 4.4 %copy-start.2 = (bf16[512,256]{1,0:T(8,128)(2,1)}, bf16[512,256]{1,0:T(8,128)(2,1)S(1)}, u32[]{:S(2)}) copy-start(bf16[512,256]{1,0:T(8,128)(2,1)S(1)} %collective-permute-done.1) | copy-start | bytes 786436
  55.4 1.1 copy-start.6
  56.5 14.9 %collective-permute-start.3 = (bf16[2048,256]{1,0:T(8,128)(2,1)}, bf16[2048,256]{1,0:T(8,128)(2,1)}, u32[]{:S(2)}, u32[]{:S(2)}) collective-permute-start(bf16[2048,256]{1,0:T(8,128)(2,1)} %pad_maximum_fusion.1), channel_id=1, source_target_pairs={{0,1},{1,0},{2,3},{3,2},{4,5},{5,4},{6,7},{7,6},{8,9},{9,8},{10,11... | collective-permute-start | bytes 3145736 | tf_op jit(solution)/shard_map/dispatch/ppermute | solution.py:25
  68.8 1.6 copy-start.5
  72.6 3.8 %copy-start.3 = (bf16[512,256]{1,0:T(8,128)(2,1)S(1)}, bf16[512,256]{1,0:T(8,128)(2,1)}, u32[]{:S(2)}) copy-start(bf16[512,256]{1,0:T(8,128)(2,1)} %copy-done.2) | copy-start | bytes 786436
  76.9 5.2 %copy-start.11 = (bf16[192,2048]{1,0:T(8,128)(2,1)S(1)}, bf16[192,2048]{1,0:T(8,128)(2,1)}, u32[]{:S(2)}) copy-start(bf16[192,2048]{1,0:T(8,128)(2,1)} %param.11) | copy-start | bytes 2359300
  77.5 4.6 %collective-permute-start.4 = (bf16[512,1024]{1,0:T(8,128)(2,1)S(1)}, bf16[512,1024]{1,0:T(8,128)(2,1)S(1)}, u32[]{:S(2)}, u32[]{:S(2)}) collective-permute-start(bf16[512,1024]{1,0:T(8,128)(2,1)S(1)} %convolution_convert_fusion), channel_id=1, source_target_pairs={{0,1},{1,0},{2,3},{3,2},{4,5},{5,4},{6,7},{7,6},{8,9},{9,8},{10,11... | collective-permute-start | bytes 3145736 | tf_op jit(solution)/shard_map/combine/ppermute | solution.py:25
  82.3 13.6 %collective-permute-start.5 = (bf16[512,256]{1,0:T(8,128)(2,1)S(1)}, bf16[512,256]{1,0:T(8,128)(2,1)S(1)}, u32[]{:S(2)}, u32[]{:S(2)}) collective-permute-start(bf16[512,256]{1,0:T(8,128)(2,1)S(1)} %add_convert_fusion.3), channel_id=1, source_target_pairs={{0,2},{2,0},{4,6},{6,4},{1,3},{3,1},{5,7},{7,5},{8,10},{10,8},{12,... | collective-permute-start | bytes 786440 | tf_op jit(solution)/shard_map/combine/ppermute | solution.py:21
  86.9 21.3 %collective-permute-start.6 = (bf16[512,256]{1,0:T(8,128)(2,1)S(1)}, bf16[512,256]{1,0:T(8,128)(2,1)S(1)}, u32[]{:S(2)}, u32[]{:S(2)}) collective-permute-start(bf16[512,256]{1,0:T(8,128)(2,1)S(1)} %add_convert_fusion.2), channel_id=1, source_target_pairs={{0,4},{2,6},{4,0},{6,2},{1,5},{3,7},{5,1},{7,3},{8,12},{10,14},{12... | collective-permute-start | bytes 786440 | tf_op jit(solution)/shard_map/combine/ppermute | solution.py:21
  90.2 29.9 %copy-start.13 = (bf16[256,8]{0,1:T(8,128)(2,1)S(1)}, bf16[256,8]{0,1:T(8,128)(2,1)}, u32[]{:S(2)}) copy-start(bf16[256,8]{0,1:T(8,128)(2,1)} %param.8) | copy-start | bytes 12292
  90.2 29.9 %copy-start.12 = (s32[256,8]{0,1:T(8,128)S(1)}, s32[256,8]{0,1:T(8,128)}, u32[]{:S(2)}) copy-start(s32[256,8]{0,1:T(8,128)} %param.7) | copy-start | bytes 24580
  90.2 18.1 %collective-permute-start.7 = (bf16[512,256]{1,0:T(8,128)(2,1)S(1)}, bf16[512,256]{1,0:T(8,128)(2,1)S(1)}, u32[]{:S(2)}, u32[]{:S(2)}) collective-permute-start(bf16[512,256]{1,0:T(8,128)(2,1)S(1)} %add_convert_fusion.1), channel_id=1, source_target_pairs={{0,6},{2,4},{4,2},{6,0},{1,7},{3,5},{5,3},{7,1},{8,14},{10,12},{12... | collective-permute-start | bytes 786440 | tf_op jit(solution)/shard_map/combine/ppermute | solution.py:21
  109.1 23.7 %all-to-all-start.1 = ((bf16[16,32,256]{2,1,0:T(8,128)(2,1)}), bf16[16,32,256]{2,1,0:T(8,128)(2,1)S(1)}, u32[]{:S(2)}, u32[]{:S(2)}) async-start(bf16[16,32,256]{2,1,0:T(8,128)(2,1)} %bitcast.4), calls=%async_computation.1 | async-start | bytes 524288 | tf_op jit(solution)/shard_map/combine/all_to_all | solution.py:66
  144.0 9.6 %collective-permute-start.8 = (bf16[256,256]{1,0:T(8,128)(2,1)S(1)}, bf16[256,256]{1,0:T(8,128)(2,1)S(1)}, u32[]{:S(2)}, u32[]{:S(2)}) collective-permute-start(bf16[256,256]{1,0:T(8,128)(2,1)S(1)} %reduce_sum.31), channel_id=1, source_target_pairs={{0,8},{8,0},{1,9},{9,1},{2,10},{10,2},{3,11},{11,3},{4,12},{12,4},... | collective-permute-start | bytes 393224 | tf_op jit(solution)/shard_map/combine/ppermute | solution.py:29
  154.6 30.5 %all-to-all-start.3 = ((bf16[16,32,256]{2,1,0:T(8,128)(2,1)}), bf16[16,32,256]{2,1,0:T(8,128)(2,1)S(1)}, u32[]{:S(2)}, u32[]{:S(2)}) async-start(bf16[16,32,256]{2,1,0:T(8,128)(2,1)} %bitcast.6), calls=%async_computation.3 | async-start | bytes 524288 | tf_op jit(solution)/shard_map/curvature/all_to_all | solution.py:66
  164.6 15.4 %collective-permute-start.10 = (bf16[256,256]{1,0:T(8,128)(2,1)S(1)}, bf16[256,256]{1,0:T(8,128)(2,1)S(1)}, u32[]{:S(2)}, u32[]{:S(2)}) collective-permute-start(bf16[256,256]{1,0:T(8,128)(2,1)S(1)} %add_convert_fusion.5), channel_id=1, source_target_pairs={{0,4},{2,6},{4,0},{6,2},{1,5},{3,7},{5,1},{7,3},{8,12},{10,14},{12... | collective-permute-start | bytes 393224 | tf_op jit(solution)/shard_map/tangent/ppermute | solution.py:21
  175.1 9.0 %collective-permute-start.11 = (bf16[256,256]{1,0:T(8,128)(2,1)S(1)}, bf16[256,256]{1,0:T(8,128)(2,1)S(1)}, u32[]{:S(2)}, u32[]{:S(2)}) collective-permute-start(bf16[256,256]{1,0:T(8,128)(2,1)S(1)} %add_convert_fusion.5), channel_id=1, source_target_pairs={{0,6},{2,4},{4,2},{6,0},{1,7},{3,5},{5,3},{7,1},{8,14},{10,12},{12... | collective-permute-start | bytes 393224 | tf_op jit(solution)/shard_map/tangent/ppermute | solution.py:21
  178.1 7.0 %collective-permute-start.9 = (bf16[256,256]{1,0:T(8,128)(2,1)S(1)}, bf16[256,256]{1,0:T(8,128)(2,1)S(1)}, u32[]{:S(2)}, u32[]{:S(2)}) collective-permute-start(bf16[256,256]{1,0:T(8,128)(2,1)S(1)} %add_convert_fusion.5), channel_id=1, source_target_pairs={{0,2},{2,0},{4,6},{6,4},{1,3},{3,1},{5,7},{7,5},{8,10},{10,8},{12,... | collective-permute-start | bytes 393224 | tf_op jit(solution)/shard_map/tangent/ppermute | solution.py:21
  185.1 18.0 %collective-permute-start.13 = (bf16[512,256]{1,0:T(8,128)(2,1)S(1)}, bf16[512,256]{1,0:T(8,128)(2,1)S(1)}, u32[]{:S(2)}, u32[]{:S(2)}) collective-permute-start(bf16[512,256]{1,0:T(8,128)(2,1)S(1)} %bitcast.51), channel_id=1, source_target_pairs={{0,2},{2,0},{4,6},{6,4},{1,3},{3,1},{5,7},{7,5},{8,10},{10,8},{12,... | collective-permute-start | bytes 786440 | tf_op jit(solution)/shard_map/curvature/ppermute | solution.py:21
  187.1 16.0 %collective-permute-start.14 = (bf16[512,256]{1,0:T(8,128)(2,1)S(1)}, bf16[512,256]{1,0:T(8,128)(2,1)S(1)}, u32[]{:S(2)}, u32[]{:S(2)}) collective-permute-start(bf16[512,256]{1,0:T(8,128)(2,1)S(1)} %bitcast.52), channel_id=1, source_target_pairs={{0,4},{2,6},{4,0},{6,2},{1,5},{3,7},{5,1},{7,3},{8,12},{10,14},{12... | collective-permute-start | bytes 786440 | tf_op jit(solution)/shard_map/curvature/ppermute | solution.py:21
  191.1 12.0 %collective-permute-start.15 = (bf16[512,256]{1,0:T(8,128)(2,1)S(1)}, bf16[512,256]{1,0:T(8,128)(2,1)S(1)}, u32[]{:S(2)}, u32[]{:S(2)}) collective-permute-start(bf16[512,256]{1,0:T(8,128)(2,1)S(1)} %bitcast.53), channel_id=1, source_target_pairs={{0,6},{2,4},{4,2},{6,0},{1,7},{3,5},{5,3},{7,1},{8,14},{10,12},{12... | collective-permute-start | bytes 786440 | tf_op jit(solution)/shard_map/curvature/ppermute | solution.py:21
  194.5 20.8 %collective-permute-start.12 = (bf16[1024,256]{1,0:T(8,128)(2,1)S(1)}, bf16[1024,256]{1,0:T(8,128)(2,1)S(1)}, u32[]{:S(2)}, u32[]{:S(2)}) collective-permute-start(bf16[1024,256]{1,0:T(8,128)(2,1)S(1)} %pad_maximum_fusion.3), channel_id=1, source_target_pairs={{0,1},{1,0},{2,3},{3,2},{4,5},{5,4},{6,7},{7,6},{8,9},{9,8},{10,11... | collective-permute-start | bytes 1572872 | tf_op jit(solution)/shard_map/tangent/ppermute | solution.py:25
  203.2 13.7 %collective-permute-start.16 = (bf16[2048,256]{1,0:T(8,128)(2,1)S(1)}, bf16[2048,256]{1,0:T(8,128)(2,1)S(1)}, u32[]{:S(2)}, u32[]{:S(2)}) collective-permute-start(bf16[2048,256]{1,0:T(8,128)(2,1)S(1)} %pad_maximum_fusion.2), channel_id=1, source_target_pairs={{0,1},{1,0},{2,3},{3,2},{4,5},{5,4},{6,7},{7,6},{8,9},{9,8},{10,11... | collective-permute-start | bytes 3145736 | tf_op jit(solution)/shard_map/curvature/ppermute | solution.py:25
  215.4 2.4 %copy-start.1 = (bf16[256,2048]{1,0:T(8,128)(2,1)}, bf16[256,2048]{1,0:T(8,128)(2,1)S(1)}, u32[]{:S(2)}) copy-start(bf16[256,2048]{1,0:T(8,128)(2,1)S(1)} %slice_dynamic-update-slice_fusion) | copy-start | bytes 3145732
  217.8 0.9 copy-start.7

commit v6 on v5

--- a/solution.py
+++ b/solution.py
@@ -68,13 +68,18 @@
         )
         return moved.reshape(rows, cols)
 
-    def with_cores(pieces):
-        crossed = swap_cores(jnp.concatenate(pieces)).reshape(LINE, *pieces[0].shape)
-        return {
-            (mask, other): (pieces[mask], crossed[mask])[other]
-            for other in range(CORES)
-            for mask in range(LINE)
-        }
+    def swap_in_two(pieces):
+        half = LINE // 2
+        crossed = []
+        for group in (pieces[:half], pieces[half:]):
+            arrived = swap_cores(jnp.concatenate(group))
+            crossed += list(arrived.reshape(half, *group[0].shape))
+        return crossed
+
+    def place(whole, pieces, other):
+        for mask in reversed(range(LINE)):
+            whole = lax.dynamic_update_slice_in_dim(whole, pieces[mask], first_col(mask, other), 1)
+        return whole
 
     def gather_line(block):
         return [block, *(swap_line(block, mask) for mask in MASKS)]
@@ -83,10 +88,15 @@
         own_cols = columns(tokens, 0, 0)
         outgoing = jnp.dot(select, own_cols, preferred_element_type=jnp.float32)
         arrived = over_planes(outgoing.astype(jnp.bfloat16))
-        other_cols = jnp.concatenate([columns(direction, mask, 1) for mask in range(LINE)], axis=1)
+        direction_other = swap_cores(
+            jnp.concatenate([columns(direction, mask, 1) for mask in range(LINE)], axis=1)
+        )
         both = jnp.concatenate([gate_weight, up_weight], axis=0)
-        arrived, other_cols, both = lax.optimization_barrier((arrived, other_cols, both))
-        row_blocks = with_cores(gather_line(arrived))
+        arrived, direction_other, both = lax.optimization_barrier((arrived, direction_other, both))
+        near_blocks = gather_line(arrived)
+        row_blocks = {(mask, 0): block for mask, block in enumerate(near_blocks)}
+        for mask, block in enumerate(swap_in_two(near_blocks)):
+            row_blocks[(mask, 1)] = block
 
     with jax.named_scope("experts"):
         value = 0.0
@@ -99,17 +109,18 @@
             )
         hidden = jax.nn.silu(value[:, :unit_count]) * value[:, unit_count:]
         hidden = hidden.astype(jnp.bfloat16)
+        hidden_other = swap_cores(hidden)
 
     with jax.named_scope("combine"):
-        crossed = swap_cores(
-            jnp.dot(hidden, other_cols, preferred_element_type=jnp.float32).astype(jnp.bfloat16)
-        )
-
         def pair_out(mask):
             own = jnp.dot(
                 hidden, columns(direction, mask, 0), preferred_element_type=jnp.float32
             )
-            other = crossed[:, mask * cols : (mask + 1) * cols].astype(jnp.float32)
+            other = jnp.dot(
+                hidden_other,
+                direction_other[:, mask * cols : (mask + 1) * cols],
+                preferred_element_type=jnp.float32,
+            )
             return (own + other).astype(jnp.bfloat16)
 
         arrived = [swap_line(pair_out(mask), mask).astype(jnp.float32) for mask in MASKS]
@@ -135,22 +146,19 @@
         moved, *pieces = lax.optimization_barrier((moved, *pieces))
 
     with jax.named_scope("curvature"):
-        scaled_blocks = with_cores(gather_line(moved))
+        scaled_blocks = gather_line(moved)
+
+        def products(units):
+            return [contract_rows(units, block).astype(jnp.bfloat16) for block in scaled_blocks]
+
         curvature = jnp.zeros((unit_count, width), jnp.bfloat16)
-        for (mask, other), block in scaled_blocks.items():
-            curvature = lax.dynamic_update_slice_in_dim(
-                curvature,
-                contract_rows(hidden, block).astype(jnp.bfloat16),
-                first_col(mask, other),
-                1,
-            )
+        curvature = place(curvature, products(hidden), 0)
+        curvature = place(curvature, swap_in_two(products(hidden_other)), 1)
 
     with jax.named_scope("tangent"):
-        tangent_out = jnp.zeros((col_tok, width), jnp.bfloat16)
-        for (mask, other), block in with_cores(pieces).items():
-            tangent_out = lax.dynamic_update_slice_in_dim(
-                tangent_out, block, first_col(mask, other), 1
-            )
+        tangent_out = place(jnp.zeros((col_tok, width), jnp.bfloat16), pieces, 0)
+        crossed = swap_cores(jnp.concatenate(pieces)).reshape(LINE, col_tok, cols)
+        tangent_out = place(tangent_out, list(crossed), 1)
     return tangent_out, curvature
 
 

time: 222 us -> 223 us (level)
    ppermute x12, waiting for transfers between devices: 29.5 us -> 36.6 us  [swap_line(): return lax.ppermute(value, 'line', [(i, i ^ mask) for i in range(LINE)])]
    dot_general x1 -> x4, matrix products: 0.47 us -> 5.42 us  [pair_out(): jnp.dot(hidden_other, direction_other[:, mask * cols:(mask + 1) * cols],...]
    dot_general x8, matrix products: 7.28 us -> 3.47 us  [shards(): lax.dot_general(block, columns(both, mask, other), (((1,), (1,)), ((), ()...]
    all_to_all x3, waiting for transfers between devices: 24.2 us -> 21.1 us  [over_planes(): lax.all_to_all(slots.reshape(n_expert, slot_count, cols), 'expert', 0, 0,...]
    ppermute x4 -> x7, starting transfers between devices: 34.1 us -> 31 us  [swap_cores(): return lax.ppermute(value, 'core', [(i, i ^ 1) for i in range(CORES)])]
  transfers between devices with their start and end apart: 20 -> 23, of which waited for: 12 -> 11; matrix products, arithmetic and copies ran while one was open for 2% -> 4% of each run, Pallas kernels for 0% -> 0%
where the time goes in v6:
time: 223 us; the launch traced here: 220 us
  starting transfers between devices  124 us (56%)
  waiting for transfers between devices  63.1 us (28%)
  matrix products  13.9 us (6%)
  blocking collectives  10.8 us (5%)
  other arithmetic  3.58 us (2%)
  local copies, waits for them, and re-layouts  3.17 us (1%)
    ppermute x12, starting transfers between devices, swap_line(): return lax.ppermute(value, 'line', [(i, i ^ mask) for i in range(LINE)])  45.1 us
    all_to_all x3, starting transfers between devices, over_planes(): lax.all_to_all(slots.reshape(n_expert, slot_count, cols), 'expert', 0, 0,...  41.9 us
    ppermute x12, waiting for transfers between devices, swap_line(): return lax.ppermute(value, 'line', [(i, i ^ mask) for i in range(LINE)])  36.6 us
    ppermute x7, starting transfers between devices, swap_cores(): return lax.ppermute(value, 'core', [(i, i ^ 1) for i in range(CORES)])  31 us
    all_to_all x3, waiting for transfers between devices, over_planes(): lax.all_to_all(slots.reshape(n_expert, slot_count, cols), 'expert', 0, 0,...  21.1 us
    all_to_all x1, blocking collectives, shards(): lax.all_to_all(jnp.broadcast_to(part, (EXP_COL // HALVES, col_tok, cols))...  10.8 us
    ppermute x1, starting transfers between devices, swap_halves(): return lax.ppermute(value, 'half', [(i, i ^ 1) for i in range(HALVES)])  6.21 us
    dot_general x4, matrix products, pair_out(): jnp.dot(hidden_other, direction_other[:, mask * cols:(mask + 1) * cols],...  5.42 us
  transfers between devices with their start and end apart: 23, of which 11 were waited for; matrix products, arithmetic and copies ran while one was open for 4% of the time, Pallas kernels for 0%

profile of v6, /device:TPU:1, one launch (start us, length us, event | category | flops | bytes accessed | tf_op | source)
XLA Modules:
  0.0 220.2 jit_solution(9889048030194408760)
XLA Ops:
  0.7 0.9 compare_reduce_fusion
  1.7 0.6 reduce-window.6
  2.8 1.0 convolution_convert_fusion
  3.8 19.4 %all-to-all-start = ((bf16[16,32,256]{2,1,0:T(8,128)(2,1)}), bf16[16,32,256]{2,1,0:T(8,128)(2,1)S(1)}, u32[]{:S(2)}, u32[]{:S(2)}) async-start(bf16[16,32,256]{2,1,0:T(8,128)(2,1)} %bitcast.2), calls=%async_computation | async-start | bytes 524288 | tf_op jit(solution)/shard_map/dispatch/all_to_all | solution.py:66
  23.4 3.0 %collective-permute-start = (bf16[192,1024]{1,0:T(8,128)(2,1)S(1)}, bf16[192,1024]{1,0:T(8,128)(2,1)}, u32[]{:S(2)}, u32[]{:S(2)}) collective-permute-start(bf16[192,1024]{1,0:T(8,128)(2,1)S(1)} %pad_maximum_fusion.4), channel_id=1, source_target_pairs={{0,1},{1,0},{2,3},{3,2},{4,5},{5,4},{6,7},{7,6},{8,9},{9,8},{10,11... | collective-permute-start | bytes 1179656 | tf_op jit(solution)/shard_map/dispatch/ppermute | solution.py:25
  26.5 1.3 collective-permute-done
  27.9 8.5 %all-to-all-done = bf16[16,32,256]{2,1,0:T(8,128)(2,1)S(1)} async-done(((bf16[16,32,256]{2,1,0:T(8,128)(2,1)}), bf16[16,32,256]{2,1,0:T(8,128)(2,1)S(1)}, u32[]{:S(2)}, u32[]{:S(2)}) %all-to-all-start) | async-done | bytes 262176 | tf_op jit(solution)/shard_map/dispatch/all_to_all | solution.py:66
  36.3 3.2 %collective-permute-start.1 = (bf16[512,256]{1,0:T(8,128)(2,1)S(1)}, bf16[512,256]{1,0:T(8,128)(2,1)S(1)}, u32[]{:S(2)}, u32[]{:S(2)}) collective-permute-start(bf16[512,256]{1,0:T(8,128)(2,1)S(1)} %bitcast.62), channel_id=1, source_target_pairs={{0,2},{2,0},{4,6},{6,4},{1,3},{3,1},{5,7},{7,5},{8,10},{10,8},{12,... | collective-permute-start | bytes 786440 | tf_op jit(solution)/shard_map/dispatch/ppermute | solution.py:21
  39.5 4.1 %collective-permute-start.3 = (bf16[512,256]{1,0:T(8,128)(2,1)S(1)}, bf16[512,256]{1,0:T(8,128)(2,1)S(1)}, u32[]{:S(2)}, u32[]{:S(2)}) collective-permute-start(bf16[512,256]{1,0:T(8,128)(2,1)S(1)} %bitcast.63), channel_id=1, source_target_pairs={{0,6},{2,4},{4,2},{6,0},{1,7},{3,5},{5,3},{7,1},{8,14},{10,12},{12... | collective-permute-start | bytes 786440 | tf_op jit(solution)/shard_map/dispatch/ppermute | solution.py:21
  43.7 2.0 collective-permute-start.2
  45.8 8.9 %collective-permute-start.4 = (bf16[1024,256]{1,0:T(8,128)(2,1)S(1)}, bf16[1024,256]{1,0:T(8,128)(2,1)S(1)}, u32[]{:S(2)}, u32[]{:S(2)}) collective-permute-start(bf16[1024,256]{1,0:T(8,128)(2,1)S(1)} %pad_maximum_fusion.1), channel_id=1, source_target_pairs={{0,1},{1,0},{2,3},{3,2},{4,5},{5,4},{6,7},{7,6},{8,9},{9,8},{10,11... | collective-permute-start | bytes 1572872 | tf_op jit(solution)/shard_map/dispatch/ppermute | solution.py:25
  54.7 10.3 %collective-permute-done.2 = bf16[512,256]{1,0:T(8,128)(2,1)} collective-permute-done((bf16[512,256]{1,0:T(8,128)(2,1)S(1)}, bf16[512,256]{1,0:T(8,128)(2,1)}, u32[]{:S(2)}, u32[]{:S(2)}) %collective-permute-start.2) | collective-permute-done | bytes 262176 | tf_op jit(solution)/shard_map/dispatch/ppermute | solution.py:21
  65.0 1.0 pad_maximum_fusion.2
  66.0 4.9 %collective-permute-start.5 = (bf16[1024,256]{1,0:T(8,128)(2,1)S(1)}, bf16[1024,256]{1,0:T(8,128)(2,1)S(1)}, u32[]{:S(2)}, u32[]{:S(2)}) collective-permute-start(bf16[1024,256]{1,0:T(8,128)(2,1)S(1)} %pad_maximum_fusion.2), channel_id=1, source_target_pairs={{0,1},{1,0},{2,3},{3,2},{4,5},{5,4},{6,7},{7,6},{8,9},{9,8},{10,11... | collective-permute-start | bytes 1572872 | tf_op jit(solution)/shard_map/dispatch/ppermute | solution.py:25
  71.2 1.2 fusion.42
  74.0 0.4 fusion.5
  74.5 0.5 copy-done.6
  75.3 1.9 collective-permute-start.6
  77.8 0.9 collective-permute-done.6
  78.7 1.2 fusion.12
  79.9 1.9 collective-permute-start.7
  81.8 1.2 fusion.13
  82.9 4.5 %collective-permute-start.8 = (bf16[512,256]{1,0:T(8,128)(2,1)S(1)}, bf16[512,256]{1,0:T(8,128)(2,1)S(1)}, u32[]{:S(2)}, u32[]{:S(2)}) collective-permute-start(bf16[512,256]{1,0:T(8,128)(2,1)S(1)} %fusion.13), channel_id=1, source_target_pairs={{0,4},{2,6},{4,0},{6,2},{1,5},{3,7},{5,1},{7,3},{8,12},{10,14},{12... | collective-permute-start | bytes 786440 | tf_op jit(solution)/shard_map/combine/ppermute | solution.py:21
  87.5 1.2 fusion.14
  88.7 2.8 %collective-permute-start.9 = (bf16[512,256]{1,0:T(8,128)(2,1)S(1)}, bf16[512,256]{1,0:T(8,128)(2,1)S(1)}, u32[]{:S(2)}, u32[]{:S(2)}) collective-permute-start(bf16[512,256]{1,0:T(8,128)(2,1)S(1)} %fusion.14), channel_id=1, source_target_pairs={{0,6},{2,4},{4,2},{6,0},{1,7},{3,5},{5,3},{7,1},{8,14},{10,12},{12... | collective-permute-start | bytes 786440 | tf_op jit(solution)/shard_map/combine/ppermute | solution.py:21
  91.8 13.2 %collective-permute-done.8 = bf16[512,256]{1,0:T(8,128)(2,1)S(1)} collective-permute-done((bf16[512,256]{1,0:T(8,128)(2,1)S(1)}, bf16[512,256]{1,0:T(8,128)(2,1)S(1)}, u32[]{:S(2)}, u32[]{:S(2)}) %collective-permute-start.8) | collective-permute-done | bytes 262176 | tf_op jit(solution)/shard_map/combine/ppermute | solution.py:21
  105.1 1.9 fusion.11
  107.0 10.9 %all-to-all-start.1 = ((bf16[16,32,256]{2,1,0:T(8,128)(2,1)}), bf16[16,32,256]{2,1,0:T(8,128)(2,1)S(1)}, u32[]{:S(2)}, u32[]{:S(2)}) async-start(bf16[16,32,256]{2,1,0:T(8,128)(2,1)} %bitcast.4), calls=%async_computation.1 | async-start | bytes 524288 | tf_op jit(solution)/shard_map/combine/all_to_all | solution.py:66
  118.1 12.6 %all-to-all-done.1 = bf16[16,32,256]{2,1,0:T(8,128)(2,1)S(1)} async-done(((bf16[16,32,256]{2,1,0:T(8,128)(2,1)}), bf16[16,32,256]{2,1,0:T(8,128)(2,1)S(1)}, u32[]{:S(2)}, u32[]{:S(2)}) %all-to-all-start.1) | async-done | bytes 262176 | tf_op jit(solution)/shard_map/combine/all_to_all | solution.py:66
  131.1 10.8 %all_to_all.20 = bf16[4,256,256]{2,1,0:T(8,128)(2,1)S(1)} all-to-all(bf16[4,256,256]{2,1,0:T(8,128)(2,1)S(1)} %broadcast_in_dim.45), channel_id=1, replica_groups=mesh['expert'=16,'x'=4,'half'=2,'line'=4,'core'=2] {'x'}, dimensions={0} | all-to-all | bytes 1048576 | tf_op jit(solution)/shard_map/combine/all_to_all | solution.py:130
  141.9 6.2 %collective-permute-start.10 = (bf16[256,256]{1,0:T(8,128)(2,1)S(1)}, bf16[256,256]{1,0:T(8,128)(2,1)S(1)}, u32[]{:S(2)}, u32[]{:S(2)}) collective-permute-start(bf16[256,256]{1,0:T(8,128)(2,1)S(1)} %reduce_sum.31), channel_id=1, source_target_pairs={{0,8},{8,0},{1,9},{9,1},{2,10},{10,2},{3,11},{11,3},{4,12},{12,4},... | collective-permute-start | bytes 393224 | tf_op jit(solution)/shard_map/combine/ppermute | solution.py:29
  148.4 3.1 %collective-permute-done.10 = bf16[256,256]{1,0:T(8,128)(2,1)S(1)} collective-permute-done((bf16[256,256]{1,0:T(8,128)(2,1)S(1)}, bf16[256,256]{1,0:T(8,128)(2,1)S(1)}, u32[]{:S(2)}, u32[]{:S(2)}) %collective-permute-start.10) | collective-permute-done | bytes 131104 | tf_op jit(solution)/shard_map/combine/ppermute | solution.py:29
  151.6 0.9 fusion.15
  152.5 11.6 %all-to-all-start.3 = ((bf16[16,32,256]{2,1,0:T(8,128)(2,1)}), bf16[16,32,256]{2,1,0:T(8,128)(2,1)S(1)}, u32[]{:S(2)}, u32[]{:S(2)}) async-start(bf16[16,32,256]{2,1,0:T(8,128)(2,1)} %bitcast.6), calls=%async_computation.3 | async-start | bytes 524288 | tf_op jit(solution)/shard_map/curvature/all_to_all | solution.py:66
  164.1 9.1 %collective-permute-start.11 = (bf16[256,256]{1,0:T(8,128)(2,1)S(1)}, bf16[256,256]{1,0:T(8,128)(2,1)S(1)}, u32[]{:S(2)}, u32[]{:S(2)}) collective-permute-start(bf16[256,256]{1,0:T(8,128)(2,1)S(1)} %add_convert_fusion), channel_id=1, source_target_pairs={{0,2},{2,0},{4,6},{6,4},{1,3},{3,1},{5,7},{7,5},{8,10},{10,8},{12,... | collective-permute-start | bytes 393224 | tf_op jit(solution)/shard_map/tangent/ppermute | solution.py:21
  173.2 2.8 %collective-permute-start.12 = (bf16[256,256]{1,0:T(8,128)(2,1)S(1)}, bf16[256,256]{1,0:T(8,128)(2,1)S(1)}, u32[]{:S(2)}, u32[]{:S(2)}) collective-permute-start(bf16[256,256]{1,0:T(8,128)(2,1)S(1)} %add_convert_fusion), channel_id=1, source_target_pairs={{0,4},{2,6},{4,0},{6,2},{1,5},{3,7},{5,1},{7,3},{8,12},{10,14},{12... | collective-permute-start | bytes 393224 | tf_op jit(solution)/shard_map/tangent/ppermute | solution.py:21
  176.0 3.1 %collective-permute-start.13 = (bf16[256,256]{1,0:T(8,128)(2,1)S(1)}, bf16[256,256]{1,0:T(8,128)(2,1)S(1)}, u32[]{:S(2)}, u32[]{:S(2)}) collective-permute-start(bf16[256,256]{1,0:T(8,128)(2,1)S(1)} %add_convert_fusion), channel_id=1, source_target_pairs={{0,6},{2,4},{4,2},{6,0},{1,7},{3,5},{5,3},{7,1},{8,14},{10,12},{12... | collective-permute-start | bytes 393224 | tf_op jit(solution)/shard_map/tangent/ppermute | solution.py:21
  179.1 2.1 collective-permute-done.12
  181.3 3.6 %collective-permute-done.13 = bf16[256,256]{1,0:T(8,128)(2,1)S(1)} collective-permute-done((bf16[256,256]{1,0:T(8,128)(2,1)S(1)}, bf16[256,256]{1,0:T(8,128)(2,1)S(1)}, u32[]{:S(2)}, u32[]{:S(2)}) %collective-permute-start.13) | collective-permute-done | bytes 131104 | tf_op jit(solution)/shard_map/tangent/ppermute | solution.py:21
  184.9 5.6 %collective-permute-start.17 = (bf16[512,256]{1,0:T(8,128)(2,1)S(1)}, bf16[512,256]{1,0:T(8,128)(2,1)S(1)}, u32[]{:S(2)}, u32[]{:S(2)}) collective-permute-start(bf16[512,256]{1,0:T(8,128)(2,1)S(1)} %bitcast.57), channel_id=1, source_target_pairs={{0,2},{2,0},{4,6},{6,4},{1,3},{3,1},{5,7},{7,5},{8,10},{10,8},{12,... | collective-permute-start | bytes 786440 | tf_op jit(solution)/shard_map/curvature/ppermute | solution.py:21
  190.5 2.4 %collective-permute-start.16 = (bf16[512,256]{1,0:T(8,128)(2,1)S(1)}, bf16[512,256]{1,0:T(8,128)(2,1)S(1)}, u32[]{:S(2)}, u32[]{:S(2)}) collective-permute-start(bf16[512,256]{1,0:T(8,128)(2,1)S(1)} %bitcast.58), channel_id=1, source_target_pairs={{0,4},{2,6},{4,0},{6,2},{1,5},{3,7},{5,1},{7,3},{8,12},{10,14},{12... | collective-permute-start | bytes 786440 | tf_op jit(solution)/shard_map/curvature/ppermute | solution.py:21
  192.8 3.5 %collective-permute-start.15 = (bf16[512,256]{1,0:T(8,128)(2,1)S(1)}, bf16[512,256]{1,0:T(8,128)(2,1)S(1)}, u32[]{:S(2)}, u32[]{:S(2)}) collective-permute-start(bf16[512,256]{1,0:T(8,128)(2,1)S(1)} %bitcast.59), channel_id=1, source_target_pairs={{0,6},{2,4},{4,2},{6,0},{1,7},{3,5},{5,3},{7,1},{8,14},{10,12},{12... | collective-permute-start | bytes 786440 | tf_op jit(solution)/shard_map/curvature/ppermute | solution.py:21
  196.4 4.9 %collective-permute-start.14 = (bf16[1024,256]{1,0:T(8,128)(2,1)S(1)}, bf16[1024,256]{1,0:T(8,128)(2,1)S(1)}, u32[]{:S(2)}, u32[]{:S(2)}) collective-permute-start(bf16[1024,256]{1,0:T(8,128)(2,1)S(1)} %pad_maximum_fusion.3), channel_id=1, source_target_pairs={{0,1},{1,0},{2,3},{3,2},{4,5},{5,4},{6,7},{7,6},{8,9},{9,8},{10,11... | collective-permute-start | bytes 1572872 | tf_op jit(solution)/shard_map/tangent/ppermute | solution.py:25
  202.0 1.9 collective-permute-start.19
  203.9 7.3 %collective-permute-done.16 = bf16[512,256]{1,0:T(8,128)(2,1)S(1)} collective-permute-done((bf16[512,256]{1,0:T(8,128)(2,1)S(1)}, bf16[512,256]{1,0:T(8,128)(2,1)S(1)}, u32[]{:S(2)}, u32[]{:S(2)}) %collective-permute-start.16) | collective-permute-done | bytes 262176 | tf_op jit(solution)/shard_map/curvature/ppermute | solution.py:21
  211.7 5.5 %collective-permute-start.18 = (bf16[384,256]{1,0:T(8,128)(2,1)S(1)}, bf16[384,256]{1,0:T(8,128)(2,1)S(1)}, u32[]{:S(2)}, u32[]{:S(2)}) collective-permute-start(bf16[384,256]{1,0:T(8,128)(2,1)S(1)} %pad_maximum_fusion.5), channel_id=1, source_target_pairs={{0,1},{1,0},{2,3},{3,2},{4,5},{5,4},{6,7},{7,6},{8,9},{9,8},{10,11... | collective-permute-start | bytes 589832 | tf_op jit(solution)/shard_map/curvature/ppermute | solution.py:25
  218.5 0.8 copy-done.2
  219.2 1.0 copy-done.1
  (93 shorter events, 6.9 us)
Async XLA Ops:
  0.6 2.2 copy-start
  0.6 22.6 %copy-start.5 = (bf16[192,2048]{1,0:T(8,128)(2,1)S(1)}, bf16[192,2048]{1,0:T(8,128)(2,1)}, u32[]{:S(2)}) copy-start(bf16[192,2048]{1,0:T(8,128)(2,1)} %param.11) | copy-start | bytes 2359300
  0.7 1.0 copy-start.11
  1.6 24.9 %copy-start.7 = (pred[16,256]{1,0:T(8,128)(4,1)}, pred[16,256]{1,0:T(8,128)(4,1)S(1)}, u32[]{:S(2)}) copy-start(pred[16,256]{1,0:T(8,128)(4,1)S(1)} %compare_reduce_fusion) | copy-start | bytes 12292
  3.8 32.6 %all-to-all-start = ((bf16[16,32,256]{2,1,0:T(8,128)(2,1)}), bf16[16,32,256]{2,1,0:T(8,128)(2,1)S(1)}, u32[]{:S(2)}, u32[]{:S(2)}) async-start(bf16[16,32,256]{2,1,0:T(8,128)(2,1)} %bitcast.2), calls=%async_computation | async-start | bytes 524288 | tf_op jit(solution)/shard_map/dispatch/all_to_all | solution.py:66
  23.2 3.1 %copy-start.3 = (bf16[192,2048]{1,0:T(8,128)(2,1)S(1)}, bf16[192,2048]{1,0:T(8,128)(2,1)}, u32[]{:S(2)}) copy-start(bf16[192,2048]{1,0:T(8,128)(2,1)} %param.10) | copy-start | bytes 2359300
  23.3 3.1 %copy-start.4 = (bf16[192,2048]{1,0:T(8,128)(2,1)S(1)}, bf16[192,2048]{1,0:T(8,128)(2,1)}, u32[]{:S(2)}) copy-start(bf16[192,2048]{1,0:T(8,128)(2,1)} %param.9) | copy-start | bytes 2359300
  23.4 4.5 %collective-permute-start = (bf16[192,1024]{1,0:T(8,128)(2,1)S(1)}, bf16[192,1024]{1,0:T(8,128)(2,1)}, u32[]{:S(2)}, u32[]{:S(2)}) collective-permute-start(bf16[192,1024]{1,0:T(8,128)(2,1)S(1)} %pad_maximum_fusion.4), channel_id=1, source_target_pairs={{0,1},{1,0},{2,3},{3,2},{4,5},{5,4},{6,7},{7,6},{8,9},{9,8},{10,11... | collective-permute-start | bytes 1179656 | tf_op jit(solution)/shard_map/dispatch/ppermute | solution.py:25
  36.3 9.4 %collective-permute-start.1 = (bf16[512,256]{1,0:T(8,128)(2,1)S(1)}, bf16[512,256]{1,0:T(8,128)(2,1)S(1)}, u32[]{:S(2)}, u32[]{:S(2)}) collective-permute-start(bf16[512,256]{1,0:T(8,128)(2,1)S(1)} %bitcast.62), channel_id=1, source_target_pairs={{0,2},{2,0},{4,6},{6,4},{1,3},{3,1},{5,7},{7,5},{8,10},{10,8},{12,... | collective-permute-start | bytes 786440 | tf_op jit(solution)/shard_map/dispatch/ppermute | solution.py:21
  39.5 15.2 %collective-permute-start.3 = (bf16[512,256]{1,0:T(8,128)(2,1)S(1)}, bf16[512,256]{1,0:T(8,128)(2,1)S(1)}, u32[]{:S(2)}, u32[]{:S(2)}) collective-permute-start(bf16[512,256]{1,0:T(8,128)(2,1)S(1)} %bitcast.63), channel_id=1, source_target_pairs={{0,6},{2,4},{4,2},{6,0},{1,7},{3,5},{5,3},{7,1},{8,14},{10,12},{12... | collective-permute-start | bytes 786440 | tf_op jit(solution)/shard_map/dispatch/ppermute | solution.py:21
  43.7 21.3 %collective-permute-start.2 = (bf16[512,256]{1,0:T(8,128)(2,1)S(1)}, bf16[512,256]{1,0:T(8,128)(2,1)}, u32[]{:S(2)}, u32[]{:S(2)}) collective-permute-start(bf16[512,256]{1,0:T(8,128)(2,1)S(1)} %bitcast.64), channel_id=1, source_target_pairs={{0,4},{2,6},{4,0},{6,2},{1,5},{3,7},{5,1},{7,3},{8,12},{10,14},{12... | collective-permute-start | bytes 786440 | tf_op jit(solution)/shard_map/dispatch/ppermute | solution.py:21
  45.8 27.0 %collective-permute-start.4 = (bf16[1024,256]{1,0:T(8,128)(2,1)S(1)}, bf16[1024,256]{1,0:T(8,128)(2,1)S(1)}, u32[]{:S(2)}, u32[]{:S(2)}) collective-permute-start(bf16[1024,256]{1,0:T(8,128)(2,1)S(1)} %pad_maximum_fusion.1), channel_id=1, source_target_pairs={{0,1},{1,0},{2,3},{3,2},{4,5},{5,4},{6,7},{7,6},{8,9},{9,8},{10,11... | collective-permute-start | bytes 1572872 | tf_op jit(solution)/shard_map/dispatch/ppermute | solution.py:25
  66.0 7.3 %collective-permute-start.5 = (bf16[1024,256]{1,0:T(8,128)(2,1)S(1)}, bf16[1024,256]{1,0:T(8,128)(2,1)S(1)}, u32[]{:S(2)}, u32[]{:S(2)}) collective-permute-start(bf16[1024,256]{1,0:T(8,128)(2,1)S(1)} %pad_maximum_fusion.2), channel_id=1, source_target_pairs={{0,1},{1,0},{2,3},{3,2},{4,5},{5,4},{6,7},{7,6},{8,9},{9,8},{10,11... | collective-permute-start | bytes 1572872 | tf_op jit(solution)/shard_map/dispatch/ppermute | solution.py:25
  73.9 1.1 copy-start.6
  75.3 3.3 %collective-permute-start.6 = (bf16[512,192]{0,1:T(8,128)(2,1)S(1)}, bf16[512,192]{0,1:T(8,128)(2,1)S(1)}, u32[]{:S(2)}, u32[]{:S(2)}) collective-permute-start(bf16[512,192]{0,1:T(8,128)(2,1)S(1)} %fusion.23), channel_id=1, source_target_pairs={{0,1},{1,0},{2,3},{3,2},{4,5},{5,4},{6,7},{7,6},{8,9},{9,8},{10,11... | collective-permute-start | bytes 589832 | tf_op jit(solution)/shard_map/experts/ppermute | solution.py:25
  79.9 12.0 %collective-permute-start.7 = (bf16[512,256]{1,0:T(8,128)(2,1)S(1)}, bf16[512,256]{1,0:T(8,128)(2,1)S(1)}, u32[]{:S(2)}, u32[]{:S(2)}) collective-permute-start(bf16[512,256]{1,0:T(8,128)(2,1)S(1)} %fusion.12), channel_id=1, source_target_pairs={{0,2},{2,0},{4,6},{6,4},{1,3},{3,1},{5,7},{7,5},{8,10},{10,8},{12,... | collective-permute-start | bytes 786440 | tf_op jit(solution)/shard_map/combine/ppermute | solution.py:21
  82.9 22.1 %collective-permute-start.8 = (bf16[512,256]{1,0:T(8,128)(2,1)S(1)}, bf16[512,256]{1,0:T(8,128)(2,1)S(1)}, u32[]{:S(2)}, u32[]{:S(2)}) collective-permute-start(bf16[512,256]{1,0:T(8,128)(2,1)S(1)} %fusion.13), channel_id=1, source_target_pairs={{0,4},{2,6},{4,0},{6,2},{1,5},{3,7},{5,1},{7,3},{8,12},{10,14},{12... | collective-permute-start | bytes 786440 | tf_op jit(solution)/shard_map/combine/ppermute | solution.py:21
  88.7 29.3 %copy-start.10 = (bf16[256,8]{0,1:T(8,128)(2,1)S(1)}, bf16[256,8]{0,1:T(8,128)(2,1)}, u32[]{:S(2)}) copy-start(bf16[256,8]{0,1:T(8,128)(2,1)} %param.8) | copy-start | bytes 12292
  88.7 29.3 %copy-start.9 = (s32[256,8]{0,1:T(8,128)S(1)}, s32[256,8]{0,1:T(8,128)}, u32[]{:S(2)}) copy-start(s32[256,8]{0,1:T(8,128)} %param.7) | copy-start | bytes 24580
  88.7 29.3 %copy-start.12 = (s32[16]{0:T(128)S(1)}, s32[16]{0:T(128)}, u32[]{:S(2)}) copy-start(s32[16]{0:T(128)} %copy-done.11) | copy-start | bytes 196
  88.7 42.0 %copy-start.8 = (pred[16,256]{1,0:T(8,128)(4,1)S(1)}, pred[16,256]{1,0:T(8,128)(4,1)}, u32[]{:S(2)}) copy-start(pred[16,256]{1,0:T(8,128)(4,1)} %copy-done.7) | copy-start | bytes 12292
  88.7 16.4 %collective-permute-start.9 = (bf16[512,256]{1,0:T(8,128)(2,1)S(1)}, bf16[512,256]{1,0:T(8,128)(2,1)S(1)}, u32[]{:S(2)}, u32[]{:S(2)}) collective-permute-start(bf16[512,256]{1,0:T(8,128)(2,1)S(1)} %fusion.14), channel_id=1, source_target_pairs={{0,6},{2,4},{4,2},{6,0},{1,7},{3,5},{5,3},{7,1},{8,14},{10,12},{12... | collective-permute-start | bytes 786440 | tf_op jit(solution)/shard_map/combine/ppermute | solution.py:21
  107.0 23.7 %all-to-all-start.1 = ((bf16[16,32,256]{2,1,0:T(8,128)(2,1)}), bf16[16,32,256]{2,1,0:T(8,128)(2,1)S(1)}, u32[]{:S(2)}, u32[]{:S(2)}) async-start(bf16[16,32,256]{2,1,0:T(8,128)(2,1)} %bitcast.4), calls=%async_computation.1 | async-start | bytes 524288 | tf_op jit(solution)/shard_map/combine/all_to_all | solution.py:66
  141.9 9.6 %collective-permute-start.10 = (bf16[256,256]{1,0:T(8,128)(2,1)S(1)}, bf16[256,256]{1,0:T(8,128)(2,1)S(1)}, u32[]{:S(2)}, u32[]{:S(2)}) collective-permute-start(bf16[256,256]{1,0:T(8,128)(2,1)S(1)} %reduce_sum.31), channel_id=1, source_target_pairs={{0,8},{8,0},{1,9},{9,1},{2,10},{10,2},{3,11},{11,3},{4,12},{12,4},... | collective-permute-start | bytes 393224 | tf_op jit(solution)/shard_map/combine/ppermute | solution.py:29
  152.5 32.4 %all-to-all-start.3 = ((bf16[16,32,256]{2,1,0:T(8,128)(2,1)}), bf16[16,32,256]{2,1,0:T(8,128)(2,1)S(1)}, u32[]{:S(2)}, u32[]{:S(2)}) async-start(bf16[16,32,256]{2,1,0:T(8,128)(2,1)} %bitcast.6), calls=%async_computation.3 | async-start | bytes 524288 | tf_op jit(solution)/shard_map/curvature/all_to_all | solution.py:66
  164.1 15.0 %collective-permute-start.11 = (bf16[256,256]{1,0:T(8,128)(2,1)S(1)}, bf16[256,256]{1,0:T(8,128)(2,1)S(1)}, u32[]{:S(2)}, u32[]{:S(2)}) collective-permute-start(bf16[256,256]{1,0:T(8,128)(2,1)S(1)} %add_convert_fusion), channel_id=1, source_target_pairs={{0,2},{2,0},{4,6},{6,4},{1,3},{3,1},{5,7},{7,5},{8,10},{10,8},{12,... | collective-permute-start | bytes 393224 | tf_op jit(solution)/shard_map/tangent/ppermute | solution.py:21
  173.2 8.0 %collective-permute-start.12 = (bf16[256,256]{1,0:T(8,128)(2,1)S(1)}, bf16[256,256]{1,0:T(8,128)(2,1)S(1)}, u32[]{:S(2)}, u32[]{:S(2)}) collective-permute-start(bf16[256,256]{1,0:T(8,128)(2,1)S(1)} %add_convert_fusion), channel_id=1, source_target_pairs={{0,4},{2,6},{4,0},{6,2},{1,5},{3,7},{5,1},{7,3},{8,12},{10,14},{12... | collective-permute-start | bytes 393224 | tf_op jit(solution)/shard_map/tangent/ppermute | solution.py:21
  176.0 8.9 %collective-permute-start.13 = (bf16[256,256]{1,0:T(8,128)(2,1)S(1)}, bf16[256,256]{1,0:T(8,128)(2,1)S(1)}, u32[]{:S(2)}, u32[]{:S(2)}) collective-permute-start(bf16[256,256]{1,0:T(8,128)(2,1)S(1)} %add_convert_fusion), channel_id=1, source_target_pairs={{0,6},{2,4},{4,2},{6,0},{1,7},{3,5},{5,3},{7,1},{8,14},{10,12},{12... | collective-permute-start | bytes 393224 | tf_op jit(solution)/shard_map/tangent/ppermute | solution.py:21
  184.9 16.9 %collective-permute-start.17 = (bf16[512,256]{1,0:T(8,128)(2,1)S(1)}, bf16[512,256]{1,0:T(8,128)(2,1)S(1)}, u32[]{:S(2)}, u32[]{:S(2)}) collective-permute-start(bf16[512,256]{1,0:T(8,128)(2,1)S(1)} %bitcast.57), channel_id=1, source_target_pairs={{0,2},{2,0},{4,6},{6,4},{1,3},{3,1},{5,7},{7,5},{8,10},{10,8},{12,... | collective-permute-start | bytes 786440 | tf_op jit(solution)/shard_map/curvature/ppermute | solution.py:21
  190.5 20.7 %collective-permute-start.16 = (bf16[512,256]{1,0:T(8,128)(2,1)S(1)}, bf16[512,256]{1,0:T(8,128)(2,1)S(1)}, u32[]{:S(2)}, u32[]{:S(2)}) collective-permute-start(bf16[512,256]{1,0:T(8,128)(2,1)S(1)} %bitcast.58), channel_id=1, source_target_pairs={{0,4},{2,6},{4,0},{6,2},{1,5},{3,7},{5,1},{7,3},{8,12},{10,14},{12... | collective-permute-start | bytes 786440 | tf_op jit(solution)/shard_map/curvature/ppermute | solution.py:21
  192.8 18.6 %collective-permute-start.15 = (bf16[512,256]{1,0:T(8,128)(2,1)S(1)}, bf16[512,256]{1,0:T(8,128)(2,1)S(1)}, u32[]{:S(2)}, u32[]{:S(2)}) collective-permute-start(bf16[512,256]{1,0:T(8,128)(2,1)S(1)} %bitcast.59), channel_id=1, source_target_pairs={{0,6},{2,4},{4,2},{6,0},{1,7},{3,5},{5,3},{7,1},{8,14},{10,12},{12... | collective-permute-start | bytes 786440 | tf_op jit(solution)/shard_map/curvature/ppermute | solution.py:21
  196.4 21.9 %collective-permute-start.14 = (bf16[1024,256]{1,0:T(8,128)(2,1)S(1)}, bf16[1024,256]{1,0:T(8,128)(2,1)S(1)}, u32[]{:S(2)}, u32[]{:S(2)}) collective-permute-start(bf16[1024,256]{1,0:T(8,128)(2,1)S(1)} %pad_maximum_fusion.3), channel_id=1, source_target_pairs={{0,1},{1,0},{2,3},{3,2},{4,5},{5,4},{6,7},{7,6},{8,9},{9,8},{10,11... | collective-permute-start | bytes 1572872 | tf_op jit(solution)/shard_map/tangent/ppermute | solution.py:25
  202.0 16.3 %collective-permute-start.19 = (bf16[384,256]{1,0:T(8,128)(2,1)S(1)}, bf16[384,256]{1,0:T(8,128)(2,1)S(1)}, u32[]{:S(2)}, u32[]{:S(2)}) collective-permute-start(bf16[384,256]{1,0:T(8,128)(2,1)S(1)} %pad_maximum_fusion.6), channel_id=1, source_target_pairs={{0,1},{1,0},{2,3},{3,2},{4,5},{5,4},{6,7},{7,6},{8,9},{9,8},{10,11... | collective-permute-start | bytes 589832 | tf_op jit(solution)/shard_map/curvature/ppermute | solution.py:25
  211.7 6.6 %collective-permute-start.18 = (bf16[384,256]{1,0:T(8,128)(2,1)S(1)}, bf16[384,256]{1,0:T(8,128)(2,1)S(1)}, u32[]{:S(2)}, u32[]{:S(2)}) collective-permute-start(bf16[384,256]{1,0:T(8,128)(2,1)S(1)} %pad_maximum_fusion.5), channel_id=1, source_target_pairs={{0,1},{1,0},{2,3},{3,2},{4,5},{5,4},{6,7},{7,6},{8,9},{9,8},{10,11... | collective-permute-start | bytes 589832 | tf_op jit(solution)/shard_map/curvature/ppermute | solution.py:25
  218.3 0.9 copy-start.2
  219.2 1.0 copy-start.1

commit v7 on v6

--- a/solution.py
+++ b/solution.py
@@ -8,7 +8,6 @@
 CORES = 2
 LINE = 4
 HALVES = 2
-MASKS = (1, 2, 3)
 
 
 def contract_rows(left, right):
@@ -17,8 +16,46 @@
     )
 
 
-def swap_line(value, mask):
-    return lax.ppermute(value, "line", [(i, i ^ mask) for i in range(LINE)])
+def send_line(value, pairs):
+    return lax.ppermute(value, "line", pairs)
+
+
+PAIRS = [(0, 1), (1, 0), (2, 3), (3, 2)]
+INNER = [(1, 2), (2, 1)]
+OUTWARD = [(1, 0), (2, 3)]
+INWARD = [(0, 1), (3, 2)]
+FAR_OUT = [(2, 0), (1, 3)]
+FAR_IN = [(0, 2), (3, 1)]
+
+
+def gather_line(block):
+    paired = send_line(block, PAIRS)
+    inner = send_line(block, INNER)
+    second = inner + send_line(inner, OUTWARD)
+    third = send_line(paired, INNER) + send_line(paired, FAR_OUT)
+    return [block, paired, second, third]
+
+
+def reduce_line(pieces):
+    def send(value, pairs):
+        return send_line(value.astype(jnp.bfloat16), pairs)
+
+    far = send(pieces[3], FAR_IN)
+    inner, near = send(pieces[2], INNER), send(pieces[2], INWARD)
+    far, inner, near = lax.optimization_barrier((far, inner, near))
+    paired, crossed = send(pieces[1] + far + inner, PAIRS), send(pieces[3] + near, INNER)
+    return pieces[0] + paired + crossed
+
+
+def gather_ring(block):
+    ring = HALVES * LINE
+    return [
+        block,
+        *(
+            lax.ppermute(block, ("half", "line"), [(i, (i + step) % ring) for i in range(ring)])
+            for step in (1, ring - 1, 2)
+        ),
+    ]
 
 
 def swap_cores(value):
@@ -41,11 +78,14 @@
     line_index = lax.axis_index("line")
     core_index = lax.axis_index("core")
 
-    def first_col(mask, other):
-        return ((line_index ^ mask) * CORES + (core_index ^ other)) * cols
-
-    def columns(weight, mask, other):
-        return lax.dynamic_slice_in_dim(weight, first_col(mask, other), cols, 1)
+    is_inner = ((line_index == 1) | (line_index == 2)).astype(jnp.int32)
+    gathered = [line_index ^ mask for mask in (0, 1, 2 + is_inner, 3 - is_inner)]
+
+    def first_col(line, other):
+        return ((line & (LINE - 1)) * CORES + (core_index ^ other)) * cols
+
+    def columns(weight, line, other):
+        return lax.dynamic_slice_in_dim(weight, first_col(line, other), cols, 1)
 
     with jax.named_scope("routing"):
         owner_ids = jnp.arange(n_expert, dtype=jnp.int32) * EXP_COL + local_index
@@ -70,43 +110,41 @@
 
     def swap_in_two(pieces):
         half = LINE // 2
-        crossed = []
-        for group in (pieces[:half], pieces[half:]):
-            arrived = swap_cores(jnp.concatenate(group))
-            crossed += list(arrived.reshape(half, *group[0].shape))
+        crossed = [None] * LINE
+        for first in range(half):
+            arrived = swap_cores(jnp.concatenate(pieces[first::half]))
+            crossed[first::half] = list(arrived.reshape(half, *pieces[0].shape))
         return crossed
 
-    def place(whole, pieces, other):
-        for mask in reversed(range(LINE)):
-            whole = lax.dynamic_update_slice_in_dim(whole, pieces[mask], first_col(mask, other), 1)
+    def place(whole, pieces, lines, other):
+        for line, piece in reversed(list(zip(lines, pieces))):
+            whole = lax.dynamic_update_slice_in_dim(whole, piece, first_col(line, other), 1)
         return whole
 
-    def gather_line(block):
-        return [block, *(swap_line(block, mask) for mask in MASKS)]
-
     with jax.named_scope("dispatch"):
-        own_cols = columns(tokens, 0, 0)
+        own_cols = columns(tokens, line_index, 0)
         outgoing = jnp.dot(select, own_cols, preferred_element_type=jnp.float32)
         arrived = over_planes(outgoing.astype(jnp.bfloat16))
         direction_other = swap_cores(
-            jnp.concatenate([columns(direction, mask, 1) for mask in range(LINE)], axis=1)
+            jnp.concatenate(
+                [columns(direction, line_index ^ mask, 1) for mask in range(LINE)], axis=1
+            )
         )
         both = jnp.concatenate([gate_weight, up_weight], axis=0)
         arrived, direction_other, both = lax.optimization_barrier((arrived, direction_other, both))
         near_blocks = gather_line(arrived)
-        row_blocks = {(mask, 0): block for mask, block in enumerate(near_blocks)}
-        for mask, block in enumerate(swap_in_two(near_blocks)):
-            row_blocks[(mask, 1)] = block
+        row_blocks = [near_blocks, swap_in_two(near_blocks)]
 
     with jax.named_scope("experts"):
         value = 0.0
-        for (mask, other), block in row_blocks.items():
-            value += lax.dot_general(
-                block,
-                columns(both, mask, other),
-                (((1,), (1,)), ((), ())),
-                preferred_element_type=jnp.float32,
-            )
+        for other, blocks in enumerate(row_blocks):
+            for line, block in zip(gathered, blocks):
+                value += lax.dot_general(
+                    block,
+                    columns(both, line, other),
+                    (((1,), (1,)), ((), ())),
+                    preferred_element_type=jnp.float32,
+                )
         hidden = jax.nn.silu(value[:, :unit_count]) * value[:, unit_count:]
         hidden = hidden.astype(jnp.bfloat16)
         hidden_other = swap_cores(hidden)
@@ -114,17 +152,16 @@
     with jax.named_scope("combine"):
         def pair_out(mask):
             own = jnp.dot(
-                hidden, columns(direction, mask, 0), preferred_element_type=jnp.float32
+                hidden, columns(direction, line_index ^ mask, 0), preferred_element_type=jnp.float32
             )
             other = jnp.dot(
                 hidden_other,
                 direction_other[:, mask * cols : (mask + 1) * cols],
                 preferred_element_type=jnp.float32,
             )
-            return (own + other).astype(jnp.bfloat16)
-
-        arrived = [swap_line(pair_out(mask), mask).astype(jnp.float32) for mask in MASKS]
-        expert_out = pair_out(0).astype(jnp.float32) + arrived[0] + arrived[1] + arrived[2]
+            return own + other
+
+        expert_out = reduce_line([pair_out(mask) for mask in range(LINE)])
         returned = over_planes(expert_out.astype(jnp.bfloat16))
         part = contract_rows(spread, returned).astype(jnp.bfloat16)
         parts = lax.all_to_all(
@@ -142,23 +179,25 @@
         moved = over_planes(scaled)
 
     with jax.named_scope("tangent"):
-        pieces = gather_line(tangent_late)
+        pieces = gather_ring(tangent_late)
         moved, *pieces = lax.optimization_barrier((moved, *pieces))
+        around = [line_index + step for step in (0, -1, 1, -2)]
 
     with jax.named_scope("curvature"):
         scaled_blocks = gather_line(moved)
 
+    with jax.named_scope("curvature"):
         def products(units):
             return [contract_rows(units, block).astype(jnp.bfloat16) for block in scaled_blocks]
 
         curvature = jnp.zeros((unit_count, width), jnp.bfloat16)
-        curvature = place(curvature, products(hidden), 0)
-        curvature = place(curvature, swap_in_two(products(hidden_other)), 1)
+        curvature = place(curvature, products(hidden), gathered, 0)
+        curvature = place(curvature, swap_in_two(products(hidden_other)), gathered, 1)
 
     with jax.named_scope("tangent"):
-        tangent_out = place(jnp.zeros((col_tok, width), jnp.bfloat16), pieces, 0)
+        tangent_out = place(jnp.zeros((col_tok, width), jnp.bfloat16), pieces, around, 0)
         crossed = swap_cores(jnp.concatenate(pieces)).reshape(LINE, col_tok, cols)
-        tangent_out = place(tangent_out, list(crossed), 1)
+        tangent_out = place(tangent_out, list(crossed), around, 1)
     return tangent_out, curvature
 
 

time: 223 us -> 215 us (0.964)
  starting transfers between devices: 124 us -> 121 us
    ppermute x12 -> x18, starting transfers between devices: 45.1 us -> 38 us  [the longest x15 26.8 us: send_line(): return lax.ppermute(value, 'line', pairs)]
    ppermute x7, starting transfers between devices: 31 us -> 37.1 us  [swap_cores(): return lax.ppermute(value, 'core', [(i, i ^ 1) for i in range(CORES)])]
    all_to_all x3, starting transfers between devices: 41.9 us -> 39.7 us  [over_planes(): lax.all_to_all(slots.reshape(n_expert, slot_count, cols), 'expert', 0, 0,...]
    ppermute x12 -> x18, waiting for transfers between devices: 36.6 us -> 35.3 us  [the longest x15 28.5 us: send_line(): return lax.ppermute(value, 'line', pairs)]
  transfers between devices with their start and end apart: 23 -> 29, of which waited for: 11 -> 14; matrix products, arithmetic and copies ran while one was open for 4% -> 3% of each run, Pallas kernels for 0% -> 0%
where the time goes in v7:
time: 215 us; the launch traced here: 214 us
  starting transfers between devices  121 us (56%)
  waiting for transfers between devices  62.3 us (29%)
  matrix products  12.9 us (6%)
  blocking collectives  10.7 us (5%)
  other arithmetic  3.78 us (2%)
    all_to_all x3, starting transfers between devices, over_planes(): lax.all_to_all(slots.reshape(n_expert, slot_count, cols), 'expert', 0, 0,...  39.7 us
    ppermute x7, starting transfers between devices, swap_cores(): return lax.ppermute(value, 'core', [(i, i ^ 1) for i in range(CORES)])  37.1 us
    ppermute x15, waiting for transfers between devices, send_line(): return lax.ppermute(value, 'line', pairs)  28.5 us
    ppermute x15, starting transfers between devices, send_line(): return lax.ppermute(value, 'line', pairs)  26.8 us
    all_to_all x3, waiting for transfers between devices, over_planes(): lax.all_to_all(slots.reshape(n_expert, slot_count, cols), 'expert', 0, 0,...  21.1 us
    ppermute x3, starting transfers between devices, gather_ring(): lax.ppermute(block, ('half', 'line'), [(i, (i + step) % ring) for i in ra...  11.2 us
    all_to_all x1, blocking collectives, shards(): lax.all_to_all(jnp.broadcast_to(part, (EXP_COL // HALVES, col_tok, cols))...  10.7 us
    ppermute x3, waiting for transfers between devices, gather_ring(): lax.ppermute(block, ('half', 'line'), [(i, (i + step) % ring) for i in ra...  6.87 us
  transfers between devices with their start and end apart: 29, of which 14 were waited for; matrix products, arithmetic and copies ran while one was open for 3% of the time, Pallas kernels for 0%

profile of v7, /device:TPU:1, one launch (start us, length us, event | category | flops | bytes accessed | tf_op | source)
XLA Modules:
  0.0 214.2 jit_solution(1611447149564148788)
XLA Ops:
  0.7 0.9 compare_reduce_fusion
  2.8 1.0 convolution_convert_fusion
  3.8 19.4 %all-to-all-start = ((bf16[16,32,256]{2,1,0:T(8,128)(2,1)}), bf16[16,32,256]{2,1,0:T(8,128)(2,1)S(1)}, u32[]{:S(2)}, u32[]{:S(2)}) async-start(bf16[16,32,256]{2,1,0:T(8,128)(2,1)} %bitcast.2), calls=%async_computation | async-start | bytes 524288 | tf_op jit(solution)/shard_map/dispatch/all_to_all | solution.py:106
  23.4 3.0 %collective-permute-start = (bf16[192,1024]{1,0:T(8,128)(2,1)S(1)}, bf16[192,1024]{1,0:T(8,128)(2,1)}, u32[]{:S(2)}, u32[]{:S(2)}) collective-permute-start(bf16[192,1024]{1,0:T(8,128)(2,1)S(1)} %pad_maximum_fusion.4), channel_id=1, source_target_pairs={{0,1},{1,0},{2,3},{3,2},{4,5},{5,4},{6,7},{7,6},{8,9},{9,8},{10,11... | collective-permute-start | bytes 1179656 | tf_op jit(solution)/shard_map/dispatch/ppermute | solution.py:62
  26.5 1.3 collective-permute-done
  27.9 8.5 %all-to-all-done = bf16[16,32,256]{2,1,0:T(8,128)(2,1)S(1)} async-done(((bf16[16,32,256]{2,1,0:T(8,128)(2,1)}), bf16[16,32,256]{2,1,0:T(8,128)(2,1)S(1)}, u32[]{:S(2)}, u32[]{:S(2)}) %all-to-all-start) | async-done | bytes 262176 | tf_op jit(solution)/shard_map/dispatch/all_to_all | solution.py:106
  37.0 5.7 %collective-permute-start.1 = (bf16[512,256]{1,0:T(8,128)(2,1)S(1)}, bf16[512,256]{1,0:T(8,128)(2,1)S(1)}, u32[]{:S(2)}, u32[]{:S(2)}) collective-permute-start(bf16[512,256]{1,0:T(8,128)(2,1)S(1)} %bitcast.58), channel_id=1, source_target_pairs={{0,2},{2,0},{4,6},{6,4},{1,3},{3,1},{5,7},{7,5},{8,10},{10,8},{12,... | collective-permute-start | bytes 786440 | tf_op jit(solution)/shard_map/dispatch/ppermute | solution.py:20
  42.8 1.3 collective-permute-start.3
  44.1 2.4 %collective-permute-done.1 = bf16[512,256]{1,0:T(8,128)(2,1)S(1)} collective-permute-done((bf16[512,256]{1,0:T(8,128)(2,1)S(1)}, bf16[512,256]{1,0:T(8,128)(2,1)S(1)}, u32[]{:S(2)}, u32[]{:S(2)}) %collective-permute-start.1) | collective-permute-done | bytes 262176 | tf_op jit(solution)/shard_map/dispatch/ppermute | solution.py:20
  47.2 1.3 collective-permute-start.5
  48.8 1.2 collective-permute-done.3
  50.0 1.0 add.252
  51.0 12.8 %collective-permute-start.6 = (bf16[1024,256]{1,0:T(8,128)(2,1)S(1)}, bf16[1024,256]{1,0:T(8,128)(2,1)S(1)}, u32[]{:S(2)}, u32[]{:S(2)}) collective-permute-start(bf16[1024,256]{1,0:T(8,128)(2,1)S(1)} %pad_maximum_fusion.1), channel_id=1, source_target_pairs={{0,1},{1,0},{2,3},{3,2},{4,5},{5,4},{6,7},{7,6},{8,9},{9,8},{10,11... | collective-permute-start | bytes 1572872 | tf_op jit(solution)/shard_map/dispatch/ppermute | solution.py:62
  64.0 4.4 %collective-permute-start.7 = (bf16[1024,256]{1,0:T(8,128)(2,1)S(1)}, bf16[1024,256]{1,0:T(8,128)(2,1)S(1)}, u32[]{:S(2)}, u32[]{:S(2)}) collective-permute-start(bf16[1024,256]{1,0:T(8,128)(2,1)S(1)} %pad_maximum_fusion.2), channel_id=1, source_target_pairs={{0,1},{1,0},{2,3},{3,2},{4,5},{5,4},{6,7},{7,6},{8,9},{9,8},{10,11... | collective-permute-start | bytes 1572872 | tf_op jit(solution)/shard_map/dispatch/ppermute | solution.py:62
  71.3 2.3 %collective-permute-start.8 = (bf16[512,192]{0,1:T(8,128)(2,1)S(1)}, bf16[512,192]{0,1:T(8,128)(2,1)S(1)}, u32[]{:S(2)}, u32[]{:S(2)}) collective-permute-start(bf16[512,192]{0,1:T(8,128)(2,1)S(1)} %fusion.20), channel_id=1, source_target_pairs={{0,1},{1,0},{2,3},{3,2},{4,5},{5,4},{6,7},{7,6},{8,9},{9,8},{10,11... | collective-permute-start | bytes 589832 | tf_op jit(solution)/shard_map/experts/ppermute | solution.py:62
  74.7 1.2 fusion.11
  75.8 0.7 collective-permute-start.10
  76.5 2.7 %collective-permute-start.11 = (bf16[512,256]{1,0:T(8,128)(2,1)S(1)}, bf16[512,256]{1,0:T(8,128)(2,1)S(1)}, u32[]{:S(2)}, u32[]{:S(2)}) collective-permute-start(bf16[512,256]{1,0:T(8,128)(2,1)S(1)} %fusion.11), channel_id=1, source_target_pairs={{0,2},{6,4},{1,3},{7,5},{8,10},{14,12},{9,11},{15,13},{16,18},{22,... | collective-permute-start | bytes 786440 | tf_op jit(solution)/shard_map/combine/ppermute | solution.py:20
  79.2 1.2 fusion.75
  80.4 1.3 collective-permute-start.9
  82.0 2.2 %collective-permute-done.11 = bf16[512,256]{1,0:T(8,128)(2,1)S(1)} collective-permute-done((bf16[512,256]{1,0:T(8,128)(2,1)S(1)}, bf16[512,256]{1,0:T(8,128)(2,1)S(1)}, u32[]{:S(2)}, u32[]{:S(2)}) %collective-permute-start.11) | collective-permute-done | bytes 262176 | tf_op jit(solution)/shard_map/combine/ppermute | solution.py:20
  84.2 5.6 %collective-permute-done.9 = bf16[512,256]{1,0:T(8,128)(2,1)S(1)} collective-permute-done((bf16[512,256]{1,0:T(8,128)(2,1)S(1)}, bf16[512,256]{1,0:T(8,128)(2,1)S(1)}, u32[]{:S(2)}, u32[]{:S(2)}) %collective-permute-start.9) | collective-permute-done | bytes 262176 | tf_op jit(solution)/shard_map/combine/ppermute | solution.py:20
  89.8 1.2 fusion.9
  91.0 4.0 %collective-permute-start.12 = (bf16[512,256]{1,0:T(8,128)(2,1)S(1)}, bf16[512,256]{1,0:T(8,128)(2,1)S(1)}, u32[]{:S(2)}, u32[]{:S(2)}) collective-permute-start(bf16[512,256]{1,0:T(8,128)(2,1)S(1)} %fusion.9), channel_id=1, source_target_pairs={{0,2},{2,0},{4,6},{6,4},{1,3},{3,1},{5,7},{7,5},{8,10},{10,8},{12,... | collective-permute-start | bytes 786440 | tf_op jit(solution)/shard_map/combine/ppermute | solution.py:20
  95.1 0.7 collective-permute-start.13
  96.1 4.0 %collective-permute-done.12 = bf16[512,256]{1,0:T(8,128)(2,1)S(1)} collective-permute-done((bf16[512,256]{1,0:T(8,128)(2,1)S(1)}, bf16[512,256]{1,0:T(8,128)(2,1)S(1)}, u32[]{:S(2)}, u32[]{:S(2)}) %collective-permute-start.12) | collective-permute-done | bytes 262176 | tf_op jit(solution)/shard_map/combine/ppermute | solution.py:20
  100.1 1.9 fusion.10
  102.0 10.3 %all-to-all-start.1 = ((bf16[16,32,256]{2,1,0:T(8,128)(2,1)}), bf16[16,32,256]{2,1,0:T(8,128)(2,1)S(1)}, u32[]{:S(2)}, u32[]{:S(2)}) async-start(bf16[16,32,256]{2,1,0:T(8,128)(2,1)} %bitcast.4), calls=%async_computation.1 | async-start | bytes 524288 | tf_op jit(solution)/shard_map/combine/all_to_all | solution.py:106
  112.4 12.6 %all-to-all-done.1 = bf16[16,32,256]{2,1,0:T(8,128)(2,1)S(1)} async-done(((bf16[16,32,256]{2,1,0:T(8,128)(2,1)}), bf16[16,32,256]{2,1,0:T(8,128)(2,1)S(1)}, u32[]{:S(2)}, u32[]{:S(2)}) %all-to-all-start.1) | async-done | bytes 262176 | tf_op jit(solution)/shard_map/combine/all_to_all | solution.py:106
  125.4 10.7 %all_to_all.20 = bf16[4,256,256]{2,1,0:T(8,128)(2,1)S(1)} all-to-all(bf16[4,256,256]{2,1,0:T(8,128)(2,1)S(1)} %broadcast_in_dim.45), channel_id=1, replica_groups=mesh['expert'=16,'x'=4,'half'=2,'line'=4,'core'=2] {'x'}, dimensions={0} | all-to-all | bytes 1048576 | tf_op jit(solution)/shard_map/combine/all_to_all | solution.py:167
  136.2 6.3 %collective-permute-start.14 = (bf16[256,256]{1,0:T(8,128)(2,1)S(1)}, bf16[256,256]{1,0:T(8,128)(2,1)S(1)}, u32[]{:S(2)}, u32[]{:S(2)}) collective-permute-start(bf16[256,256]{1,0:T(8,128)(2,1)S(1)} %reduce_sum.31), channel_id=1, source_target_pairs={{0,8},{8,0},{1,9},{9,1},{2,10},{10,2},{3,11},{11,3},{4,12},{12,4},... | collective-permute-start | bytes 393224 | tf_op jit(solution)/shard_map/combine/ppermute | solution.py:66
  142.9 3.0 %collective-permute-done.14 = bf16[256,256]{1,0:T(8,128)(2,1)S(1)} collective-permute-done((bf16[256,256]{1,0:T(8,128)(2,1)S(1)}, bf16[256,256]{1,0:T(8,128)(2,1)S(1)}, u32[]{:S(2)}, u32[]{:S(2)}) %collective-permute-start.14) | collective-permute-done | bytes 131104 | tf_op jit(solution)/shard_map/combine/ppermute | solution.py:66
  145.9 0.9 fusion.12
  146.9 10.0 %all-to-all-start.3 = ((bf16[16,32,256]{2,1,0:T(8,128)(2,1)}), bf16[16,32,256]{2,1,0:T(8,128)(2,1)S(1)}, u32[]{:S(2)}, u32[]{:S(2)}) async-start(bf16[16,32,256]{2,1,0:T(8,128)(2,1)} %bitcast.6), calls=%async_computation.3 | async-start | bytes 524288 | tf_op jit(solution)/shard_map/curvature/all_to_all | solution.py:106
  156.8 5.3 %collective-permute-start.15 = (bf16[256,256]{1,0:T(8,128)(2,1)S(1)}, bf16[256,256]{1,0:T(8,128)(2,1)S(1)}, u32[]{:S(2)}, u32[]{:S(2)}) collective-permute-start(bf16[256,256]{1,0:T(8,128)(2,1)S(1)} %add_convert_fusion.1), channel_id=1, source_target_pairs={{0,2},{2,4},{4,6},{6,8},{8,10},{10,12},{12,14},{14,0},{1,3},{3,5},... | collective-permute-start | bytes 393224 | tf_op jit(solution)/shard_map/tangent/ppermute | solution.py:55
  162.1 1.9 collective-permute-start.16
  164.1 4.0 %collective-permute-start.17 = (bf16[256,256]{1,0:T(8,128)(2,1)S(1)}, bf16[256,256]{1,0:T(8,128)(2,1)S(1)}, u32[]{:S(2)}, u32[]{:S(2)}) collective-permute-start(bf16[256,256]{1,0:T(8,128)(2,1)S(1)} %add_convert_fusion.1), channel_id=1, source_target_pairs={{0,4},{2,6},{4,8},{6,10},{8,12},{10,14},{12,0},{14,2},{1,5},{3,7},... | collective-permute-start | bytes 393224 | tf_op jit(solution)/shard_map/tangent/ppermute | solution.py:55
  168.1 6.8 %collective-permute-done.17 = bf16[256,256]{1,0:T(8,128)(2,1)S(1)} collective-permute-done((bf16[256,256]{1,0:T(8,128)(2,1)S(1)}, bf16[256,256]{1,0:T(8,128)(2,1)S(1)}, u32[]{:S(2)}, u32[]{:S(2)}) %collective-permute-start.17) | collective-permute-done | bytes 131104 | tf_op jit(solution)/shard_map/tangent/ppermute | solution.py:55
  175.0 0.7 collective-permute-start.22
  175.7 3.8 %collective-permute-start.19 = (bf16[512,256]{1,0:T(8,128)(2,1)S(1)}, bf16[512,256]{1,0:T(8,128)(2,1)S(1)}, u32[]{:S(2)}, u32[]{:S(2)}) collective-permute-start(bf16[512,256]{1,0:T(8,128)(2,1)S(1)} %bitcast.54), channel_id=1, source_target_pairs={{0,2},{2,0},{4,6},{6,4},{1,3},{3,1},{5,7},{7,5},{8,10},{10,8},{12,... | collective-permute-start | bytes 786440 | tf_op jit(solution)/shard_map/curvature/ppermute | solution.py:20
  179.5 8.7 %collective-permute-start.18 = (bf16[1024,256]{1,0:T(8,128)(2,1)S(1)}, bf16[1024,256]{1,0:T(8,128)(2,1)S(1)}, u32[]{:S(2)}, u32[]{:S(2)}) collective-permute-start(bf16[1024,256]{1,0:T(8,128)(2,1)S(1)} %pad_maximum_fusion.3), channel_id=1, source_target_pairs={{0,1},{1,0},{2,3},{3,2},{4,5},{5,4},{6,7},{7,6},{8,9},{9,8},{10,11... | collective-permute-start | bytes 1572872 | tf_op jit(solution)/shard_map/tangent/ppermute | solution.py:62
  188.7 0.7 collective-permute-start.20
  189.4 1.3 collective-permute-start.21
  190.7 1.3 collective-permute-start.23
  192.3 13.0 %collective-permute-done.23 = bf16[512,256]{1,0:T(8,128)(2,1)S(1)} collective-permute-done((bf16[512,256]{1,0:T(8,128)(2,1)S(1)}, bf16[512,256]{1,0:T(8,128)(2,1)S(1)}, u32[]{:S(2)}, u32[]{:S(2)}) %collective-permute-start.23) | collective-permute-done | bytes 262176 | tf_op jit(solution)/shard_map/curvature/ppermute | solution.py:20
  205.6 4.0 %collective-permute-start.25 = (bf16[384,256]{1,0:T(8,128)(2,1)S(1)}, bf16[384,256]{1,0:T(8,128)(2,1)S(1)}, u32[]{:S(2)}, u32[]{:S(2)}) collective-permute-start(bf16[384,256]{1,0:T(8,128)(2,1)S(1)} %pad_maximum_fusion.6), channel_id=1, source_target_pairs={{0,1},{1,0},{2,3},{3,2},{4,5},{5,4},{6,7},{7,6},{8,9},{9,8},{10,11... | collective-permute-start | bytes 589832 | tf_op jit(solution)/shard_map/curvature/ppermute | solution.py:62
  209.9 1.9 collective-permute-start.24
  213.3 0.9 copy-done.2
  (108 shorter events, 11.2 us)
Async XLA Ops:
  0.6 2.2 %copy-start = (bf16[256,2048]{1,0:T(8,128)(2,1)S(1)}, bf16[256,2048]{1,0:T(8,128)(2,1)}, u32[]{:S(2)}) copy-start(bf16[256,2048]{1,0:T(8,128)(2,1)} %param.6) | copy-start | bytes 3145732
  0.6 22.6 %copy-start.5 = (bf16[192,2048]{1,0:T(8,128)(2,1)S(1)}, bf16[192,2048]{1,0:T(8,128)(2,1)}, u32[]{:S(2)}) copy-start(bf16[192,2048]{1,0:T(8,128)(2,1)} %param.11) | copy-start | bytes 2359300
  0.7 1.0 copy-start.11
  1.6 24.9 %copy-start.7 = (pred[16,256]{1,0:T(8,128)(4,1)}, pred[16,256]{1,0:T(8,128)(4,1)S(1)}, u32[]{:S(2)}) copy-start(pred[16,256]{1,0:T(8,128)(4,1)S(1)} %compare_reduce_fusion) | copy-start | bytes 12292
  3.8 32.6 %all-to-all-start = ((bf16[16,32,256]{2,1,0:T(8,128)(2,1)}), bf16[16,32,256]{2,1,0:T(8,128)(2,1)S(1)}, u32[]{:S(2)}, u32[]{:S(2)}) async-start(bf16[16,32,256]{2,1,0:T(8,128)(2,1)} %bitcast.2), calls=%async_computation | async-start | bytes 524288 | tf_op jit(solution)/shard_map/dispatch/all_to_all | solution.py:106
  23.3 3.1 %copy-start.3 = (bf16[192,2048]{1,0:T(8,128)(2,1)S(1)}, bf16[192,2048]{1,0:T(8,128)(2,1)}, u32[]{:S(2)}) copy-start(bf16[192,2048]{1,0:T(8,128)(2,1)} %param.10) | copy-start | bytes 2359300
  23.3 3.1 %copy-start.4 = (bf16[192,2048]{1,0:T(8,128)(2,1)S(1)}, bf16[192,2048]{1,0:T(8,128)(2,1)}, u32[]{:S(2)}) copy-start(bf16[192,2048]{1,0:T(8,128)(2,1)} %param.9) | copy-start | bytes 2359300
  23.4 4.5 %collective-permute-start = (bf16[192,1024]{1,0:T(8,128)(2,1)S(1)}, bf16[192,1024]{1,0:T(8,128)(2,1)}, u32[]{:S(2)}, u32[]{:S(2)}) collective-permute-start(bf16[192,1024]{1,0:T(8,128)(2,1)S(1)} %pad_maximum_fusion.4), channel_id=1, source_target_pairs={{0,1},{1,0},{2,3},{3,2},{4,5},{5,4},{6,7},{7,6},{8,9},{9,8},{10,11... | collective-permute-start | bytes 1179656 | tf_op jit(solution)/shard_map/dispatch/ppermute | solution.py:62
  36.3 6.4 %collective-permute-start.2 = (bf16[512,256]{1,0:T(8,128)(2,1)S(1)}, bf16[512,256]{1,0:T(8,128)(2,1)S(1)}, u32[]{:S(2)}, u32[]{:S(2)}) collective-permute-start(bf16[512,256]{1,0:T(8,128)(2,1)S(1)} %bitcast.57), channel_id=1, source_target_pairs={{2,4},{4,2},{3,5},{5,3},{10,12},{12,10},{11,13},{13,11},{18,20},{2... | collective-permute-start | bytes 786440 | tf_op jit(solution)/shard_map/dispatch/ppermute | solution.py:20
  37.0 9.5 %collective-permute-start.1 = (bf16[512,256]{1,0:T(8,128)(2,1)S(1)}, bf16[512,256]{1,0:T(8,128)(2,1)S(1)}, u32[]{:S(2)}, u32[]{:S(2)}) collective-permute-start(bf16[512,256]{1,0:T(8,128)(2,1)S(1)} %bitcast.58), channel_id=1, source_target_pairs={{0,2},{2,0},{4,6},{6,4},{1,3},{3,1},{5,7},{7,5},{8,10},{10,8},{12,... | collective-permute-start | bytes 786440 | tf_op jit(solution)/shard_map/dispatch/ppermute | solution.py:20
  42.8 7.2 %collective-permute-start.3 = (bf16[512,256]{1,0:T(8,128)(2,1)S(1)}, bf16[512,256]{1,0:T(8,128)(2,1)}, u32[]{:S(2)}, u32[]{:S(2)}) collective-permute-start(bf16[512,256]{1,0:T(8,128)(2,1)S(1)} %collective-permute-done.2), channel_id=1, source_target_pairs={{2,0},{4,6},{3,1},{5,7},{10,8},{12,14},{11,9},{13,15},{18,16},{20,... | collective-permute-start | bytes 786440 | tf_op jit(solution)/shard_map/dispatch/ppermute | solution.py:20
  46.5 17.4 %collective-permute-start.4 = (bf16[512,256]{1,0:T(8,128)(2,1)S(1)}, bf16[512,256]{1,0:T(8,128)(2,1)S(1)}, u32[]{:S(2)}, u32[]{:S(2)}) collective-permute-start(bf16[512,256]{1,0:T(8,128)(2,1)S(1)} %collective-permute-done.1), channel_id=1, source_target_pairs={{2,4},{4,2},{3,5},{5,3},{10,12},{12,10},{11,13},{13,11},{18,20},{2... | collective-permute-start | bytes 786440 | tf_op jit(solution)/shard_map/dispatch/ppermute | solution.py:20
  47.2 16.7 %collective-permute-start.5 = (bf16[512,256]{1,0:T(8,128)(2,1)S(1)}, bf16[512,256]{1,0:T(8,128)(2,1)S(1)}, u32[]{:S(2)}, u32[]{:S(2)}) collective-permute-start(bf16[512,256]{1,0:T(8,128)(2,1)S(1)} %collective-permute-done.1), channel_id=1, source_target_pairs={{4,0},{2,6},{5,1},{3,7},{12,8},{10,14},{13,9},{11,15},{20,16},{18,... | collective-permute-start | bytes 786440 | tf_op jit(solution)/shard_map/dispatch/ppermute | solution.py:20
  51.0 17.9 %collective-permute-start.6 = (bf16[1024,256]{1,0:T(8,128)(2,1)S(1)}, bf16[1024,256]{1,0:T(8,128)(2,1)S(1)}, u32[]{:S(2)}, u32[]{:S(2)}) collective-permute-start(bf16[1024,256]{1,0:T(8,128)(2,1)S(1)} %pad_maximum_fusion.1), channel_id=1, source_target_pairs={{0,1},{1,0},{2,3},{3,2},{4,5},{5,4},{6,7},{7,6},{8,9},{9,8},{10,11... | collective-permute-start | bytes 1572872 | tf_op jit(solution)/shard_map/dispatch/ppermute | solution.py:62
  64.0 5.9 %collective-permute-start.7 = (bf16[1024,256]{1,0:T(8,128)(2,1)S(1)}, bf16[1024,256]{1,0:T(8,128)(2,1)S(1)}, u32[]{:S(2)}, u32[]{:S(2)}) collective-permute-start(bf16[1024,256]{1,0:T(8,128)(2,1)S(1)} %pad_maximum_fusion.2), channel_id=1, source_target_pairs={{0,1},{1,0},{2,3},{3,2},{4,5},{5,4},{6,7},{7,6},{8,9},{9,8},{10,11... | collective-permute-start | bytes 1572872 | tf_op jit(solution)/shard_map/dispatch/ppermute | solution.py:62
  70.8 2.8 %copy-start.6 = (bf16[192,2048]{1,0:T(8,128)(2,1)S(1)}, bf16[192,2048]{1,0:T(8,128)(2,1)}, u32[]{:S(2)}) copy-start(bf16[192,2048]{1,0:T(8,128)(2,1)} %param.11) | copy-start | bytes 2359300
  71.3 3.3 %collective-permute-start.8 = (bf16[512,192]{0,1:T(8,128)(2,1)S(1)}, bf16[512,192]{0,1:T(8,128)(2,1)S(1)}, u32[]{:S(2)}, u32[]{:S(2)}) collective-permute-start(bf16[512,192]{0,1:T(8,128)(2,1)S(1)} %fusion.20), channel_id=1, source_target_pairs={{0,1},{1,0},{2,3},{3,2},{4,5},{5,4},{6,7},{7,6},{8,9},{9,8},{10,11... | collective-permute-start | bytes 589832 | tf_op jit(solution)/shard_map/experts/ppermute | solution.py:62
  75.8 6.2 %collective-permute-start.10 = (bf16[512,256]{1,0:T(8,128)(2,1)S(1)}, bf16[512,256]{1,0:T(8,128)(2,1)S(1)}, u32[]{:S(2)}, u32[]{:S(2)}) collective-permute-start(bf16[512,256]{1,0:T(8,128)(2,1)S(1)} %fusion.11), channel_id=1, source_target_pairs={{2,4},{4,2},{3,5},{5,3},{10,12},{12,10},{11,13},{13,11},{18,20},{2... | collective-permute-start | bytes 786440 | tf_op jit(solution)/shard_map/combine/ppermute | solution.py:20
  76.5 7.7 %collective-permute-start.11 = (bf16[512,256]{1,0:T(8,128)(2,1)S(1)}, bf16[512,256]{1,0:T(8,128)(2,1)S(1)}, u32[]{:S(2)}, u32[]{:S(2)}) collective-permute-start(bf16[512,256]{1,0:T(8,128)(2,1)S(1)} %fusion.11), channel_id=1, source_target_pairs={{0,2},{6,4},{1,3},{7,5},{8,10},{14,12},{9,11},{15,13},{16,18},{22,... | collective-permute-start | bytes 786440 | tf_op jit(solution)/shard_map/combine/ppermute | solution.py:20
  80.4 9.4 %collective-permute-start.9 = (bf16[512,256]{1,0:T(8,128)(2,1)S(1)}, bf16[512,256]{1,0:T(8,128)(2,1)S(1)}, u32[]{:S(2)}, u32[]{:S(2)}) collective-permute-start(bf16[512,256]{1,0:T(8,128)(2,1)S(1)} %get-tuple-element.32), channel_id=1, source_target_pairs={{0,4},{6,2},{1,5},{7,3},{8,12},{14,10},{9,13},{15,11},{16,20},{22,... | collective-permute-start | bytes 786440 | tf_op jit(solution)/shard_map/combine/ppermute | solution.py:20
  91.0 9.1 %collective-permute-start.12 = (bf16[512,256]{1,0:T(8,128)(2,1)S(1)}, bf16[512,256]{1,0:T(8,128)(2,1)S(1)}, u32[]{:S(2)}, u32[]{:S(2)}) collective-permute-start(bf16[512,256]{1,0:T(8,128)(2,1)S(1)} %fusion.9), channel_id=1, source_target_pairs={{0,2},{2,0},{4,6},{6,4},{1,3},{3,1},{5,7},{7,5},{8,10},{10,8},{12,... | collective-permute-start | bytes 786440 | tf_op jit(solution)/shard_map/combine/ppermute | solution.py:20
  95.1 17.2 %copy-start.10 = (bf16[256,8]{0,1:T(8,128)(2,1)S(1)}, bf16[256,8]{0,1:T(8,128)(2,1)}, u32[]{:S(2)}) copy-start(bf16[256,8]{0,1:T(8,128)(2,1)} %param.8) | copy-start | bytes 12292
  95.1 17.2 %copy-start.9 = (s32[256,8]{0,1:T(8,128)S(1)}, s32[256,8]{0,1:T(8,128)}, u32[]{:S(2)}) copy-start(s32[256,8]{0,1:T(8,128)} %param.7) | copy-start | bytes 24580
  95.1 17.2 %copy-start.12 = (s32[16]{0:T(128)S(1)}, s32[16]{0:T(128)}, u32[]{:S(2)}) copy-start(s32[16]{0:T(128)} %copy-done.11) | copy-start | bytes 196
  95.1 29.9 %copy-start.8 = (pred[16,256]{1,0:T(8,128)(4,1)S(1)}, pred[16,256]{1,0:T(8,128)(4,1)}, u32[]{:S(2)}) copy-start(pred[16,256]{1,0:T(8,128)(4,1)} %copy-done.7) | copy-start | bytes 12292
  95.1 5.0 %collective-permute-start.13 = (bf16[512,256]{1,0:T(8,128)(2,1)S(1)}, bf16[512,256]{1,0:T(8,128)(2,1)S(1)}, u32[]{:S(2)}, u32[]{:S(2)}) collective-permute-start(bf16[512,256]{1,0:T(8,128)(2,1)S(1)} %add_convert_fusion), channel_id=1, source_target_pairs={{2,4},{4,2},{3,5},{5,3},{10,12},{12,10},{11,13},{13,11},{18,20},{2... | collective-permute-start | bytes 786440 | tf_op jit(solution)/shard_map/combine/ppermute | solution.py:20
  102.0 23.1 %all-to-all-start.1 = ((bf16[16,32,256]{2,1,0:T(8,128)(2,1)}), bf16[16,32,256]{2,1,0:T(8,128)(2,1)S(1)}, u32[]{:S(2)}, u32[]{:S(2)}) async-start(bf16[16,32,256]{2,1,0:T(8,128)(2,1)} %bitcast.4), calls=%async_computation.1 | async-start | bytes 524288 | tf_op jit(solution)/shard_map/combine/all_to_all | solution.py:106
  136.2 9.6 %collective-permute-start.14 = (bf16[256,256]{1,0:T(8,128)(2,1)S(1)}, bf16[256,256]{1,0:T(8,128)(2,1)S(1)}, u32[]{:S(2)}, u32[]{:S(2)}) collective-permute-start(bf16[256,256]{1,0:T(8,128)(2,1)S(1)} %reduce_sum.31), channel_id=1, source_target_pairs={{0,8},{8,0},{1,9},{9,1},{2,10},{10,2},{3,11},{11,3},{4,12},{12,4},... | collective-permute-start | bytes 393224 | tf_op jit(solution)/shard_map/combine/ppermute | solution.py:66
  146.9 28.1 %all-to-all-start.3 = ((bf16[16,32,256]{2,1,0:T(8,128)(2,1)}), bf16[16,32,256]{2,1,0:T(8,128)(2,1)S(1)}, u32[]{:S(2)}, u32[]{:S(2)}) async-start(bf16[16,32,256]{2,1,0:T(8,128)(2,1)} %bitcast.6), calls=%async_computation.3 | async-start | bytes 524288 | tf_op jit(solution)/shard_map/curvature/all_to_all | solution.py:106
  156.8 11.3 %collective-permute-start.15 = (bf16[256,256]{1,0:T(8,128)(2,1)S(1)}, bf16[256,256]{1,0:T(8,128)(2,1)S(1)}, u32[]{:S(2)}, u32[]{:S(2)}) collective-permute-start(bf16[256,256]{1,0:T(8,128)(2,1)S(1)} %add_convert_fusion.1), channel_id=1, source_target_pairs={{0,2},{2,4},{4,6},{6,8},{8,10},{10,12},{12,14},{14,0},{1,3},{3,5},... | collective-permute-start | bytes 393224 | tf_op jit(solution)/shard_map/tangent/ppermute | solution.py:55
  162.1 6.0 %collective-permute-start.16 = (bf16[256,256]{1,0:T(8,128)(2,1)S(1)}, bf16[256,256]{1,0:T(8,128)(2,1)S(1)}, u32[]{:S(2)}, u32[]{:S(2)}) collective-permute-start(bf16[256,256]{1,0:T(8,128)(2,1)S(1)} %add_convert_fusion.1), channel_id=1, source_target_pairs={{0,14},{2,0},{4,2},{6,4},{8,6},{10,8},{12,10},{14,12},{1,15},{3,1}... | collective-permute-start | bytes 393224 | tf_op jit(solution)/shard_map/tangent/ppermute | solution.py:55
  164.1 10.9 %collective-permute-start.17 = (bf16[256,256]{1,0:T(8,128)(2,1)S(1)}, bf16[256,256]{1,0:T(8,128)(2,1)S(1)}, u32[]{:S(2)}, u32[]{:S(2)}) collective-permute-start(bf16[256,256]{1,0:T(8,128)(2,1)S(1)} %add_convert_fusion.1), channel_id=1, source_target_pairs={{0,4},{2,6},{4,8},{6,10},{8,12},{10,14},{12,0},{14,2},{1,5},{3,7},... | collective-permute-start | bytes 393224 | tf_op jit(solution)/shard_map/tangent/ppermute | solution.py:55
  175.0 15.7 %collective-permute-start.22 = (bf16[512,256]{1,0:T(8,128)(2,1)S(1)}, bf16[512,256]{1,0:T(8,128)(2,1)S(1)}, u32[]{:S(2)}, u32[]{:S(2)}) collective-permute-start(bf16[512,256]{1,0:T(8,128)(2,1)S(1)} %bitcast.53), channel_id=1, source_target_pairs={{2,4},{4,2},{3,5},{5,3},{10,12},{12,10},{11,13},{13,11},{18,20},{2... | collective-permute-start | bytes 786440 | tf_op jit(solution)/shard_map/curvature/ppermute | solution.py:20
  175.7 13.0 %collective-permute-start.19 = (bf16[512,256]{1,0:T(8,128)(2,1)S(1)}, bf16[512,256]{1,0:T(8,128)(2,1)S(1)}, u32[]{:S(2)}, u32[]{:S(2)}) collective-permute-start(bf16[512,256]{1,0:T(8,128)(2,1)S(1)} %bitcast.54), channel_id=1, source_target_pairs={{0,2},{2,0},{4,6},{6,4},{1,3},{3,1},{5,7},{7,5},{8,10},{10,8},{12,... | collective-permute-start | bytes 786440 | tf_op jit(solution)/shard_map/curvature/ppermute | solution.py:20
  179.5 12.7 %collective-permute-start.18 = (bf16[1024,256]{1,0:T(8,128)(2,1)S(1)}, bf16[1024,256]{1,0:T(8,128)(2,1)S(1)}, u32[]{:S(2)}, u32[]{:S(2)}) collective-permute-start(bf16[1024,256]{1,0:T(8,128)(2,1)S(1)} %pad_maximum_fusion.3), channel_id=1, source_target_pairs={{0,1},{1,0},{2,3},{3,2},{4,5},{5,4},{6,7},{7,6},{8,9},{9,8},{10,11... | collective-permute-start | bytes 1572872 | tf_op jit(solution)/shard_map/tangent/ppermute | solution.py:62
  188.7 20.9 %collective-permute-start.20 = (bf16[512,256]{1,0:T(8,128)(2,1)S(1)}, bf16[512,256]{1,0:T(8,128)(2,1)S(1)}, u32[]{:S(2)}, u32[]{:S(2)}) collective-permute-start(bf16[512,256]{1,0:T(8,128)(2,1)S(1)} %collective-permute-done.19), channel_id=1, source_target_pairs={{2,4},{4,2},{3,5},{5,3},{10,12},{12,10},{11,13},{13,11},{18,20},{2... | collective-permute-start | bytes 786440 | tf_op jit(solution)/shard_map/curvature/ppermute | solution.py:20
  189.4 20.3 %collective-permute-start.21 = (bf16[512,256]{1,0:T(8,128)(2,1)S(1)}, bf16[512,256]{1,0:T(8,128)(2,1)S(1)}, u32[]{:S(2)}, u32[]{:S(2)}) collective-permute-start(bf16[512,256]{1,0:T(8,128)(2,1)S(1)} %collective-permute-done.19), channel_id=1, source_target_pairs={{4,0},{2,6},{5,1},{3,7},{12,8},{10,14},{13,9},{11,15},{20,16},{18,... | collective-permute-start | bytes 786440 | tf_op jit(solution)/shard_map/curvature/ppermute | solution.py:20
  190.7 14.7 %collective-permute-start.23 = (bf16[512,256]{1,0:T(8,128)(2,1)S(1)}, bf16[512,256]{1,0:T(8,128)(2,1)S(1)}, u32[]{:S(2)}, u32[]{:S(2)}) collective-permute-start(bf16[512,256]{1,0:T(8,128)(2,1)S(1)} %collective-permute-done.22), channel_id=1, source_target_pairs={{2,0},{4,6},{3,1},{5,7},{10,8},{12,14},{11,9},{13,15},{18,16},{20,... | collective-permute-start | bytes 786440 | tf_op jit(solution)/shard_map/curvature/ppermute | solution.py:20
  192.3 19.6 %copy-start.1 = (bf16[256,2048]{1,0:T(8,128)(2,1)}, bf16[256,2048]{1,0:T(8,128)(2,1)S(1)}, u32[]{:S(2)}) copy-start(bf16[256,2048]{1,0:T(8,128)(2,1)S(1)} %slice_dynamic-update-slice_fusion) | copy-start | bytes 3145732
  205.6 7.7 %collective-permute-start.25 = (bf16[384,256]{1,0:T(8,128)(2,1)S(1)}, bf16[384,256]{1,0:T(8,128)(2,1)S(1)}, u32[]{:S(2)}, u32[]{:S(2)}) collective-permute-start(bf16[384,256]{1,0:T(8,128)(2,1)S(1)} %pad_maximum_fusion.6), channel_id=1, source_target_pairs={{0,1},{1,0},{2,3},{3,2},{4,5},{5,4},{6,7},{7,6},{8,9},{9,8},{10,11... | collective-permute-start | bytes 589832 | tf_op jit(solution)/shard_map/curvature/ppermute | solution.py:62
  209.9 3.3 %collective-permute-start.24 = (bf16[384,256]{1,0:T(8,128)(2,1)S(1)}, bf16[384,256]{1,0:T(8,128)(2,1)S(1)}, u32[]{:S(2)}, u32[]{:S(2)}) collective-permute-start(bf16[384,256]{1,0:T(8,128)(2,1)S(1)} %pad_maximum_fusion.5), channel_id=1, source_target_pairs={{0,1},{1,0},{2,3},{3,2},{4,5},{5,4},{6,7},{7,6},{8,9},{9,8},{10,11... | collective-permute-start | bytes 589832 | tf_op jit(solution)/shard_map/curvature/ppermute | solution.py:62
  213.3 0.9 copy-start.2

commit v8 on v7

--- a/solution.py
+++ b/solution.py
@@ -150,16 +150,13 @@
         hidden_other = swap_cores(hidden)
 
     with jax.named_scope("combine"):
+        other_out = jnp.dot(hidden_other, direction_other, preferred_element_type=jnp.float32)
+
         def pair_out(mask):
             own = jnp.dot(
                 hidden, columns(direction, line_index ^ mask, 0), preferred_element_type=jnp.float32
             )
-            other = jnp.dot(
-                hidden_other,
-                direction_other[:, mask * cols : (mask + 1) * cols],
-                preferred_element_type=jnp.float32,
-            )
-            return own + other
+            return own + other_out[:, mask * cols : (mask + 1) * cols]
 
         expert_out = reduce_line([pair_out(mask) for mask in range(LINE)])
         returned = over_planes(expert_out.astype(jnp.bfloat16))
@@ -185,6 +182,7 @@
 
     with jax.named_scope("curvature"):
         scaled_blocks = gather_line(moved)
+        scaled_blocks[1], *pieces = lax.optimization_barrier((scaled_blocks[1], *pieces))
 
     with jax.named_scope("curvature"):
         def products(units):

time: 215 us -> 216 us (level)
  waiting for transfers between devices: 62.3 us -> 66.9 us
  matrix products: 12.9 us -> 9.68 us
    ppermute x15, waiting for transfers between devices: 28.5 us -> 32.8 us  [send_line(): return lax.ppermute(value, 'line', pairs)]
    dot_general x4 -> x1, matrix products: 5.4 us -> 1.46 us  [shards(): jnp.dot(hidden_other, direction_other, preferred_element_type=jnp.float32)]
  transfers between devices with their start and end apart: 29 -> 29, of which waited for: 14 -> 17; matrix products, arithmetic and copies ran while one was open for 3% -> 3% of each run, Pallas kernels for 0% -> 0%
where the time goes in v8:
time: 216 us; the launch traced here: 215 us
  starting transfers between devices  119 us (55%)
  waiting for transfers between devices  66.9 us (31%)
  blocking collectives  10.7 us (5%)
  matrix products  9.68 us (4%)
  other arithmetic  3.98 us (2%)
  local copies, waits for them, and re-layouts  2.63 us (1%)
    all_to_all x3, starting transfers between devices, over_planes(): lax.all_to_all(slots.reshape(n_expert, slot_count, cols), 'expert', 0, 0,...  39.6 us
    ppermute x7, starting transfers between devices, swap_cores(): return lax.ppermute(value, 'core', [(i, i ^ 1) for i in range(CORES)])  37.4 us
    ppermute x15, waiting for transfers between devices, send_line(): return lax.ppermute(value, 'line', pairs)  32.8 us
    ppermute x15, starting transfers between devices, send_line(): return lax.ppermute(value, 'line', pairs)  24.9 us
    all_to_all x3, waiting for transfers between devices, over_planes(): lax.all_to_all(slots.reshape(n_expert, slot_count, cols), 'expert', 0, 0,...  21.1 us
    ppermute x3, starting transfers between devices, gather_ring(): lax.ppermute(block, ('half', 'line'), [(i, (i + step) % ring) for i in ra...  11.1 us
    all_to_all x1, blocking collectives, shards(): lax.all_to_all(jnp.broadcast_to(part, (EXP_COL // HALVES, col_tok, cols))...  10.7 us
    ppermute x3, waiting for transfers between devices, gather_ring(): lax.ppermute(block, ('half', 'line'), [(i, (i + step) % ring) for i in ra...  6.96 us
  transfers between devices with their start and end apart: 29, of which 17 were waited for; matrix products, arithmetic and copies ran while one was open for 3% of the time, Pallas kernels for 0%

profile of v8, /device:TPU:1, one launch (start us, length us, event | category | flops | bytes accessed | tf_op | source)
XLA Modules:
  0.0 214.8 jit_solution(9905759710508059712)
XLA Ops:
  0.7 0.9 compare_reduce_fusion
  2.8 1.0 convolution_convert_fusion
  3.8 19.4 %all-to-all-start = ((bf16[16,32,256]{2,1,0:T(8,128)(2,1)}), bf16[16,32,256]{2,1,0:T(8,128)(2,1)S(1)}, u32[]{:S(2)}, u32[]{:S(2)}) async-start(bf16[16,32,256]{2,1,0:T(8,128)(2,1)} %bitcast.2), calls=%async_computation | async-start | bytes 524288 | tf_op jit(solution)/shard_map/dispatch/all_to_all | solution.py:106
  23.4 3.0 %collective-permute-start = (bf16[192,1024]{1,0:T(8,128)(2,1)S(1)}, bf16[192,1024]{1,0:T(8,128)(2,1)}, u32[]{:S(2)}, u32[]{:S(2)}) collective-permute-start(bf16[192,1024]{1,0:T(8,128)(2,1)S(1)} %pad_maximum_fusion.4), channel_id=1, source_target_pairs={{0,1},{1,0},{2,3},{3,2},{4,5},{5,4},{6,7},{7,6},{8,9},{9,8},{10,11... | collective-permute-start | bytes 1179656 | tf_op jit(solution)/shard_map/dispatch/ppermute | solution.py:62
  26.5 1.3 collective-permute-done
  27.9 8.5 %all-to-all-done = bf16[16,32,256]{2,1,0:T(8,128)(2,1)S(1)} async-done(((bf16[16,32,256]{2,1,0:T(8,128)(2,1)}), bf16[16,32,256]{2,1,0:T(8,128)(2,1)S(1)}, u32[]{:S(2)}, u32[]{:S(2)}) %all-to-all-start) | async-done | bytes 262176 | tf_op jit(solution)/shard_map/dispatch/all_to_all | solution.py:106
  37.0 5.7 %collective-permute-start.1 = (bf16[512,256]{1,0:T(8,128)(2,1)S(1)}, bf16[512,256]{1,0:T(8,128)(2,1)S(1)}, u32[]{:S(2)}, u32[]{:S(2)}) collective-permute-start(bf16[512,256]{1,0:T(8,128)(2,1)S(1)} %bitcast.56), channel_id=1, source_target_pairs={{0,2},{2,0},{4,6},{6,4},{1,3},{3,1},{5,7},{7,5},{8,10},{10,8},{12,... | collective-permute-start | bytes 786440 | tf_op jit(solution)/shard_map/dispatch/ppermute | solution.py:20
  42.8 1.3 collective-permute-start.3
  44.1 2.4 %collective-permute-done.1 = bf16[512,256]{1,0:T(8,128)(2,1)S(1)} collective-permute-done((bf16[512,256]{1,0:T(8,128)(2,1)S(1)}, bf16[512,256]{1,0:T(8,128)(2,1)S(1)}, u32[]{:S(2)}, u32[]{:S(2)}) %collective-permute-start.1) | collective-permute-done | bytes 262176 | tf_op jit(solution)/shard_map/dispatch/ppermute | solution.py:20
  47.2 1.3 collective-permute-start.5
  48.8 1.2 collective-permute-done.3
  50.0 1.0 add.252
  51.0 12.8 %collective-permute-start.6 = (bf16[1024,256]{1,0:T(8,128)(2,1)S(1)}, bf16[1024,256]{1,0:T(8,128)(2,1)S(1)}, u32[]{:S(2)}, u32[]{:S(2)}) collective-permute-start(bf16[1024,256]{1,0:T(8,128)(2,1)S(1)} %pad_maximum_fusion.1), channel_id=1, source_target_pairs={{0,1},{1,0},{2,3},{3,2},{4,5},{5,4},{6,7},{7,6},{8,9},{9,8},{10,11... | collective-permute-start | bytes 1572872 | tf_op jit(solution)/shard_map/dispatch/ppermute | solution.py:62
  64.0 4.4 %collective-permute-start.7 = (bf16[1024,256]{1,0:T(8,128)(2,1)S(1)}, bf16[1024,256]{1,0:T(8,128)(2,1)S(1)}, u32[]{:S(2)}, u32[]{:S(2)}) collective-permute-start(bf16[1024,256]{1,0:T(8,128)(2,1)S(1)} %pad_maximum_fusion.2), channel_id=1, source_target_pairs={{0,1},{1,0},{2,3},{3,2},{4,5},{5,4},{6,7},{7,6},{8,9},{9,8},{10,11... | collective-permute-start | bytes 1572872 | tf_op jit(solution)/shard_map/dispatch/ppermute | solution.py:62
  71.3 2.4 %collective-permute-start.8 = (bf16[512,192]{0,1:T(8,128)(2,1)S(1)}, bf16[512,192]{0,1:T(8,128)(2,1)S(1)}, u32[]{:S(2)}, u32[]{:S(2)}) collective-permute-start(bf16[512,192]{0,1:T(8,128)(2,1)S(1)} %fusion.20), channel_id=1, source_target_pairs={{0,1},{1,0},{2,3},{3,2},{4,5},{5,4},{6,7},{7,6},{8,9},{9,8},{10,11... | collective-permute-start | bytes 589832 | tf_op jit(solution)/shard_map/experts/ppermute | solution.py:62
  73.8 1.0 collective-permute-done.8
  74.8 1.5 fusion.74
  76.6 0.7 collective-permute-start.10
  77.2 2.7 %collective-permute-start.11 = (bf16[512,256]{1,0:T(8,128)(2,1)S(1)}, bf16[512,256]{1,0:T(8,128)(2,1)S(1)}, u32[]{:S(2)}, u32[]{:S(2)}) collective-permute-start(bf16[512,256]{1,0:T(8,128)(2,1)S(1)} %fusion.11), channel_id=1, source_target_pairs={{0,2},{6,4},{1,3},{7,5},{8,10},{14,12},{9,11},{15,13},{16,18},{22,... | collective-permute-start | bytes 786440 | tf_op jit(solution)/shard_map/combine/ppermute | solution.py:20
  80.2 1.3 collective-permute-start.9
  81.9 3.1 %collective-permute-done.11 = bf16[512,256]{1,0:T(8,128)(2,1)S(1)} collective-permute-done((bf16[512,256]{1,0:T(8,128)(2,1)S(1)}, bf16[512,256]{1,0:T(8,128)(2,1)S(1)}, u32[]{:S(2)}, u32[]{:S(2)}) %collective-permute-start.11) | collective-permute-done | bytes 262176 | tf_op jit(solution)/shard_map/combine/ppermute | solution.py:20
  84.9 5.6 %collective-permute-done.9 = bf16[512,256]{1,0:T(8,128)(2,1)S(1)} collective-permute-done((bf16[512,256]{1,0:T(8,128)(2,1)S(1)}, bf16[512,256]{1,0:T(8,128)(2,1)S(1)}, u32[]{:S(2)}, u32[]{:S(2)}) %collective-permute-start.9) | collective-permute-done | bytes 262176 | tf_op jit(solution)/shard_map/combine/ppermute | solution.py:20
  90.9 4.0 %collective-permute-start.12 = (bf16[512,256]{1,0:T(8,128)(2,1)S(1)}, bf16[512,256]{1,0:T(8,128)(2,1)S(1)}, u32[]{:S(2)}, u32[]{:S(2)}) collective-permute-start(bf16[512,256]{1,0:T(8,128)(2,1)S(1)} %get-tuple-element.38), channel_id=1, source_target_pairs={{0,2},{2,0},{4,6},{6,4},{1,3},{3,1},{5,7},{7,5},{8,10},{10,8},{12,... | collective-permute-start | bytes 786440 | tf_op jit(solution)/shard_map/combine/ppermute | solution.py:20
  94.9 0.7 collective-permute-start.13
  95.6 4.4 %collective-permute-done.12 = bf16[512,256]{1,0:T(8,128)(2,1)S(1)} collective-permute-done((bf16[512,256]{1,0:T(8,128)(2,1)S(1)}, bf16[512,256]{1,0:T(8,128)(2,1)S(1)}, u32[]{:S(2)}, u32[]{:S(2)}) %collective-permute-start.12) | collective-permute-done | bytes 262176 | tf_op jit(solution)/shard_map/combine/ppermute | solution.py:20
  100.0 1.0 fusion.17
  101.0 10.3 %all-to-all-start.1 = ((bf16[16,32,256]{2,1,0:T(8,128)(2,1)}), bf16[16,32,256]{2,1,0:T(8,128)(2,1)S(1)}, u32[]{:S(2)}, u32[]{:S(2)}) async-start(bf16[16,32,256]{2,1,0:T(8,128)(2,1)} %bitcast.4), calls=%async_computation.1 | async-start | bytes 524288 | tf_op jit(solution)/shard_map/combine/all_to_all | solution.py:106
  111.4 12.6 %all-to-all-done.1 = bf16[16,32,256]{2,1,0:T(8,128)(2,1)S(1)} async-done(((bf16[16,32,256]{2,1,0:T(8,128)(2,1)}), bf16[16,32,256]{2,1,0:T(8,128)(2,1)S(1)}, u32[]{:S(2)}, u32[]{:S(2)}) %all-to-all-start.1) | async-done | bytes 262176 | tf_op jit(solution)/shard_map/combine/all_to_all | solution.py:106
  124.4 10.7 %all_to_all.20 = bf16[4,256,256]{2,1,0:T(8,128)(2,1)S(1)} all-to-all(bf16[4,256,256]{2,1,0:T(8,128)(2,1)S(1)} %broadcast_in_dim.45), channel_id=1, replica_groups=mesh['expert'=16,'x'=4,'half'=2,'line'=4,'core'=2] {'x'}, dimensions={0} | all-to-all | bytes 1048576 | tf_op jit(solution)/shard_map/combine/all_to_all | solution.py:164
  135.2 6.3 %collective-permute-start.14 = (bf16[256,256]{1,0:T(8,128)(2,1)S(1)}, bf16[256,256]{1,0:T(8,128)(2,1)S(1)}, u32[]{:S(2)}, u32[]{:S(2)}) collective-permute-start(bf16[256,256]{1,0:T(8,128)(2,1)S(1)} %reduce_sum.31), channel_id=1, source_target_pairs={{0,8},{8,0},{1,9},{9,1},{2,10},{10,2},{3,11},{11,3},{4,12},{12,4},... | collective-permute-start | bytes 393224 | tf_op jit(solution)/shard_map/combine/ppermute | solution.py:66
  141.8 3.0 %collective-permute-done.14 = bf16[256,256]{1,0:T(8,128)(2,1)S(1)} collective-permute-done((bf16[256,256]{1,0:T(8,128)(2,1)S(1)}, bf16[256,256]{1,0:T(8,128)(2,1)S(1)}, u32[]{:S(2)}, u32[]{:S(2)}) %collective-permute-start.14) | collective-permute-done | bytes 131104 | tf_op jit(solution)/shard_map/combine/ppermute | solution.py:66
  144.9 0.9 fusion.5
  145.8 9.9 %all-to-all-start.3 = ((bf16[16,32,256]{2,1,0:T(8,128)(2,1)}), bf16[16,32,256]{2,1,0:T(8,128)(2,1)S(1)}, u32[]{:S(2)}, u32[]{:S(2)}) async-start(bf16[16,32,256]{2,1,0:T(8,128)(2,1)} %bitcast.6), calls=%async_computation.3 | async-start | bytes 524288 | tf_op jit(solution)/shard_map/curvature/all_to_all | solution.py:106
  155.8 5.3 %collective-permute-start.15 = (bf16[256,256]{1,0:T(8,128)(2,1)S(1)}, bf16[256,256]{1,0:T(8,128)(2,1)S(1)}, u32[]{:S(2)}, u32[]{:S(2)}) collective-permute-start(bf16[256,256]{1,0:T(8,128)(2,1)S(1)} %add_convert_fusion.1), channel_id=1, source_target_pairs={{0,2},{2,4},{4,6},{6,8},{8,10},{10,12},{12,14},{14,0},{1,3},{3,5},... | collective-permute-start | bytes 393224 | tf_op jit(solution)/shard_map/tangent/ppermute | solution.py:55
  161.1 1.9 collective-permute-start.16
  163.0 3.9 %collective-permute-start.17 = (bf16[256,256]{1,0:T(8,128)(2,1)S(1)}, bf16[256,256]{1,0:T(8,128)(2,1)S(1)}, u32[]{:S(2)}, u32[]{:S(2)}) collective-permute-start(bf16[256,256]{1,0:T(8,128)(2,1)S(1)} %add_convert_fusion.1), channel_id=1, source_target_pairs={{0,4},{2,6},{4,8},{6,10},{8,12},{10,14},{12,0},{14,2},{1,5},{3,7},... | collective-permute-start | bytes 393224 | tf_op jit(solution)/shard_map/tangent/ppermute | solution.py:55
  167.1 6.8 %collective-permute-done.17 = bf16[256,256]{1,0:T(8,128)(2,1)S(1)} collective-permute-done((bf16[256,256]{1,0:T(8,128)(2,1)S(1)}, bf16[256,256]{1,0:T(8,128)(2,1)S(1)}, u32[]{:S(2)}, u32[]{:S(2)}) %collective-permute-start.17) | collective-permute-done | bytes 131104 | tf_op jit(solution)/shard_map/tangent/ppermute | solution.py:55
  173.9 1.9 collective-permute-start.18
  176.7 4.3 %collective-permute-done.18 = bf16[512,256]{1,0:T(8,128)(2,1)S(1)} collective-permute-done((bf16[512,256]{1,0:T(8,128)(2,1)S(1)}, bf16[512,256]{1,0:T(8,128)(2,1)S(1)}, u32[]{:S(2)}, u32[]{:S(2)}) %collective-permute-start.18) | collective-permute-done | bytes 262176 | tf_op jit(solution)/shard_map/curvature/ppermute | solution.py:20
  181.0 9.1 %collective-permute-start.19 = (bf16[1024,256]{1,0:T(8,128)(2,1)S(1)}, bf16[1024,256]{1,0:T(8,128)(2,1)S(1)}, u32[]{:S(2)}, u32[]{:S(2)}) collective-permute-start(bf16[1024,256]{1,0:T(8,128)(2,1)S(1)} %pad_maximum_fusion.3), channel_id=1, source_target_pairs={{0,1},{1,0},{2,3},{3,2},{4,5},{5,4},{6,7},{7,6},{8,9},{9,8},{10,11... | collective-permute-start | bytes 1572872 | tf_op jit(solution)/shard_map/tangent/ppermute | solution.py:62
  190.3 1.3 collective-permute-start.23
  192.3 1.3 collective-permute-start.21
  193.8 6.3 %collective-permute-done.23 = bf16[512,256]{1,0:T(8,128)(2,1)S(1)} collective-permute-done((bf16[512,256]{1,0:T(8,128)(2,1)S(1)}, bf16[512,256]{1,0:T(8,128)(2,1)S(1)}, u32[]{:S(2)}, u32[]{:S(2)}) %collective-permute-start.23) | collective-permute-done | bytes 262176 | tf_op jit(solution)/shard_map/curvature/ppermute | solution.py:20
  200.4 2.7 %collective-permute-start.25 = (bf16[384,256]{1,0:T(8,128)(2,1)S(1)}, bf16[384,256]{1,0:T(8,128)(2,1)S(1)}, u32[]{:S(2)}, u32[]{:S(2)}) collective-permute-start(bf16[384,256]{1,0:T(8,128)(2,1)S(1)} %pad_maximum_fusion.6), channel_id=1, source_target_pairs={{0,1},{1,0},{2,3},{3,2},{4,5},{5,4},{6,7},{7,6},{8,9},{9,8},{10,11... | collective-permute-start | bytes 589832 | tf_op jit(solution)/shard_map/curvature/ppermute | solution.py:62
  203.1 5.5 %collective-permute-done.21 = bf16[512,256]{1,0:T(8,128)(2,1)S(1)} collective-permute-done((bf16[512,256]{1,0:T(8,128)(2,1)S(1)}, bf16[512,256]{1,0:T(8,128)(2,1)S(1)}, u32[]{:S(2)}, u32[]{:S(2)}) %collective-permute-start.21) | collective-permute-done | bytes 262176 | tf_op jit(solution)/shard_map/curvature/ppermute | solution.py:20
  208.8 3.0 %collective-permute-start.24 = (bf16[384,256]{1,0:T(8,128)(2,1)S(1)}, bf16[384,256]{1,0:T(8,128)(2,1)S(1)}, u32[]{:S(2)}, u32[]{:S(2)}) collective-permute-start(bf16[384,256]{1,0:T(8,128)(2,1)S(1)} %pad_maximum_fusion.5), channel_id=1, source_target_pairs={{0,1},{1,0},{2,3},{3,2},{4,5},{5,4},{6,7},{7,6},{8,9},{9,8},{10,11... | collective-permute-start | bytes 589832 | tf_op jit(solution)/shard_map/curvature/ppermute | solution.py:62
  213.1 0.8 copy-done.2
  213.9 1.0 copy-done.1
  (105 shorter events, 11.8 us)
Async XLA Ops:
  0.6 2.2 %copy-start = (bf16[256,2048]{1,0:T(8,128)(2,1)S(1)}, bf16[256,2048]{1,0:T(8,128)(2,1)}, u32[]{:S(2)}) copy-start(bf16[256,2048]{1,0:T(8,128)(2,1)} %param.6) | copy-start | bytes 3145732
  0.6 22.6 %copy-start.5 = (bf16[192,2048]{1,0:T(8,128)(2,1)S(1)}, bf16[192,2048]{1,0:T(8,128)(2,1)}, u32[]{:S(2)}) copy-start(bf16[192,2048]{1,0:T(8,128)(2,1)} %param.11) | copy-start | bytes 2359300
  0.7 1.0 copy-start.11
  1.6 24.9 %copy-start.7 = (pred[16,256]{1,0:T(8,128)(4,1)}, pred[16,256]{1,0:T(8,128)(4,1)S(1)}, u32[]{:S(2)}) copy-start(pred[16,256]{1,0:T(8,128)(4,1)S(1)} %compare_reduce_fusion) | copy-start | bytes 12292
  3.8 32.6 %all-to-all-start = ((bf16[16,32,256]{2,1,0:T(8,128)(2,1)}), bf16[16,32,256]{2,1,0:T(8,128)(2,1)S(1)}, u32[]{:S(2)}, u32[]{:S(2)}) async-start(bf16[16,32,256]{2,1,0:T(8,128)(2,1)} %bitcast.2), calls=%async_computation | async-start | bytes 524288 | tf_op jit(solution)/shard_map/dispatch/all_to_all | solution.py:106
  23.3 3.1 %copy-start.3 = (bf16[192,2048]{1,0:T(8,128)(2,1)S(1)}, bf16[192,2048]{1,0:T(8,128)(2,1)}, u32[]{:S(2)}) copy-start(bf16[192,2048]{1,0:T(8,128)(2,1)} %param.10) | copy-start | bytes 2359300
  23.3 3.1 %copy-start.4 = (bf16[192,2048]{1,0:T(8,128)(2,1)S(1)}, bf16[192,2048]{1,0:T(8,128)(2,1)}, u32[]{:S(2)}) copy-start(bf16[192,2048]{1,0:T(8,128)(2,1)} %param.9) | copy-start | bytes 2359300
  23.4 4.5 %collective-permute-start = (bf16[192,1024]{1,0:T(8,128)(2,1)S(1)}, bf16[192,1024]{1,0:T(8,128)(2,1)}, u32[]{:S(2)}, u32[]{:S(2)}) collective-permute-start(bf16[192,1024]{1,0:T(8,128)(2,1)S(1)} %pad_maximum_fusion.4), channel_id=1, source_target_pairs={{0,1},{1,0},{2,3},{3,2},{4,5},{5,4},{6,7},{7,6},{8,9},{9,8},{10,11... | collective-permute-start | bytes 1179656 | tf_op jit(solution)/shard_map/dispatch/ppermute | solution.py:62
  36.3 6.4 %collective-permute-start.2 = (bf16[512,256]{1,0:T(8,128)(2,1)S(1)}, bf16[512,256]{1,0:T(8,128)(2,1)S(1)}, u32[]{:S(2)}, u32[]{:S(2)}) collective-permute-start(bf16[512,256]{1,0:T(8,128)(2,1)S(1)} %bitcast.55), channel_id=1, source_target_pairs={{2,4},{4,2},{3,5},{5,3},{10,12},{12,10},{11,13},{13,11},{18,20},{2... | collective-permute-start | bytes 786440 | tf_op jit(solution)/shard_map/dispatch/ppermute | solution.py:20
  37.0 9.5 %collective-permute-start.1 = (bf16[512,256]{1,0:T(8,128)(2,1)S(1)}, bf16[512,256]{1,0:T(8,128)(2,1)S(1)}, u32[]{:S(2)}, u32[]{:S(2)}) collective-permute-start(bf16[512,256]{1,0:T(8,128)(2,1)S(1)} %bitcast.56), channel_id=1, source_target_pairs={{0,2},{2,0},{4,6},{6,4},{1,3},{3,1},{5,7},{7,5},{8,10},{10,8},{12,... | collective-permute-start | bytes 786440 | tf_op jit(solution)/shard_map/dispatch/ppermute | solution.py:20
  42.8 7.2 %collective-permute-start.3 = (bf16[512,256]{1,0:T(8,128)(2,1)S(1)}, bf16[512,256]{1,0:T(8,128)(2,1)}, u32[]{:S(2)}, u32[]{:S(2)}) collective-permute-start(bf16[512,256]{1,0:T(8,128)(2,1)S(1)} %collective-permute-done.2), channel_id=1, source_target_pairs={{2,0},{4,6},{3,1},{5,7},{10,8},{12,14},{11,9},{13,15},{18,16},{20,... | collective-permute-start | bytes 786440 | tf_op jit(solution)/shard_map/dispatch/ppermute | solution.py:20
  46.5 17.4 %collective-permute-start.4 = (bf16[512,256]{1,0:T(8,128)(2,1)S(1)}, bf16[512,256]{1,0:T(8,128)(2,1)S(1)}, u32[]{:S(2)}, u32[]{:S(2)}) collective-permute-start(bf16[512,256]{1,0:T(8,128)(2,1)S(1)} %collective-permute-done.1), channel_id=1, source_target_pairs={{2,4},{4,2},{3,5},{5,3},{10,12},{12,10},{11,13},{13,11},{18,20},{2... | collective-permute-start | bytes 786440 | tf_op jit(solution)/shard_map/dispatch/ppermute | solution.py:20
  47.2 16.7 %collective-permute-start.5 = (bf16[512,256]{1,0:T(8,128)(2,1)S(1)}, bf16[512,256]{1,0:T(8,128)(2,1)S(1)}, u32[]{:S(2)}, u32[]{:S(2)}) collective-permute-start(bf16[512,256]{1,0:T(8,128)(2,1)S(1)} %collective-permute-done.1), channel_id=1, source_target_pairs={{4,0},{2,6},{5,1},{3,7},{12,8},{10,14},{13,9},{11,15},{20,16},{18,... | collective-permute-start | bytes 786440 | tf_op jit(solution)/shard_map/dispatch/ppermute | solution.py:20
  51.0 17.9 %collective-permute-start.6 = (bf16[1024,256]{1,0:T(8,128)(2,1)S(1)}, bf16[1024,256]{1,0:T(8,128)(2,1)S(1)}, u32[]{:S(2)}, u32[]{:S(2)}) collective-permute-start(bf16[1024,256]{1,0:T(8,128)(2,1)S(1)} %pad_maximum_fusion.1), channel_id=1, source_target_pairs={{0,1},{1,0},{2,3},{3,2},{4,5},{5,4},{6,7},{7,6},{8,9},{9,8},{10,11... | collective-permute-start | bytes 1572872 | tf_op jit(solution)/shard_map/dispatch/ppermute | solution.py:62
  64.0 5.9 %collective-permute-start.7 = (bf16[1024,256]{1,0:T(8,128)(2,1)S(1)}, bf16[1024,256]{1,0:T(8,128)(2,1)S(1)}, u32[]{:S(2)}, u32[]{:S(2)}) collective-permute-start(bf16[1024,256]{1,0:T(8,128)(2,1)S(1)} %pad_maximum_fusion.2), channel_id=1, source_target_pairs={{0,1},{1,0},{2,3},{3,2},{4,5},{5,4},{6,7},{7,6},{8,9},{9,8},{10,11... | collective-permute-start | bytes 1572872 | tf_op jit(solution)/shard_map/dispatch/ppermute | solution.py:62
  71.3 4.9 %copy-start.6 = (bf16[192,2048]{1,0:T(8,128)(2,1)S(1)}, bf16[192,2048]{1,0:T(8,128)(2,1)}, u32[]{:S(2)}) copy-start(bf16[192,2048]{1,0:T(8,128)(2,1)} %param.11) | copy-start | bytes 2359300
  71.3 3.5 %collective-permute-start.8 = (bf16[512,192]{0,1:T(8,128)(2,1)S(1)}, bf16[512,192]{0,1:T(8,128)(2,1)S(1)}, u32[]{:S(2)}, u32[]{:S(2)}) collective-permute-start(bf16[512,192]{0,1:T(8,128)(2,1)S(1)} %fusion.20), channel_id=1, source_target_pairs={{0,1},{1,0},{2,3},{3,2},{4,5},{5,4},{6,7},{7,6},{8,9},{9,8},{10,11... | collective-permute-start | bytes 589832 | tf_op jit(solution)/shard_map/experts/ppermute | solution.py:62
  76.6 5.3 %collective-permute-start.10 = (bf16[512,256]{1,0:T(8,128)(2,1)S(1)}, bf16[512,256]{1,0:T(8,128)(2,1)S(1)}, u32[]{:S(2)}, u32[]{:S(2)}) collective-permute-start(bf16[512,256]{1,0:T(8,128)(2,1)S(1)} %fusion.11), channel_id=1, source_target_pairs={{2,4},{4,2},{3,5},{5,3},{10,12},{12,10},{11,13},{13,11},{18,20},{2... | collective-permute-start | bytes 786440 | tf_op jit(solution)/shard_map/combine/ppermute | solution.py:20
  77.2 7.7 %collective-permute-start.11 = (bf16[512,256]{1,0:T(8,128)(2,1)S(1)}, bf16[512,256]{1,0:T(8,128)(2,1)S(1)}, u32[]{:S(2)}, u32[]{:S(2)}) collective-permute-start(bf16[512,256]{1,0:T(8,128)(2,1)S(1)} %fusion.11), channel_id=1, source_target_pairs={{0,2},{6,4},{1,3},{7,5},{8,10},{14,12},{9,11},{15,13},{16,18},{22,... | collective-permute-start | bytes 786440 | tf_op jit(solution)/shard_map/combine/ppermute | solution.py:20
  80.2 10.3 %collective-permute-start.9 = (bf16[512,256]{1,0:T(8,128)(2,1)S(1)}, bf16[512,256]{1,0:T(8,128)(2,1)S(1)}, u32[]{:S(2)}, u32[]{:S(2)}) collective-permute-start(bf16[512,256]{1,0:T(8,128)(2,1)S(1)} %get-tuple-element.44), channel_id=1, source_target_pairs={{0,4},{6,2},{1,5},{7,3},{8,12},{14,10},{9,13},{15,11},{16,20},{22,... | collective-permute-start | bytes 786440 | tf_op jit(solution)/shard_map/combine/ppermute | solution.py:20
  90.8 20.4 %copy-start.10 = (bf16[256,8]{0,1:T(8,128)(2,1)S(1)}, bf16[256,8]{0,1:T(8,128)(2,1)}, u32[]{:S(2)}) copy-start(bf16[256,8]{0,1:T(8,128)(2,1)} %param.8) | copy-start | bytes 12292
  90.8 20.4 %copy-start.9 = (s32[256,8]{0,1:T(8,128)S(1)}, s32[256,8]{0,1:T(8,128)}, u32[]{:S(2)}) copy-start(s32[256,8]{0,1:T(8,128)} %param.7) | copy-start | bytes 24580
  90.9 20.4 %copy-start.12 = (s32[16]{0:T(128)S(1)}, s32[16]{0:T(128)}, u32[]{:S(2)}) copy-start(s32[16]{0:T(128)} %copy-done.11) | copy-start | bytes 196
  90.9 33.2 %copy-start.8 = (pred[16,256]{1,0:T(8,128)(4,1)S(1)}, pred[16,256]{1,0:T(8,128)(4,1)}, u32[]{:S(2)}) copy-start(pred[16,256]{1,0:T(8,128)(4,1)} %copy-done.7) | copy-start | bytes 12292
  90.9 9.1 %collective-permute-start.12 = (bf16[512,256]{1,0:T(8,128)(2,1)S(1)}, bf16[512,256]{1,0:T(8,128)(2,1)S(1)}, u32[]{:S(2)}, u32[]{:S(2)}) collective-permute-start(bf16[512,256]{1,0:T(8,128)(2,1)S(1)} %get-tuple-element.38), channel_id=1, source_target_pairs={{0,2},{2,0},{4,6},{6,4},{1,3},{3,1},{5,7},{7,5},{8,10},{10,8},{12,... | collective-permute-start | bytes 786440 | tf_op jit(solution)/shard_map/combine/ppermute | solution.py:20
  94.9 5.1 %collective-permute-start.13 = (bf16[512,256]{1,0:T(8,128)(2,1)S(1)}, bf16[512,256]{1,0:T(8,128)(2,1)S(1)}, u32[]{:S(2)}, u32[]{:S(2)}) collective-permute-start(bf16[512,256]{1,0:T(8,128)(2,1)S(1)} %get-tuple-element.39), channel_id=1, source_target_pairs={{2,4},{4,2},{3,5},{5,3},{10,12},{12,10},{11,13},{13,11},{18,20},{2... | collective-permute-start | bytes 786440 | tf_op jit(solution)/shard_map/combine/ppermute | solution.py:20
  101.0 23.1 %all-to-all-start.1 = ((bf16[16,32,256]{2,1,0:T(8,128)(2,1)}), bf16[16,32,256]{2,1,0:T(8,128)(2,1)S(1)}, u32[]{:S(2)}, u32[]{:S(2)}) async-start(bf16[16,32,256]{2,1,0:T(8,128)(2,1)} %bitcast.4), calls=%async_computation.1 | async-start | bytes 524288 | tf_op jit(solution)/shard_map/combine/all_to_all | solution.py:106
  135.2 9.6 %collective-permute-start.14 = (bf16[256,256]{1,0:T(8,128)(2,1)S(1)}, bf16[256,256]{1,0:T(8,128)(2,1)S(1)}, u32[]{:S(2)}, u32[]{:S(2)}) collective-permute-start(bf16[256,256]{1,0:T(8,128)(2,1)S(1)} %reduce_sum.31), channel_id=1, source_target_pairs={{0,8},{8,0},{1,9},{9,1},{2,10},{10,2},{3,11},{11,3},{4,12},{12,4},... | collective-permute-start | bytes 393224 | tf_op jit(solution)/shard_map/combine/ppermute | solution.py:66
  145.8 28.1 %all-to-all-start.3 = ((bf16[16,32,256]{2,1,0:T(8,128)(2,1)}), bf16[16,32,256]{2,1,0:T(8,128)(2,1)S(1)}, u32[]{:S(2)}, u32[]{:S(2)}) async-start(bf16[16,32,256]{2,1,0:T(8,128)(2,1)} %bitcast.6), calls=%async_computation.3 | async-start | bytes 524288 | tf_op jit(solution)/shard_map/curvature/all_to_all | solution.py:106
  155.8 11.2 %collective-permute-start.15 = (bf16[256,256]{1,0:T(8,128)(2,1)S(1)}, bf16[256,256]{1,0:T(8,128)(2,1)S(1)}, u32[]{:S(2)}, u32[]{:S(2)}) collective-permute-start(bf16[256,256]{1,0:T(8,128)(2,1)S(1)} %add_convert_fusion.1), channel_id=1, source_target_pairs={{0,2},{2,4},{4,6},{6,8},{8,10},{10,12},{12,14},{14,0},{1,3},{3,5},... | collective-permute-start | bytes 393224 | tf_op jit(solution)/shard_map/tangent/ppermute | solution.py:55
  161.1 6.0 %collective-permute-start.16 = (bf16[256,256]{1,0:T(8,128)(2,1)S(1)}, bf16[256,256]{1,0:T(8,128)(2,1)S(1)}, u32[]{:S(2)}, u32[]{:S(2)}) collective-permute-start(bf16[256,256]{1,0:T(8,128)(2,1)S(1)} %add_convert_fusion.1), channel_id=1, source_target_pairs={{0,14},{2,0},{4,2},{6,4},{8,6},{10,8},{12,10},{14,12},{1,15},{3,1}... | collective-permute-start | bytes 393224 | tf_op jit(solution)/shard_map/tangent/ppermute | solution.py:55
  163.0 10.9 %collective-permute-start.17 = (bf16[256,256]{1,0:T(8,128)(2,1)S(1)}, bf16[256,256]{1,0:T(8,128)(2,1)S(1)}, u32[]{:S(2)}, u32[]{:S(2)}) collective-permute-start(bf16[256,256]{1,0:T(8,128)(2,1)S(1)} %add_convert_fusion.1), channel_id=1, source_target_pairs={{0,4},{2,6},{4,8},{6,10},{8,12},{10,14},{12,0},{14,2},{1,5},{3,7},... | collective-permute-start | bytes 393224 | tf_op jit(solution)/shard_map/tangent/ppermute | solution.py:55
  173.9 7.1 %collective-permute-start.18 = (bf16[512,256]{1,0:T(8,128)(2,1)S(1)}, bf16[512,256]{1,0:T(8,128)(2,1)S(1)}, u32[]{:S(2)}, u32[]{:S(2)}) collective-permute-start(bf16[512,256]{1,0:T(8,128)(2,1)S(1)} %bitcast.51), channel_id=1, source_target_pairs={{0,2},{2,0},{4,6},{6,4},{1,3},{3,1},{5,7},{7,5},{8,10},{10,8},{12,... | collective-permute-start | bytes 786440 | tf_op jit(solution)/shard_map/curvature/ppermute | solution.py:20
  175.8 14.5 %collective-permute-start.22 = (bf16[512,256]{1,0:T(8,128)(2,1)S(1)}, bf16[512,256]{1,0:T(8,128)(2,1)S(1)}, u32[]{:S(2)}, u32[]{:S(2)}) collective-permute-start(bf16[512,256]{1,0:T(8,128)(2,1)S(1)} %bitcast.52), channel_id=1, source_target_pairs={{2,4},{4,2},{3,5},{5,3},{10,12},{12,10},{11,13},{13,11},{18,20},{2... | collective-permute-start | bytes 786440 | tf_op jit(solution)/shard_map/curvature/ppermute | solution.py:20
  181.0 31.9 %collective-permute-start.19 = (bf16[1024,256]{1,0:T(8,128)(2,1)S(1)}, bf16[1024,256]{1,0:T(8,128)(2,1)S(1)}, u32[]{:S(2)}, u32[]{:S(2)}) collective-permute-start(bf16[1024,256]{1,0:T(8,128)(2,1)S(1)} %pad_maximum_fusion.3), channel_id=1, source_target_pairs={{0,1},{1,0},{2,3},{3,2},{4,5},{5,4},{6,7},{7,6},{8,9},{9,8},{10,11... | collective-permute-start | bytes 1572872 | tf_op jit(solution)/shard_map/tangent/ppermute | solution.py:62
  190.3 9.8 %collective-permute-start.23 = (bf16[512,256]{1,0:T(8,128)(2,1)S(1)}, bf16[512,256]{1,0:T(8,128)(2,1)S(1)}, u32[]{:S(2)}, u32[]{:S(2)}) collective-permute-start(bf16[512,256]{1,0:T(8,128)(2,1)S(1)} %collective-permute-done.22), channel_id=1, source_target_pairs={{2,0},{4,6},{3,1},{5,7},{10,8},{12,14},{11,9},{13,15},{18,16},{20,... | collective-permute-start | bytes 786440 | tf_op jit(solution)/shard_map/curvature/ppermute | solution.py:20
  191.6 11.5 %collective-permute-start.20 = (bf16[512,256]{1,0:T(8,128)(2,1)S(1)}, bf16[512,256]{1,0:T(8,128)(2,1)S(1)}, u32[]{:S(2)}, u32[]{:S(2)}) collective-permute-start(bf16[512,256]{1,0:T(8,128)(2,1)S(1)} %collective-permute-done.18), channel_id=1, source_target_pairs={{2,4},{4,2},{3,5},{5,3},{10,12},{12,10},{11,13},{13,11},{18,20},{2... | collective-permute-start | bytes 786440 | tf_op jit(solution)/shard_map/curvature/ppermute | solution.py:20
  192.3 16.2 %collective-permute-start.21 = (bf16[512,256]{1,0:T(8,128)(2,1)S(1)}, bf16[512,256]{1,0:T(8,128)(2,1)S(1)}, u32[]{:S(2)}, u32[]{:S(2)}) collective-permute-start(bf16[512,256]{1,0:T(8,128)(2,1)S(1)} %collective-permute-done.18), channel_id=1, source_target_pairs={{4,0},{2,6},{5,1},{3,7},{12,8},{10,14},{13,9},{11,15},{20,16},{18,... | collective-permute-start | bytes 786440 | tf_op jit(solution)/shard_map/curvature/ppermute | solution.py:20
  200.4 12.5 %collective-permute-start.25 = (bf16[384,256]{1,0:T(8,128)(2,1)S(1)}, bf16[384,256]{1,0:T(8,128)(2,1)S(1)}, u32[]{:S(2)}, u32[]{:S(2)}) collective-permute-start(bf16[384,256]{1,0:T(8,128)(2,1)S(1)} %pad_maximum_fusion.6), channel_id=1, source_target_pairs={{0,1},{1,0},{2,3},{3,2},{4,5},{5,4},{6,7},{7,6},{8,9},{9,8},{10,11... | collective-permute-start | bytes 589832 | tf_op jit(solution)/shard_map/curvature/ppermute | solution.py:62
  208.8 4.1 %collective-permute-start.24 = (bf16[384,256]{1,0:T(8,128)(2,1)S(1)}, bf16[384,256]{1,0:T(8,128)(2,1)S(1)}, u32[]{:S(2)}, u32[]{:S(2)}) collective-permute-start(bf16[384,256]{1,0:T(8,128)(2,1)S(1)} %pad_maximum_fusion.5), channel_id=1, source_target_pairs={{0,1},{1,0},{2,3},{3,2},{4,5},{5,4},{6,7},{7,6},{8,9},{9,8},{10,11... | collective-permute-start | bytes 589832 | tf_op jit(solution)/shard_map/curvature/ppermute | solution.py:62
  213.0 0.9 copy-start.2
  213.8 1.0 copy-start.1
